TPU v7x, 512 devices: a whole 4x8x8 slice. The times are simulated.
512 devices in a mesh: loop: 32 (over y, z_hi), grp: 16 (over z_lo, x, core).
Axes of the slice: x: 4, y: 8, z: 8 (z_hi: 4, z_lo: 2; z = z_hi * 2 + z_lo), core: 2. Of those that a mesh axis runs over, the one named last changes fastest.
Arguments:
- real_pool: bfloat16 [32, 16, 4, 32, 64], P('loop', 'grp'), may hold values from -6 to 6
- real_pick: int32 [32, 16, 2, 1], P('loop', 'grp'), may hold values from 0 to 3
- noise_latents: bfloat16 [32, 2, 128, 512], P('loop', None, None, 'grp'), may hold values from -6 to 6
- generator_in: float32 [32, 256, 128], P('loop'), may hold values from -0.5 to 0.5
- generator_out: float32 [32, 32, 256], P('loop'), may hold values from -0.375 to 0.375
- critic_lift: float32 [32, 16, 256, 32], P('loop', 'grp'), may hold values from -1 to 1
- critic_kernel: float32 [32, 16, 256, 2304], P('loop', 'grp'), may hold values from -0.125 to 0.125
- critic_head: float32 [32, 16, 256], P('loop', 'grp'), may hold values from -0.375 to 0.375
Outputs:
- updated_lift: float32 [32, 16, 256, 32], P('loop', 'grp')
- updated_kernel: float32 [32, 16, 256, 2304], P('loop', 'grp')
- updated_head: float32 [32, 16, 256], P('loop', 'grp')
- updated_first: float32 [32, 256, 128], P('loop')
- updated_second: float32 [32, 32, 256], P('loop')
- fake_gradient: float32 [32, 32, 512], P('loop', None, 'grp')
- real_scores: float32 [32, 16, 2, 1], P('loop', 'grp')
All inputs are finite; a program needn't handle non-finite values.
Results may differ from a plain program's by a relative error of at most 0.023.
Values may be sent and summed in bfloat16 or wider, within the bound.
No kernel may reach another device: no remote copies, remote signals or barrier semaphores. Data moves between devices by JAX's collectives and lax.ppermute only.
A program may use at most 64 MiB of HBM per device.

v0:
```python
import math

import jax
import jax.numpy as jnp
from jax import lax
from jax.sharding import PartitionSpec as P

IMG_H = 8
IMG_W = 8
CELLS = 64
ROUNDS = 2


critic_rate = 0.05
generator_rate = 0.2


def as_sent(x):

    def short(part):
        return part.astype(jnp.bfloat16) if part.dtype == jnp.float32 else part

    return jax.tree.map(short, x)


def from_behind(value, axis, steps):
    count = lax.axis_size(axis)
    pairs = [(source, (source + steps) % count) for source in range(count)]
    return lax.ppermute(value, axis, pairs)


def critic_scores(lift_weight, kernel_weight, head_weight, images):
    total = images.shape[1]
    image_count = total // CELLS
    lifted = jax.nn.silu(
        jnp.dot(lift_weight.astype(jnp.bfloat16), images, preferred_element_type=jnp.float32)
    ).astype(jnp.bfloat16)
    channels = lifted.shape[0]
    planes = lifted.reshape(channels, image_count, IMG_H, IMG_W)
    padded = jnp.pad(planes, ((0, 0), (0, 0), (1, 1), (1, 1)))
    tap_list = [
        padded[:, :, row_shift : row_shift + IMG_H, col_shift : col_shift + IMG_W]
        for row_shift in range(3)
        for col_shift in range(3)
    ]
    patches = jnp.stack(tap_list, 0).reshape(9 * channels, total)
    hidden = jax.nn.silu(
        jnp.dot(kernel_weight.astype(jnp.bfloat16), patches, preferred_element_type=jnp.float32)
    )
    cell_scores = jnp.dot(head_weight, hidden, precision=lax.Precision.HIGHEST)
    return jnp.sum(cell_scores.reshape(image_count, CELLS), axis=1) / math.sqrt(CELLS)


def critic_step(lift_weight, kernel_weight, head_weight, fake_rows, real_rows):
    fake_count = fake_rows.shape[1] // CELLS

    def critic_loss(lift_arg, kernel_arg, head_arg, fake_wide):
        joined = jnp.concatenate([fake_wide.astype(jnp.bfloat16), real_rows], axis=1)
        scores = critic_scores(lift_arg, kernel_arg, head_arg, joined)
        return (jnp.mean(scores[:fake_count]) - jnp.mean(scores[fake_count:]), scores)

    _, back, scores = jax.vjp(
        critic_loss,
        lift_weight,
        kernel_weight,
        head_weight,
        fake_rows.astype(jnp.float32),
        has_aux=True,
    )
    grad_lift, grad_kernel, grad_head, grad_fake = back(jnp.ones((), jnp.float32))
    updated = (
        lift_weight - critic_rate * grad_lift,
        kernel_weight - critic_rate * grad_kernel,
        head_weight - critic_rate * grad_head,
    )
    return (updated, -fake_count * grad_fake, scores[fake_count:])


def generate(first_weight, second_weight, latents):
    inner = jnp.dot(first_weight, latents.astype(jnp.float32), precision=lax.Precision.HIGHEST)
    return jnp.dot(second_weight, jax.nn.silu(inner), precision=lax.Precision.HIGHEST)


def generator_grads(first_weight, second_weight, latents, pull_back):
    _, back = jax.vjp(lambda a, b: generate(a, b, latents), first_weight, second_weight)
    return back(pull_back)


def pick_images(pool_images, picks):
    chosen = jnp.take(pool_images, picks, axis=0)
    return jnp.transpose(chosen, (1, 0, 2)).reshape(
        chosen.shape[1], chosen.shape[0] * chosen.shape[2]
    )


def per_device(
    real_pool,
    real_pick,
    noise_latents,
    generator_in,
    generator_out,
    critic_lift,
    critic_kernel,
    critic_head,
):
    pool_images = real_pool[0, 0]
    picks_all = real_pick[0, 0]
    first_weight = generator_in[0]
    second_weight = generator_out[0]
    lift_weight = critic_lift[0, 0]
    kernel_weight = critic_kernel[0, 0]
    head_weight = critic_head[0, 0]
    score_list = []
    owner_grad = None
    for round_index in range(ROUNDS):
        latents = noise_latents[0, round_index]
        own_fake = generate(first_weight, second_weight, latents).astype(jnp.bfloat16)
        own_real = pick_images(pool_images, picks_all[round_index])
        fake_part, real_rows = (own_fake, own_real)
        fake_rows = lax.all_gather(fake_part, "grp", axis=1, tiled=True)
        updated, contrib, real_part = critic_step(
            lift_weight, kernel_weight, head_weight, fake_rows, real_rows
        )
        lift_weight, kernel_weight, head_weight = updated
        reduced = lax.psum_scatter(
            contrib.astype(jnp.bfloat16), "grp", scatter_dimension=1, tiled=True
        ).astype(jnp.float32)
        lift_weight, kernel_weight, head_weight = (
            from_behind(as_sent(lift_weight), "loop", 1).astype(lift_weight.dtype),
            from_behind(as_sent(kernel_weight), "loop", 1).astype(kernel_weight.dtype),
            from_behind(as_sent(head_weight), "loop", 1).astype(head_weight.dtype),
        )
        grad_first, grad_second = generator_grads(first_weight, second_weight, latents, reduced)
        grad_first, grad_second = (
            lax.psum(grad_first.astype(jnp.bfloat16), "grp").astype(jnp.float32),
            lax.psum(grad_second.astype(jnp.bfloat16), "grp").astype(jnp.float32),
        )
        owner_grad = reduced
        first_weight = first_weight - generator_rate * grad_first
        second_weight = second_weight - generator_rate * grad_second
        score_list.append(real_part)
    scores_out = jnp.stack(score_list, axis=0)
    return (
        lift_weight[None, None],
        kernel_weight[None, None],
        head_weight[None, None],
        first_weight[None],
        second_weight[None],
        owner_grad[None],
        scores_out[None, None],
    )


def solution(mesh):
    return jax.shard_map(
        per_device,
        mesh=mesh,
        in_specs=(
            P("loop", "grp", None, None, None),
            P("loop", "grp", None, None),
            P("loop", None, None, "grp"),
            P("loop", None, None),
            P("loop", None, None),
            P("loop", "grp", None, None),
            P("loop", "grp", None, None),
            P("loop", "grp", None),
        ),
        out_specs=(
            P("loop", "grp", None, None),
            P("loop", "grp", None, None),
            P("loop", "grp", None),
            P("loop", None, None),
            P("loop", None, None),
            P("loop", None, "grp"),
            P("loop", "grp", None, None),
        ),
        check_vma=False,
    )
```

profile of v0, /device:TPU:6, one launch (start us, length us, event | category | flops | bytes accessed | tf_op | source)
XLA Modules:
  0.0 533.5 jit_solution(15588159179366780548)
XLA Ops:
  15.3 19.4 %all_gather.6 = bf16[32,512]{0,1:T(8,128)(2,1)S(1)} all-gather(bf16[32,32]{0,1:T(8,128)(2,1)S(1)} %fusion.17), channel_id=1, replica_groups=mesh['loop'=32,'grp'=16] {'grp'}, dimensions={1}, use_global_device_ids=true | all-gather | bytes 34816 | tf_op jit(solution)/shard_map/all_gather | solution.py:120
  35.5 1.8 multiply_convert_fusion.1
  38.1 1.5 copy-done
  39.5 1.7 divide_multiply_fusion
  41.8 3.1 collective-permute-start.2
  45.0 4.1 fusion.6
  49.0 6.6 %collective-permute-start.1 = (bf16[256,2304]{1,0:T(8,128)(2,1)}, bf16[256,2304]{1,0:T(8,128)(2,1)}, u32[]{:S(2)}, u32[]{:S(2)}) collective-permute-start(bf16[256,2304]{1,0:T(8,128)(2,1)} %fusion.6), channel_id=1, source_target_pairs={{0,16},{16,32},{32,48},{48,64},{64,80},{80,96},{96,112},{112,128},... | collective-permute-start | bytes 3538952 | tf_op jit(solution)/shard_map/ppermute | solution.py:29
  58.4 4.2 collective-permute-start
  66.3 60.7 %reduce-scatter.7.cloned.1.call-done = bf16[32,32]{1,0:T(8,128)(2,1)} async-done(((bf16[512,32]{1,0:T(8,128)(2,1)}), bf16[32,32]{1,0:T(8,128)(2,1)}) %reduce-scatter.7.cloned.1.call-update) | async-done | bytes 2064
  129.8 52.5 %psum.28 = bf16[32,256]{1,0:T(8,128)(2,1)S(1)} all-reduce(bf16[32,256]{1,0:T(8,128)(2,1)S(1)} %convolution_convert_fusion.8), channel_id=1, replica_groups=mesh['loop'=32,'grp'=16] {'grp'}, use_global_device_ids=true, to_apply=%region_1.3 | all-reduce | flops 8192 | bytes 32768 | tf_op jit(solution)/shard_map/psum | solution.py:136
  182.3 84.8 %all-reduce.24.cloned.1.call-done = bf16[256,128]{1,0:T(8,128)(2,1)} async-done(((bf16[256,128]{1,0:T(8,128)(2,1)}), bf16[256,128]{1,0:T(8,128)(2,1)}) %all-reduce.24.cloned.1.call-update) | async-done | bytes 65552 | tf_op jit(solution)/shard_map/psum | solution.py:135
  268.4 17.1 %all_gather.7 = bf16[32,512]{0,1:T(8,128)(2,1)S(1)} all-gather(bf16[32,32]{0,1:T(8,128)(2,1)S(1)} %copy.52), channel_id=1, replica_groups=mesh['loop'=32,'grp'=16] {'grp'}, dimensions={1}, use_global_device_ids=true | all-gather | bytes 34816 | tf_op jit(solution)/shard_map/all_gather | solution.py:120
  286.7 2.2 fusion.140
  291.7 4.7 collective-permute-start.5
  296.4 2.5 convolution_convert_fusion
  300.6 5.8 %collective-permute-start.3 = (bf16[256,32]{0,1:T(8,128)(2,1)S(1)}, bf16[256,32]{0,1:T(8,128)(2,1)S(1)}, u32[]{:S(2)}, u32[]{:S(2)}) collective-permute-start(bf16[256,32]{0,1:T(8,128)(2,1)S(1)} %subtract_convert_fusion.1), channel_id=1, source_target_pairs={{0,16},{16,32},{32,48},{48,64},{64,80},{80,96},{96,112},{112,128},... | collective-permute-start | bytes 49160 | tf_op jit(solution)/shard_map/ppermute | solution.py:29
  307.3 3.7 subtract_convert_fusion
  311.1 2.8 collective-permute-start.4
  313.9 1.9 maximum_bitcast_fusion
  317.6 51.0 %reduce-scatter.9.cloned.1.call-done = bf16[32,32]{1,0:T(8,128)(2,1)} async-done(((bf16[512,32]{1,0:T(8,128)(2,1)}), bf16[32,32]{1,0:T(8,128)(2,1)}) %reduce-scatter.9.cloned.1.call-update) | async-done | bytes 2064
  372.2 52.1 %psum.31 = bf16[32,256]{1,0:T(8,128)(2,1)S(1)} all-reduce(bf16[32,256]{1,0:T(8,128)(2,1)S(1)} %convolution_convert_fusion.7), channel_id=1, replica_groups=mesh['loop'=32,'grp'=16] {'grp'}, use_global_device_ids=true, to_apply=%region_5.7 | all-reduce | flops 8192 | bytes 32768 | tf_op jit(solution)/shard_map/psum | solution.py:136
  425.5 98.3 %all-reduce.26.cloned.1.call-done = bf16[256,128]{1,0:T(8,128)(2,1)} async-done(((bf16[256,128]{1,0:T(8,128)(2,1)}), bf16[256,128]{1,0:T(8,128)(2,1)}) %all-reduce.26.cloned.1.call-update) | async-done | bytes 65552 | tf_op jit(solution)/shard_map/psum | solution.py:135
  523.9 1.5 subtract_bitcast_fusion
  525.4 1.6 bitcast_convert_fusion.2
  (119 shorter events, 29.5 us)
Async XLA Ops:
  7.2 119.8 %reduce-scatter.7.cloned.1.call-start = ((), (), s32[]{:S(2)}) async-start(), calls=%async_computation.4 | async-start | bytes 139264
  37.9 1.7 copy-start
  39.5 2.2 copy-start.8
  41.8 23.4 %collective-permute-start.2 = (bf16[256]{0:T(256)(128)(2,1)S(1)}, bf16[256]{0:T(256)(128)(2,1)S(1)}, u32[]{:S(2)}, u32[]{:S(2)}) collective-permute-start(bf16[256]{0:T(256)(128)(2,1)S(1)} %subtract_convert_fusion.3), channel_id=1, source_target_pairs={{0,16},{16,32},{32,48},{48,64},{64,80},{80,96},{96,112},{112,128},... | collective-permute-start | bytes 1544 | tf_op jit(solution)/shard_map/ppermute | solution.py:29
  45.0 10.7 %copy-start.1 = (f32[1,1,256,2304]{3,2,1,0:T(8,128)S(1)}, f32[1,1,256,2304]{3,2,1,0:T(8,128)}, u32[]{:S(2)}) copy-start(f32[1,1,256,2304]{3,2,1,0:T(8,128)} %param.16) | copy-start | bytes 7077892
  49.0 237.7 %collective-permute-start.1 = (bf16[256,2304]{1,0:T(8,128)(2,1)}, bf16[256,2304]{1,0:T(8,128)(2,1)}, u32[]{:S(2)}, u32[]{:S(2)}) collective-permute-start(bf16[256,2304]{1,0:T(8,128)(2,1)} %fusion.6), channel_id=1, source_target_pairs={{0,16},{16,32},{32,48},{48,64},{64,80},{80,96},{96,112},{112,128},... | collective-permute-start | bytes 3538952 | tf_op jit(solution)/shard_map/ppermute | solution.py:29
  56.9 1.1 copy-start.4
  56.9 1.3 copy-start.7
  57.3 6.4 %copy-start.3 = (f32[576,256]{1,0:T(8,128)S(1)}, f32[576,256]{1,0:T(8,128)}, u32[]{:S(2)}) copy-start(f32[576,256]{1,0:T(8,128)} %get-tuple-element.45) | copy-start | bytes 1769476
  57.3 69.7 %copy-start.5 = (f32[1,32,256]{2,1,0:T(8,128)S(1)}, f32[1,32,256]{2,1,0:T(8,128)}, u32[]{:S(2)}) copy-start(f32[1,32,256]{2,1,0:T(8,128)} %param.14) | copy-start | bytes 98308
  57.3 70.5 %copy-start.9 = (bf16[1,2,128,32]{2,3,1,0:T(8,128)(2,1)S(1)}, bf16[1,2,128,32]{2,3,1,0:T(8,128)(2,1)}, u32[]{:S(2)}) copy-start(bf16[1,2,128,32]{2,3,1,0:T(8,128)(2,1)} %param.12) | copy-start | bytes 49156
  57.3 209.8 %copy-start.2 = (f32[1,256,128]{2,1,0:T(8,128)S(1)}, f32[1,256,128]{2,1,0:T(8,128)}, u32[]{:S(2)}) copy-start(f32[1,256,128]{2,1,0:T(8,128)} %param.13) | copy-start | bytes 393220
  58.4 227.2 %collective-permute-start = (bf16[256,32]{0,1:T(8,128)(2,1)S(1)}, bf16[256,32]{0,1:T(8,128)(2,1)S(1)}, u32[]{:S(2)}, u32[]{:S(2)}) collective-permute-start(bf16[256,32]{0,1:T(8,128)(2,1)S(1)} %fusion.16), channel_id=1, source_target_pairs={{0,16},{16,32},{32,48},{48,64},{64,80},{80,96},{96,112},{112,128},... | collective-permute-start | bytes 49160 | tf_op jit(solution)/shard_map/ppermute | solution.py:29
  63.6 203.5 %all-reduce.24.cloned.1.call-start = ((), (), s32[]{:S(2)}) async-start(), calls=%async_computation.2 | async-start | bytes 131072 | tf_op jit(solution)/shard_map/psum | solution.py:135
  65.2 117.1 %copy-start.10 = (bf16[256]{0:T(256)(128)(2,1)}, bf16[256]{0:T(256)(128)(2,1)S(1)}, u32[]{:S(2)}) copy-start(bf16[256]{0:T(256)(128)(2,1)S(1)} %collective-permute-done.2) | copy-start | bytes 1540
  128.8 239.8 %reduce-scatter.9.cloned.1.call-start = ((), (), s32[]{:S(2)}) async-start(), calls=%async_computation.5 | async-start | bytes 139264
  286.7 3.0 copy-start.12
  288.9 0.8 copy-start.13
  291.7 24.1 %collective-permute-start.5 = (bf16[256]{0:T(256)(128)(2,1)S(1)}, bf16[256]{0:T(256)(128)(2,1)}, u32[]{:S(2)}, u32[]{:S(2)}) collective-permute-start(bf16[256]{0:T(256)(128)(2,1)S(1)} %subtract_convert_fusion.2), channel_id=1, source_target_pairs={{0,16},{16,32},{32,48},{48,64},{64,80},{80,96},{96,112},{112,128},... | collective-permute-start | bytes 1544 | tf_op jit(solution)/shard_map/ppermute | solution.py:29
  299.4 7.8 %copy-start.11 = (f32[256]{0:T(256)S(1)}, f32[256]{0:T(256)}, u32[]{:S(2)}) copy-start(f32[256]{0:T(256)} %convert.9) | copy-start | bytes 3076
  300.6 16.4 %collective-permute-start.3 = (bf16[256,32]{0,1:T(8,128)(2,1)S(1)}, bf16[256,32]{0,1:T(8,128)(2,1)S(1)}, u32[]{:S(2)}, u32[]{:S(2)}) collective-permute-start(bf16[256,32]{0,1:T(8,128)(2,1)S(1)} %subtract_convert_fusion.1), channel_id=1, source_target_pairs={{0,16},{16,32},{32,48},{48,64},{64,80},{80,96},{96,112},{112,128},... | collective-permute-start | bytes 49160 | tf_op jit(solution)/shard_map/ppermute | solution.py:29
  307.2 216.6 %copy-start.6 = (bf16[256,128]{1,0:T(8,128)(2,1)S(1)}, bf16[256,128]{1,0:T(8,128)(2,1)}, u32[]{:S(2)}) copy-start(bf16[256,128]{1,0:T(8,128)(2,1)} %all-reduce.24.cloned.1.call-done) | copy-start | bytes 196612
  307.2 216.6 %all-reduce.26.cloned.1.call-start = ((), (), s32[]{:S(2)}) async-start(), calls=%async_computation.3 | async-start | bytes 131072 | tf_op jit(solution)/shard_map/psum | solution.py:135
  311.1 214.3 %collective-permute-start.4 = (bf16[256,2304]{1,0:T(8,128)(2,1)}, bf16[256,2304]{1,0:T(8,128)(2,1)S(1)}, u32[]{:S(2)}, u32[]{:S(2)}) collective-permute-start(bf16[256,2304]{1,0:T(8,128)(2,1)} %subtract_convert_fusion), channel_id=1, source_target_pairs={{0,16},{16,32},{32,48},{48,64},{64,80},{80,96},{96,112},{112,128},... | collective-permute-start | bytes 3538952 | tf_op jit(solution)/shard_map/ppermute | solution.py:29
Sparse Core Ops, SparseCore 0:
  63.8 63.1 reduce-scatter.6
  130.7 136.3 all-reduce.23
  307.4 61.2 reduce-scatter.8
  372.3 151.5 all-reduce.25
where the time goes:
time: 538 us; the launch traced here: 533 us
  waiting for transfers between devices  295 us (55%)
  blocking collectives  141 us (26%)
  matrix products  28.9 us (5%)
  starting transfers between devices  27.4 us (5%)
  between operations  18.2 us (3%)
  other arithmetic  13.2 us (2%)
  local copies, waits for them, and re-layouts  9.63 us (2%)
    psum x2, waiting for transfers between devices, per_device(): lax.psum(grad_first.astype(jnp.bfloat16), 'grp').astype(jnp.float32)  183 us
    unnamed x6, waiting for transfers between devices  112 us
    psum x2, blocking collectives, per_device(): lax.psum(grad_second.astype(jnp.bfloat16), 'grp').astype(jnp.float32)  105 us
    all_gather x2, blocking collectives, per_device(): fake_rows = lax.all_gather(fake_part, 'grp', axis=1, tiled=True)  36.5 us
    ppermute x6, starting transfers between devices, from_behind(): return lax.ppermute(value, axis, pairs)  27.3 us
    dot_general x6, matrix products, critic_scores(): jnp.dot(kernel_weight.astype(jnp.bfloat16), patches, preferred_element_ty...  15.2 us
  transfers between devices with their start and end apart: 10, of which 4 were waited for; matrix products, arithmetic and copies ran while one was open for 6% of the time, Pallas kernels for 0%

commit v1 on v0

v1 whole, which is shorter than its diff:
```python
import functools

import jax
import jax.numpy as jnp
from jax import lax
from jax.experimental import pallas as pl
from jax.experimental.pallas import tpu as pltpu
from jax.sharding import PartitionSpec as P

ROUNDS = 2
CELLS = 64
C = 32
CH = 256
TAPS = 9
N_GRP = 16
FAKE = 512
ROWS = 576
WIDE = 640
KW = TAPS * CH

critic_rate = 0.05
generator_rate = 0.2

bf16 = jnp.bfloat16
f32 = jnp.float32
NN = (((1,), (0,)), ((), ()))
NT = (((1,), (1,)), ((), ()))


def dot(a, b, dims=NN):
    return lax.dot_general(a, b, dims, preferred_element_type=f32)


def exact_dot(a, b, dims=NN):
    return lax.dot_general(a, b, dims, precision=lax.Precision.HIGHEST, preferred_element_type=f32)


def sigmoid(x):
    return 1.0 / (1.0 + jnp.exp(-x))


def row_ids(width):
    return lax.broadcasted_iota(jnp.int32, (ROWS, width), 0)


def move_rows(x, by):
    if by == 0:
        return x
    pad = jnp.zeros((abs(by), x.shape[1]), x.dtype)
    if by > 0:
        return jnp.concatenate([x[by:], pad], axis=0)
    return jnp.concatenate([pad, x[:by]], axis=0)


def masks():
    rows = row_ids(CH)
    col = rows & 7
    row = (rows >> 3) & 7
    reads_x = {-1: col > 0, 1: col < 7}
    reads_y = {-1: row > 0, 1: row < 7}
    return reads_x, reads_y


def critic_forward(images, lift_t, kernel_of, head, patch_ref):
    reads_x, reads_y = masks()
    images_t = jnp.transpose(images.astype(f32))[:ROWS].astype(bf16)
    pre = dot(images_t, lift_t)
    gate = sigmoid(pre)
    lifted = (pre * gate).astype(bf16).astype(f32)
    slope = gate * (1.0 + pre * (1.0 - gate))
    z = None
    for b in range(3):
        dx = b - 1
        across = lifted
        if dx:
            across = jnp.where(reads_x[dx], pltpu.roll(lifted, (-dx) % ROWS, 0), 0.0)
        for a in range(3):
            dy = a - 1
            tap = move_rows(across, 8 * dy)
            if dy:
                tap = jnp.where(reads_y[dy], tap, 0.0)
            tap = tap.astype(bf16)
            patch_ref[3 * a + b] = tap
            part = dot(tap, kernel_of(3 * a + b), NT)
            z = part if z is None else z + part
    gate = sigmoid(z)
    hidden = z * gate
    weight = jnp.where(row_ids(CH) < FAKE, 1.0 / 64.0, -1.0 / 8.0)
    real_score = jnp.sum(hidden[FAKE:] * head, keepdims=True) / 8.0
    head_grad = jnp.sum(weight * hidden, axis=0, keepdims=True)
    z_grad = (weight * head) * (gate * (1.0 + z * (1.0 - gate)))
    return slope, z_grad, head_grad, real_score


def lift_pullback(slope, z_grad, kernel_of):
    reads_x, reads_y = masks()
    total = None
    for b in range(3):
        dx = b - 1
        across = None
        for a in range(3):
            dy = a - 1
            tap = dot(z_grad, kernel_of(3 * a + b))
            if dy:
                tap = jnp.where(reads_y[dy], tap, 0.0)
            tap = move_rows(tap, -8 * dy)
            across = tap if across is None else across + tap
        if dx:
            across = pltpu.roll(jnp.where(reads_x[dx], across, 0.0), dx % ROWS, 0)
        total = across if total is None else total + across
    return (total * slope).astype(bf16)


def real_image(pool_ref, pick_ref, round_index):
    return pool_ref[pick_ref[round_index]]


def latents_of(noise_ref, round_index):
    return noise_ref[:, C * round_index : C * (round_index + 1), :].reshape(FAKE, 128).astype(f32)


def put_images(images_ref, fakes, real):
    images_ref[:, :FAKE] = fakes.astype(bf16)
    images_ref[:, FAKE:] = jnp.concatenate([real, jnp.zeros_like(real)], axis=1)


def generate_kernel(pick_ref, noise_ref, first_ref, second_ref, pool_ref, lift_ref, head_ref, packed_in, packed_ref, images_ref):
    latents = latents_of(noise_ref, 0)
    inner = exact_dot(latents, first_ref[...], NT)
    fakes = exact_dot(second_ref[...], inner * sigmoid(inner), NT)
    put_images(images_ref, fakes, real_image(pool_ref, pick_ref, 0))
    packed_ref[:, :WIDE] = images_ref[:16]
    packed_ref[:, WIDE : 2 * WIDE] = images_ref[16:]
    lift = lift_ref[...].astype(bf16)
    packed_ref[:, 1280:1536] = lift[:16]
    packed_ref[:, 1536:1792] = lift[16:]
    packed_ref[:, 1792:2048] = jnp.broadcast_to(head_ref[...], (16, CH)).astype(bf16)
    packed_ref[:, 2048:] = jnp.zeros((16, KW - 2048), bf16)


def first_step_kernel(images_ref, lift_ref, kernel_ref, head_ref, copies_ref, lift_out, kernel_out, head_out, score_out, patch_ref, half_ref):
    for t in range(TAPS):
        half_ref[t] = kernel_ref[:, CH * t : CH * (t + 1)].astype(bf16)
    lift = lift_ref[...]
    head = head_ref[...]
    lift_half = lift.astype(bf16)
    images = images_ref[...]
    slope, z_grad, head_grad, score = critic_forward(images, lift_half, lambda t: half_ref[t], head, patch_ref)
    z_half = z_grad.astype(bf16)
    pre_grad = lift_pullback(slope, z_half, lambda t: half_ref[t])
    pull = (-8.0 * dot(lift_half, pre_grad, NT)[:, :FAKE]).astype(bf16)
    for j in range(N_GRP):
        copies_ref[j] = pull
    lift_out[...] = lift - critic_rate * dot(images[:, :ROWS], pre_grad)
    head_out[...] = head - critic_rate * head_grad
    z_turned = jnp.transpose(z_grad).astype(bf16)
    for t in range(TAPS):
        cols = slice(CH * t, CH * (t + 1))
        kernel_out[:, cols] = (kernel_ref[:, cols] - critic_rate * dot(z_turned, patch_ref[t])).astype(bf16)
    score_out[...] = jnp.broadcast_to(score, (8, 128))


def pull_only_kernel(images_ref, lift_ref, kernel_ref, head_ref, pull_ref, patch_ref):
    lift_half = lift_ref[...].astype(bf16)
    kernel_of = lambda t: kernel_ref[:, CH * t : CH * (t + 1)]
    slope, z_grad, _, score = critic_forward(images_ref[...], lift_half, kernel_of, head_ref[...], patch_ref)
    pre_grad = lift_pullback(slope, z_grad.astype(bf16), kernel_of)
    pull_ref[:, :FAKE] = (-8.0 * dot(lift_half, pre_grad, NT)[:, :FAKE]).astype(bf16)
    high = score.astype(bf16)
    middle = (score - high.astype(f32)).astype(bf16)
    low = (score - high.astype(f32) - middle.astype(f32)).astype(bf16)
    lane = lax.broadcasted_iota(jnp.int32, (C, 128), 1)
    three = jnp.where(lane == 0, high.astype(f32), jnp.where(lane == 1, middle.astype(f32), jnp.where(lane == 2, low.astype(f32), 0.0)))
    pull_ref[:, FAKE:] = three.astype(bf16)


def moved_first_kernel(packed_ref, lift_out, kernel_out, head_out, patch_ref):
    images = jnp.concatenate([packed_ref[CH:, :WIDE], packed_ref[CH:, WIDE : 2 * WIDE]], axis=0)
    lift_half = jnp.concatenate([packed_ref[CH:, 1280:1536], packed_ref[CH:, 1536:1792]], axis=0)
    head = packed_ref[CH:, 1792:2048].astype(f32)[:1]
    kernel_of = lambda t: packed_ref[:CH, CH * t : CH * (t + 1)]
    slope, z_grad, head_grad, _ = critic_forward(images, lift_half, kernel_of, head, patch_ref)
    pre_grad = lift_pullback(slope, z_grad.astype(bf16), kernel_of)
    lift_out[...] = lift_half.astype(f32) - critic_rate * dot(images[:, :ROWS], pre_grad)
    head_out[...] = head - critic_rate * head_grad
    z_turned = jnp.transpose(z_grad).astype(bf16)
    for t in range(TAPS):
        kernel_out[:, CH * t : CH * (t + 1)] = kernel_of(t).astype(f32) - critic_rate * dot(z_turned, patch_ref[t])


def moved_second_kernel(images_ref, lift_ref, kernel_ref, head_ref, lift_out, kernel_out, head_out, patch_ref, half_ref):
    for t in range(TAPS):
        half_ref[t] = kernel_ref[:, CH * t : CH * (t + 1)].astype(bf16)
    lift = lift_ref[...]
    head = head_ref[...]
    images = images_ref[...]
    kernel_of = lambda t: half_ref[t]
    slope, z_grad, head_grad, _ = critic_forward(images, lift.astype(bf16), kernel_of, head, patch_ref)
    pre_grad = lift_pullback(slope, z_grad.astype(bf16), kernel_of)
    lift_out[...] = lift - critic_rate * dot(images[:, :ROWS], pre_grad)
    head_out[...] = head - critic_rate * head_grad
    z_turned = jnp.transpose(z_grad).astype(bf16)
    for t in range(TAPS):
        cols = slice(CH * t, CH * (t + 1))
        kernel_out[:, cols] = kernel_ref[:, cols] - critic_rate * dot(z_turned, patch_ref[t])


def generator_step(pulls_ref, latents, first, second):
    total = pulls_ref[0].astype(f32)
    for j in range(1, N_GRP):
        total = total + pulls_ref[j].astype(f32)
    inner = exact_dot(latents, first, NT)
    gate = sigmoid(inner)
    second_grad = exact_dot(total, inner * gate)
    inner_grad = exact_dot(jnp.transpose(total), second) * (gate * (1.0 + inner * (1.0 - gate)))
    first_grad = exact_dot(jnp.transpose(inner_grad), latents)
    return total, first - generator_rate * first_grad, second - generator_rate * second_grad


def middle_kernel(pick_ref, pulls_ref, noise_ref, first_ref, second_ref, pool_ref, images_ref, first_out, second_out):
    _, first, second = generator_step(pulls_ref, latents_of(noise_ref, 0), first_ref[...], second_ref[...])
    first_out[...] = first
    second_out[...] = second
    inner = exact_dot(latents_of(noise_ref, 1), first, NT)
    fakes = exact_dot(second, inner * sigmoid(inner), NT)
    put_images(images_ref, fakes, real_image(pool_ref, pick_ref, 1))


def last_kernel(place_ref, pulls_ref, noise_ref, first_ref, second_ref, first_out, second_out, own_out):
    total, first, second = generator_step(pulls_ref, latents_of(noise_ref, 1), first_ref[...], second_ref[...])
    first_out[...] = first
    second_out[...] = second
    own = jnp.zeros((C, C), f32)
    for j in range(N_GRP):
        own = own + jnp.where(place_ref[0] == j, total[:, C * j : C * (j + 1)], 0.0)
    own_out[...] = own


def vmem(*_):
    return pl.BlockSpec(memory_space=pltpu.VMEM)


def smem():
    return pl.BlockSpec(memory_space=pltpu.SMEM)


def call(kernel, name, outs, ins, scratch=(), scalars=0):
    return pl.pallas_call(
        kernel,
        name=name,
        out_shape=[jax.ShapeDtypeStruct(s, d) for s, d in outs],
        in_specs=[smem()] * scalars + [vmem()] * (len(ins) - scalars),
        out_specs=[vmem()] * len(outs),
        scratch_shapes=list(scratch),
        compiler_params=pltpu.CompilerParams(vmem_limit_bytes=40 * 1024 * 1024),
    )(*ins)


def shifted(value, steps):
    count = lax.axis_size("loop")
    return lax.ppermute(value, "loop", [(s, (s + steps) % count) for s in range(count)])


def swap(copies):
    return lax.all_to_all(copies, "grp", 0, 0)


PATCHES = pltpu.VMEM((TAPS, ROWS, CH), bf16)
HALVES = pltpu.VMEM((TAPS, CH, CH), bf16)


def per_device(real_pool, real_pick, noise_latents, generator_in, generator_out, critic_lift, critic_kernel, critic_head):
    pool = real_pool[0, 0]
    pick = real_pick[0, 0, :, 0]
    first, second = generator_in[0], generator_out[0]
    lift = jnp.swapaxes(critic_lift[0, 0], 0, 1)
    kernel = critic_kernel[0, 0]
    head = critic_head[0, 0][None]

    own_noise = jnp.swapaxes(noise_latents[0], 1, 2).reshape(ROUNDS * C, 128)
    noise = swap(jnp.broadcast_to(own_noise[None], (N_GRP,) + own_noise.shape))

    packed = jnp.pad(kernel.astype(bf16), ((0, 16), (0, 0)))
    packed, images = pl.pallas_call(
        generate_kernel,
        name="make_fakes",
        grid=(1,),
        out_shape=[jax.ShapeDtypeStruct((CH + 16, KW), bf16), jax.ShapeDtypeStruct((C, WIDE), bf16)],
        in_specs=[smem()] + [vmem()] * 6 + [pl.BlockSpec(memory_space=pl.ANY)],
        out_specs=[pl.BlockSpec((16, KW), lambda i: (CH // 16, 0)), vmem()],
        input_output_aliases={7: 0},
        compiler_params=pltpu.CompilerParams(vmem_limit_bytes=40 * 1024 * 1024),
    )(pick, noise, first, second, pool, lift, head, packed)

    moved = shifted(packed, 2)

    copies, lift_1, kernel_1, head_1, score_0 = call(
        first_step_kernel,
        "first_step",
        [((N_GRP, C, FAKE), bf16), ((C, CH), f32), ((CH, KW), bf16), ((1, CH), f32), ((8, 128), f32)],
        (images, lift, kernel, head),
        (PATCHES, HALVES),
    )
    pulls = swap(copies)
    own_images, first_1, second_1 = call(
        middle_kernel,
        "generator_step",
        [((C, WIDE), bf16), ((CH, 128), f32), ((C, CH), f32)],
        (pick, pulls, noise, first, second, pool),
        scalars=1,
    )
    ahead_images = shifted(own_images, -1)
    (pull,) = call(pull_only_kernel, "second_pull", [((C, WIDE), bf16)], (ahead_images, lift_1, kernel_1, head_1), (PATCHES,))
    behind_images = shifted(own_images, 1)
    own_pull = shifted(pull, 1)
    pulls = swap(jnp.broadcast_to(own_pull[None, :, :FAKE], (N_GRP, C, FAKE)))

    moved_lift, moved_kernel, moved_head = call(
        moved_first_kernel, "moved_first", [((C, CH), f32), ((CH, KW), f32), ((1, CH), f32)], (moved,), (PATCHES,)
    )
    lift_2, kernel_2, head_2 = call(
        moved_second_kernel,
        "moved_second",
        [((C, CH), f32), ((CH, KW), f32), ((1, CH), f32)],
        (behind_images, moved_lift, moved_kernel, moved_head),
        (PATCHES, HALVES),
    )
    place = lax.axis_index("grp").astype(jnp.int32)[None]
    first_2, second_2, own_grad = call(
        last_kernel,
        "generator_last",
        [((CH, 128), f32), ((C, CH), f32), ((C, C), f32)],
        (place, pulls, noise, first_1, second_1),
        scalars=1,
    )
    score_1 = jnp.sum(own_pull[0, FAKE : FAKE + 3].astype(f32))
    scores = jnp.stack([score_0[0, 0], score_1])[:, None]
    return (
        jnp.swapaxes(lift_2, 0, 1)[None, None],
        kernel_2[None, None],
        head_2[0][None, None],
        first_2[None],
        second_2[None],
        own_grad[None],
        scores[None, None],
    )


def solution(mesh):
    return jax.shard_map(
        per_device,
        mesh=mesh,
        in_specs=(
            P("loop", "grp", None, None, None),
            P("loop", "grp", None, None),
            P("loop", None, None, "grp"),
            P("loop", None, None),
            P("loop", None, None),
            P("loop", "grp", None, None),
            P("loop", "grp", None, None),
            P("loop", "grp", None),
        ),
        out_specs=(
            P("loop", "grp", None, None),
            P("loop", "grp", None, None),
            P("loop", "grp", None),
            P("loop", None, None),
            P("loop", None, None),
            P("loop", None, "grp"),
            P("loop", "grp", None, None),
        ),
        check_vma=False,
    )
```

time: 538 us -> 156 us (0.29)
  waiting for transfers between devices: 295 us -> 16.6 us
  blocking collectives: 141 us -> 0 us
  starting transfers between devices: 27.4 us -> 94.6 us
  Pallas kernels: 0 us -> 30.1 us
  matrix products: 28.9 us -> 0 us
  between operations: 18.2 us -> 0.81 us
  other arithmetic: 13.2 us -> 4.3 us
    psum x2 -> x0, waiting for transfers between devices: 183 us -> none  [per_device(): lax.psum(grad_first.astype(jnp.bfloat16), 'grp').astype(jnp.float32)]
    unnamed x6 -> x0, waiting for transfers between devices: 112 us -> none
    psum x2 -> x0, blocking collectives: 105 us -> none  [per_device(): lax.psum(grad_second.astype(jnp.bfloat16), 'grp').astype(jnp.float32)]
    ppermute x6 -> x4, starting transfers between devices: 27.3 us -> 74.4 us  [shifted(): lax.ppermute(value, 'loop', [(s, (s + steps) % count) for s in range(coun...]
    all_gather x2 -> x0, blocking collectives: 36.5 us -> none  [per_device(): fake_rows = lax.all_gather(fake_part, 'grp', axis=1, tiled=True)]
    pallas_call x0 -> x7, Pallas kernels: none -> 30.1 us  [the longest x6 27.8 us: call(): pl.pallas_call(kernel, name=name, out_shape=[jax.ShapeDtypeStruct(s, d) f...]
    dot_general x26 -> x0, matrix products: 28.9 us -> none  [the longest x6 15.2 us: critic_scores(): jnp.dot(kernel_weight.astype(jnp.bfloat16), patches, preferred_element_ty...]
    all_to_all x0 -> x3, starting transfers between devices: none -> 20.2 us  [swap(): return lax.all_to_all(copies, 'grp', 0, 0)]
  transfers between devices with their start and end apart: 10 -> 7, of which waited for: 4 -> 5; matrix products, arithmetic and copies ran while one was open for 6% -> 4% of each run, Pallas kernels for 0% -> 12%
where the time goes in v1:
time: 156 us; the launch traced here: 155 us
  starting transfers between devices  94.6 us (61%)
  Pallas kernels  30.1 us (19%)
  waiting for transfers between devices  16.6 us (11%)
  local copies, waits for them, and re-layouts  8.65 us (6%)
  other arithmetic  4.3 us (3%)
    ppermute x4, starting transfers between devices, shifted(): lax.ppermute(value, 'loop', [(s, (s + steps) % count) for s in range(coun...  74.4 us
    pallas_call x6, Pallas kernels, call(): pl.pallas_call(kernel, name=name, out_shape=[jax.ShapeDtypeStruct(s, d) f...  27.8 us
    all_to_all x3, starting transfers between devices, swap(): return lax.all_to_all(copies, 'grp', 0, 0)  20.2 us
    ppermute x4, waiting for transfers between devices, shifted(): lax.ppermute(value, 'loop', [(s, (s + steps) % count) for s in range(coun...  12.3 us
    unnamed x22, local copies, waits for them, and re-layouts  4.67 us
    all_to_all x3, waiting for transfers between devices, swap(): return lax.all_to_all(copies, 'grp', 0, 0)  4.27 us
  transfers between devices with their start and end apart: 7, of which 5 were waited for; matrix products, arithmetic and copies ran while one was open for 4% of the time, Pallas kernels for 12%

profile of v1, /device:TPU:6, one launch (start us, length us, event | category | flops | bytes accessed | tf_op | source)
XLA Modules:
  0.0 155.0 jit_solution(10587302942578240227)
XLA Ops:
  0.6 1.5 broadcast_in_dim.32
  2.1 9.2 %all-to-all-start = ((bf16[16,64,128]{2,1,0:T(8,128)(2,1)}), bf16[16,64,128]{2,1,0:T(8,128)(2,1)S(1)}, u32[]{:S(2)}, u32[]{:S(2)}) async-start(bf16[16,64,128]{2,1,0:T(8,128)(2,1)} %broadcast_in_dim.32), calls=%async_computation | async-start | bytes 524288 | tf_op jit(solution)/shard_map/all_to_all | solution.py:265
  11.3 1.8 %bitcast_convert_fusion = bf16[256,2304]{1,0:T(8,128)(2,1)S(1)} fusion(f32[1,1,256,2304]{3,2,1,0:T(8,128)} %param.14), kind=kLoop, calls=%fused_computation.3 | loop fusion | flops 589824 | bytes 3538944 | tf_op jit(solution)/shard_map/convert_element_type | solution.py:283
  14.3 2.9 %all-to-all-done.noise_ref = bf16[16,64,128]{2,1,0:T(8,128)(2,1)S(1)} async-done(((bf16[16,64,128]{2,1,0:T(8,128)(2,1)}), bf16[16,64,128]{2,1,0:T(8,128)(2,1)S(1)}, u32[]{:S(2)}, u32[]{:S(2)}) %all-to-all-start) | async-done | bytes 262176 | tf_op jit(solution)/shard_map/all_to_all | solution.py:265
  17.3 1.3 copy-done.1
  18.6 2.3 %make_fakes.1 = (bf16[272,2304]{1,0:T(8,128)(2,1)S(1)}, bf16[32,640]{1,0:T(8,128)(2,1)S(1)}) custom-call(s32[2]{0:T(128)S(1)} %bitcast.39, bf16[16,64,128]{2,1,0:T(8,128)(2,1)S(1)} %all-to-all-done.noise_ref, f32[256,128]{1,0:T(8,128)S(1)} %bitcast.29, f32[32,256]{1,0:T(8,128)S(1)} %bitcast.33, ...), custom_call_target="tpu_custom_call", output_to_operand_aliasing={{0}: (7, {})} | custom-call | tf_op jit(solution)/shard_map/make_fakes/pallas_call | solution.py:284
  22.0 4.7 %first_step.1 = (bf16[16,32,512]{2,1,0:T(8,128)(2,1)}, f32[32,256]{1,0:T(8,128)S(1)}, bf16[256,2304]{1,0:T(8,128)(2,1)S(1)}, f32[1,256]{1,0:T(1,128)S(1)}, f32[8,128]{1,0:T(8,128)S(1)}) custom-call(bf16[32,640]{1,0:T(8,128)(2,1)S(1)} %get-tuple-element.26.images_ref, f32[32,256]{1,0:T(8,128)S(1)} %bitcast.32, f32[256,2304]{1,0:T(8,128)S(1)} %bitcast.28, ...), custom_call_target="tpu_custom_call" | custom-call | tf_op jit(solution)/shard_map/first_step/pallas_call | solution.py:248
  27.8 5.7 %all-to-all-start.1 = ((bf16[16,32,512]{2,1,0:T(8,128)(2,1)}), bf16[16,32,512]{2,1,0:T(8,128)(2,1)S(1)}, u32[]{:S(2)}, u32[]{:S(2)}) async-start(bf16[16,32,512]{2,1,0:T(8,128)(2,1)} %get-tuple-element.27), calls=%async_computation.1 | async-start | bytes 1048576 | tf_op jit(solution)/shard_map/all_to_all | solution.py:265
  33.4 7.4 %collective-permute-start.1 = (bf16[272,2304]{1,0:T(8,128)(2,1)}, bf16[272,2304]{1,0:T(8,128)(2,1)S(1)}, u32[]{:S(2)}, u32[]{:S(2)}) collective-permute-start(bf16[272,2304]{1,0:T(8,128)(2,1)} %copy-done.2), channel_id=1, source_target_pairs={{0,32},{16,48},{32,64},{48,80},{64,96},{80,112},{96,128},{112,144}... | collective-permute-start | bytes 3760136 | tf_op jit(solution)/shard_map/ppermute | solution.py:261
  40.8 1.4 all-to-all-done.1.pulls_ref
  42.2 5.1 %generator_step.1 = (bf16[32,640]{1,0:T(8,128)(2,1)S(1)}, f32[256,128]{1,0:T(8,128)S(1)}, f32[32,256]{1,0:T(8,128)S(1)}) custom-call(s32[2]{0:T(128)S(1)} %bitcast.40, bf16[16,32,512]{2,1,0:T(8,128)(2,1)S(1)} %all-to-all-done.1.pulls_ref, bf16[16,64,128]{2,1,0:T(8,128)(2,1)S(1)} %all-to-all-done.noise_ref, f32[256,128]{1,0:T(8,128)S(1)} %bitcast.30, ...), custom_call_target="tpu_custom_call" | custom-call | tf_op jit(solution)/shard_map/generator_step/pallas_call | solution.py:248
  47.2 63.2 %collective-permute-start.2 = (bf16[32,640]{1,0:T(8,128)(2,1)S(1)}, bf16[32,640]{1,0:T(8,128)(2,1)S(1)}, u32[]{:S(2)}, u32[]{:S(2)}) collective-permute-start(bf16[32,640]{1,0:T(8,128)(2,1)S(1)} %get-tuple-element.28), channel_id=1, source_target_pairs={{0,496},{16,0},{32,16},{48,32},{64,48},{80,64},{96,80},{112,96},{1... | collective-permute-start | bytes 122888 | tf_op jit(solution)/shard_map/ppermute | solution.py:261
  110.4 1.7 %collective-permute-done.2.images_ref = bf16[32,640]{1,0:T(8,128)(2,1)S(1)} collective-permute-done((bf16[32,640]{1,0:T(8,128)(2,1)S(1)}, bf16[32,640]{1,0:T(8,128)(2,1)S(1)}, u32[]{:S(2)}, u32[]{:S(2)}) %collective-permute-start.2) | collective-permute-done | bytes 40992 | tf_op jit(solution)/shard_map/ppermute | solution.py:261
  112.1 1.3 copy-done.4
  113.4 3.6 %second_pull.1 = bf16[32,640]{1,0:T(8,128)(2,1)S(1)} custom-call(bf16[32,640]{1,0:T(8,128)(2,1)S(1)} %collective-permute-done.2.images_ref, f32[32,256]{1,0:T(8,128)S(1)} %get-tuple-element.36.lift_ref, bf16[256,2304]{1,0:T(8,128)(2,1)S(1)} %copy-done.4, f32[1,256]{1,0:T(1,128)S(1)} %get-tuple-element.38.head_ref), custom_call_target="tpu_custom_call" | custom-call | tf_op jit(solution)/shard_map/second_pull/pallas_call | solution.py:248
  116.9 1.9 %collective-permute-start.3 = (bf16[32,640]{1,0:T(8,128)(2,1)S(1)}, bf16[32,640]{1,0:T(8,128)(2,1)S(1)}, u32[]{:S(2)}, u32[]{:S(2)}) collective-permute-start(bf16[32,640]{1,0:T(8,128)(2,1)S(1)} %second_pull.1), channel_id=1, source_target_pairs={{0,16},{16,32},{32,48},{48,64},{64,80},{80,96},{96,112},{112,128},... | collective-permute-start | bytes 122888 | tf_op jit(solution)/shard_map/ppermute | solution.py:261
  118.9 9.1 %collective-permute-done.3 = bf16[32,640]{1,0:T(8,128)(2,1)S(1)} collective-permute-done((bf16[32,640]{1,0:T(8,128)(2,1)S(1)}, bf16[32,640]{1,0:T(8,128)(2,1)S(1)}, u32[]{:S(2)}, u32[]{:S(2)}) %collective-permute-start.3) | collective-permute-done | bytes 40992 | tf_op jit(solution)/shard_map/ppermute | solution.py:261
  128.8 5.4 %all-to-all-start.2 = ((bf16[16,32,512]{2,1,0:T(8,128)(2,1)}), bf16[16,32,512]{2,1,0:T(8,128)(2,1)S(1)}, u32[]{:S(2)}, u32[]{:S(2)}) async-start(bf16[16,32,512]{2,1,0:T(8,128)(2,1)} %broadcast_in_dim.36), calls=%async_computation.2 | async-start | bytes 1048576 | tf_op jit(solution)/shard_map/all_to_all | solution.py:265
  134.7 1.9 %collective-permute-start = (bf16[32,640]{1,0:T(8,128)(2,1)S(1)}, bf16[32,640]{1,0:T(8,128)(2,1)S(1)}, u32[]{:S(2)}, u32[]{:S(2)}) collective-permute-start(bf16[32,640]{1,0:T(8,128)(2,1)S(1)} %get-tuple-element.28), channel_id=1, source_target_pairs={{0,16},{16,32},{32,48},{48,64},{64,80},{80,96},{96,112},{112,128},... | collective-permute-start | bytes 122888 | tf_op jit(solution)/shard_map/ppermute | solution.py:261
  137.2 1.9 %maximum_bitcast_fusion = f32[1,1,2,1]{2,3,1,0:T(1,128)} fusion(f32[1]{0:T(128)} %bitcast.20, f32[1]{0:T(128)} %bitcast.19), kind=kLoop, calls=%fused_computation.2 | loop fusion | flops 2 | bytes 16 | tf_op jit(solution)/shard_map/broadcast_in_dim;broadcast_in_dim | solution.py:345
  139.1 4.7 %moved_first.1 = (f32[32,256]{1,0:T(8,128)S(1)}, f32[256,2304]{1,0:T(8,128)S(1)}, f32[1,256]{1,0:T(1,128)S(1)}) custom-call(bf16[272,2304]{1,0:T(8,128)(2,1)S(1)} %collective-permute-done.1.packed_ref), custom_call_target="tpu_custom_call" | custom-call | tf_op jit(solution)/shard_map/moved_first/pallas_call | solution.py:248
  143.8 1.5 collective-permute-done.images_ref
  145.3 6.1 %moved_second.1 = (f32[32,256]{1,0:T(8,128)}, f32[256,2304]{1,0:T(8,128)}, f32[1,256]{1,0:T(1,128)}) custom-call(bf16[32,640]{1,0:T(8,128)(2,1)S(1)} %collective-permute-done.images_ref, f32[32,256]{1,0:T(8,128)S(1)} %get-tuple-element.30.lift_ref, f32[256,2304]{1,0:T(8,128)S(1)} %get-tuple-element.31.kernel_ref, f32[1,256]{1,0:T(1,128)S(1)} %get-tuple-element.32.head_ref), custom_call_target="tpu_custom_call" | custom-call | tf_op jit(solution)/shard_map/moved_second/pallas_call | solution.py:248
  151.3 3.7 %generator_last.1 = (f32[256,128]{1,0:T(8,128)}, f32[32,256]{1,0:T(8,128)}, f32[32,32]{1,0:T(8,128)}) custom-call(s32[1]{0:T(128)} %bitcast.15.place_ref, bf16[16,32,512]{2,1,0:T(8,128)(2,1)S(1)} %all-to-all-done.2.pulls_ref, bf16[16,64,128]{2,1,0:T(8,128)(2,1)S(1)} %all-to-all-done.noise_ref, f32[256,128]{1,0:T(8,128)S(1)} %get-tuple-element.39.first_ref, ...), custom_call_target="tpu_custom_call" | custom-call | tf_op jit(solution)/shard_map/generator_last/pallas_call | solution.py:248
  (27 shorter events, 5.2 us)
Async XLA Ops:
  2.1 15.1 %all-to-all-start = ((bf16[16,64,128]{2,1,0:T(8,128)(2,1)}), bf16[16,64,128]{2,1,0:T(8,128)(2,1)S(1)}, u32[]{:S(2)}, u32[]{:S(2)}) async-start(bf16[16,64,128]{2,1,0:T(8,128)(2,1)} %broadcast_in_dim.32), calls=%async_computation | async-start | bytes 524288 | tf_op jit(solution)/shard_map/all_to_all | solution.py:265
  11.3 5.9 %copy-start.5 = (f32[1,256,128]{2,1,0:T(8,128)S(1)}, f32[1,256,128]{2,1,0:T(8,128)}, u32[]{:S(2)}) copy-start(f32[1,256,128]{2,1,0:T(8,128)} %param.11) | copy-start | bytes 393220
  11.3 5.9 %copy-start.8 = (bf16[1,1,4,32,64]{4,3,2,1,0:T(8,128)(2,1)S(1)}, bf16[1,1,4,32,64]{4,3,2,1,0:T(8,128)(2,1)}, u32[]{:S(2)}) copy-start(bf16[1,1,4,32,64]{4,3,2,1,0:T(8,128)(2,1)} %param.8) | copy-start | bytes 49156
  13.2 4.1 %copy-start.6 = (f32[1,1,256,32]{2,3,1,0:T(8,128)S(1)}, f32[1,1,256,32]{2,3,1,0:T(8,128)}, u32[]{:S(2)}) copy-start(f32[1,1,256,32]{2,3,1,0:T(8,128)} %param.13) | copy-start | bytes 98308
  13.2 4.1 %copy-start.7 = (f32[1,32,256]{2,1,0:T(8,128)S(1)}, f32[1,32,256]{2,1,0:T(8,128)}, u32[]{:S(2)}) copy-start(f32[1,32,256]{2,1,0:T(8,128)} %param.12) | copy-start | bytes 98308
  13.2 4.1 %copy-start.9 = (f32[1,1,256]{2,1,0:T(1,128)S(1)}, f32[1,1,256]{2,1,0:T(1,128)}, u32[]{:S(2)}) copy-start(f32[1,1,256]{2,1,0:T(1,128)} %param.15) | copy-start | bytes 3076
  13.2 4.1 %copy-start.10 = (s32[1,1,2,1]{2,3,1,0:T(1,128)S(1)}, s32[1,1,2,1]{2,3,1,0:T(1,128)}, u32[]{:S(2)}) copy-start(s32[1,1,2,1]{2,3,1,0:T(1,128)} %param.9) | copy-start | bytes 28
  13.2 8.8 %copy-start = (f32[1,1,256,2304]{3,2,1,0:T(8,128)S(1)}, f32[1,1,256,2304]{3,2,1,0:T(8,128)}, u32[]{:S(2)}) copy-start(f32[1,1,256,2304]{3,2,1,0:T(8,128)} %param.14) | copy-start | bytes 7077892
  17.3 1.3 copy-start.1
  20.9 1.1 copy-start.2
  26.7 1.0 copy-start.3
  27.8 14.4 %all-to-all-start.1 = ((bf16[16,32,512]{2,1,0:T(8,128)(2,1)}), bf16[16,32,512]{2,1,0:T(8,128)(2,1)S(1)}, u32[]{:S(2)}, u32[]{:S(2)}) async-start(bf16[16,32,512]{2,1,0:T(8,128)(2,1)} %get-tuple-element.27), calls=%async_computation.1 | async-start | bytes 1048576 | tf_op jit(solution)/shard_map/all_to_all | solution.py:265
  33.4 105.7 %collective-permute-start.1 = (bf16[272,2304]{1,0:T(8,128)(2,1)}, bf16[272,2304]{1,0:T(8,128)(2,1)S(1)}, u32[]{:S(2)}, u32[]{:S(2)}) collective-permute-start(bf16[272,2304]{1,0:T(8,128)(2,1)} %copy-done.2), channel_id=1, source_target_pairs={{0,32},{16,48},{32,64},{48,80},{64,96},{80,112},{96,128},{112,144}... | collective-permute-start | bytes 3760136 | tf_op jit(solution)/shard_map/ppermute | solution.py:261
  47.2 64.9 %collective-permute-start.2 = (bf16[32,640]{1,0:T(8,128)(2,1)S(1)}, bf16[32,640]{1,0:T(8,128)(2,1)S(1)}, u32[]{:S(2)}, u32[]{:S(2)}) collective-permute-start(bf16[32,640]{1,0:T(8,128)(2,1)S(1)} %get-tuple-element.28), channel_id=1, source_target_pairs={{0,496},{16,0},{32,16},{48,32},{64,48},{80,64},{96,80},{112,96},{1... | collective-permute-start | bytes 122888 | tf_op jit(solution)/shard_map/ppermute | solution.py:261
  112.1 1.3 copy-start.4
  116.9 11.0 %collective-permute-start.3 = (bf16[32,640]{1,0:T(8,128)(2,1)S(1)}, bf16[32,640]{1,0:T(8,128)(2,1)S(1)}, u32[]{:S(2)}, u32[]{:S(2)}) collective-permute-start(bf16[32,640]{1,0:T(8,128)(2,1)S(1)} %second_pull.1), channel_id=1, source_target_pairs={{0,16},{16,32},{32,48},{48,64},{64,80},{80,96},{96,112},{112,128},... | collective-permute-start | bytes 122888 | tf_op jit(solution)/shard_map/ppermute | solution.py:261
  128.8 22.5 %all-to-all-start.2 = ((bf16[16,32,512]{2,1,0:T(8,128)(2,1)}), bf16[16,32,512]{2,1,0:T(8,128)(2,1)S(1)}, u32[]{:S(2)}, u32[]{:S(2)}) async-start(bf16[16,32,512]{2,1,0:T(8,128)(2,1)} %broadcast_in_dim.36), calls=%async_computation.2 | async-start | bytes 1048576 | tf_op jit(solution)/shard_map/all_to_all | solution.py:265
  134.7 10.5 %collective-permute-start = (bf16[32,640]{1,0:T(8,128)(2,1)S(1)}, bf16[32,640]{1,0:T(8,128)(2,1)S(1)}, u32[]{:S(2)}, u32[]{:S(2)}) collective-permute-start(bf16[32,640]{1,0:T(8,128)(2,1)S(1)} %get-tuple-element.28), channel_id=1, source_target_pairs={{0,16},{16,32},{32,48},{48,64},{64,80},{80,96},{96,112},{112,128},... | collective-permute-start | bytes 122888 | tf_op jit(solution)/shard_map/ppermute | solution.py:261

commit v2 on v1

--- a/solution.py
+++ b/solution.py
@@ -17,6 +17,9 @@
 ROWS = 576
 WIDE = 640
 KW = TAPS * CH
+PART_A = 96
+PART_B = 80
+PART_C = CH - PART_A - PART_B
 
 critic_rate = 0.05
 generator_rate = 0.2
@@ -116,7 +119,11 @@
 
 
 def latents_of(noise_ref, round_index):
-    return noise_ref[:, C * round_index : C * (round_index + 1), :].reshape(FAKE, 128).astype(f32)
+    halves = []
+    for z in range(2):
+        start = 2 * C * z + C * round_index
+        halves.append(noise_ref[:, start : start + C, :].reshape(FAKE // 2, 128))
+    return jnp.concatenate(halves, axis=0).astype(f32)
 
 
 def put_images(images_ref, fakes, real):
@@ -124,21 +131,43 @@
     images_ref[:, FAKE:] = jnp.concatenate([real, jnp.zeros_like(real)], axis=1)
 
 
-def generate_kernel(pick_ref, noise_ref, first_ref, second_ref, pool_ref, lift_ref, head_ref, packed_in, packed_ref, images_ref):
+def noise_copies_kernel(place_ref, own_ref, other_ref, copies_ref):
+    own_first = place_ref[0] < 8
+    own = own_ref[...].astype(f32)
+    other = other_ref[...].astype(f32)
+    low = jnp.where(own_first, own, other).astype(bf16)
+    high = jnp.where(own_first, other, own).astype(bf16)
+    for j in range(8):
+        copies_ref[j, : 2 * C] = low
+        copies_ref[j, 2 * C :] = high
+
+
+def pair_copies_kernel(own_ref, other_ref, copies_ref):
+    pair = (own_ref[...].astype(f32) + other_ref[...].astype(f32)).astype(bf16)
+    for j in range(8):
+        copies_ref[j] = pair
+
+
+def sum_of(pulls_ref):
+    total = pulls_ref[0].astype(f32)
+    for j in range(1, 8):
+        total = total + pulls_ref[j].astype(f32)
+    return total
+
+
+def sum_kernel(pulls_ref, score_ref, out_ref):
+    out_ref[:, :FAKE] = sum_of(pulls_ref).astype(bf16)
+    out_ref[:, FAKE:] = score_ref[...]
+
+
+def generate_kernel(pick_ref, noise_ref, first_ref, second_ref, pool_ref, images_ref):
     latents = latents_of(noise_ref, 0)
     inner = exact_dot(latents, first_ref[...], NT)
     fakes = exact_dot(second_ref[...], inner * sigmoid(inner), NT)
     put_images(images_ref, fakes, real_image(pool_ref, pick_ref, 0))
-    packed_ref[:, :WIDE] = images_ref[:16]
-    packed_ref[:, WIDE : 2 * WIDE] = images_ref[16:]
-    lift = lift_ref[...].astype(bf16)
-    packed_ref[:, 1280:1536] = lift[:16]
-    packed_ref[:, 1536:1792] = lift[16:]
-    packed_ref[:, 1792:2048] = jnp.broadcast_to(head_ref[...], (16, CH)).astype(bf16)
-    packed_ref[:, 2048:] = jnp.zeros((16, KW - 2048), bf16)
-
-
-def first_step_kernel(images_ref, lift_ref, kernel_ref, head_ref, copies_ref, lift_out, kernel_out, head_out, score_out, patch_ref, half_ref):
+
+
+def first_step_kernel(images_ref, lift_ref, kernel_ref, head_ref, pull_ref, lift_out, kernel_out, head_out, score_out, rest_out, patch_ref, half_ref):
     for t in range(TAPS):
         half_ref[t] = kernel_ref[:, CH * t : CH * (t + 1)].astype(bf16)
     lift = lift_ref[...]
@@ -148,37 +177,49 @@
     slope, z_grad, head_grad, score = critic_forward(images, lift_half, lambda t: half_ref[t], head, patch_ref)
     z_half = z_grad.astype(bf16)
     pre_grad = lift_pullback(slope, z_half, lambda t: half_ref[t])
-    pull = (-8.0 * dot(lift_half, pre_grad, NT)[:, :FAKE]).astype(bf16)
-    for j in range(N_GRP):
-        copies_ref[j] = pull
+    pull_ref[...] = (-8.0 * dot(lift_half, pre_grad, NT)[:, :FAKE]).astype(bf16)
     lift_out[...] = lift - critic_rate * dot(images[:, :ROWS], pre_grad)
     head_out[...] = head - critic_rate * head_grad
     z_turned = jnp.transpose(z_grad).astype(bf16)
     for t in range(TAPS):
         cols = slice(CH * t, CH * (t + 1))
         kernel_out[:, cols] = (kernel_ref[:, cols] - critic_rate * dot(z_turned, patch_ref[t])).astype(bf16)
+        rest_out[:PART_C, cols] = half_ref[t, CH - PART_C :, :]
+    rest_out[PART_C:, :WIDE] = images[:16]
+    rest_out[PART_C:, WIDE : 2 * WIDE] = images[16:]
+    rest_out[PART_C:, 1280:1536] = lift_half[:16]
+    rest_out[PART_C:, 1536:1792] = lift_half[16:]
+    rest_out[PART_C:, 1792:2048] = jnp.broadcast_to(head, (16, CH)).astype(bf16)
+    rest_out[PART_C:, 2048:] = jnp.zeros((16, KW - 2048), bf16)
     score_out[...] = jnp.broadcast_to(score, (8, 128))
 
 
-def pull_only_kernel(images_ref, lift_ref, kernel_ref, head_ref, pull_ref, patch_ref):
+def pull_only_kernel(images_ref, lift_ref, kernel_ref, head_ref, copies_ref, score_ref, patch_ref):
     lift_half = lift_ref[...].astype(bf16)
     kernel_of = lambda t: kernel_ref[:, CH * t : CH * (t + 1)]
     slope, z_grad, _, score = critic_forward(images_ref[...], lift_half, kernel_of, head_ref[...], patch_ref)
     pre_grad = lift_pullback(slope, z_grad.astype(bf16), kernel_of)
-    pull_ref[:, :FAKE] = (-8.0 * dot(lift_half, pre_grad, NT)[:, :FAKE]).astype(bf16)
+    pull = (-8.0 * dot(lift_half, pre_grad, NT)[:, :FAKE]).astype(bf16)
+    for j in range(8):
+        copies_ref[j] = pull
     high = score.astype(bf16)
     middle = (score - high.astype(f32)).astype(bf16)
     low = (score - high.astype(f32) - middle.astype(f32)).astype(bf16)
     lane = lax.broadcasted_iota(jnp.int32, (C, 128), 1)
     three = jnp.where(lane == 0, high.astype(f32), jnp.where(lane == 1, middle.astype(f32), jnp.where(lane == 2, low.astype(f32), 0.0)))
-    pull_ref[:, FAKE:] = three.astype(bf16)
-
-
-def moved_first_kernel(packed_ref, lift_out, kernel_out, head_out, patch_ref):
-    images = jnp.concatenate([packed_ref[CH:, :WIDE], packed_ref[CH:, WIDE : 2 * WIDE]], axis=0)
-    lift_half = jnp.concatenate([packed_ref[CH:, 1280:1536], packed_ref[CH:, 1536:1792]], axis=0)
-    head = packed_ref[CH:, 1792:2048].astype(f32)[:1]
-    kernel_of = lambda t: packed_ref[:CH, CH * t : CH * (t + 1)]
+    score_ref[...] = three.astype(bf16)
+
+
+def moved_first_kernel(part_a, part_b, part_c, lift_out, kernel_out, head_out, patch_ref, half_ref):
+    for t in range(TAPS):
+        cols = slice(CH * t, CH * (t + 1))
+        half_ref[t, :PART_A] = part_a[:, cols]
+        half_ref[t, PART_A : PART_A + PART_B] = part_b[:, cols]
+        half_ref[t, PART_A + PART_B :] = part_c[:PART_C, cols]
+    images = jnp.concatenate([part_c[PART_C:, :WIDE], part_c[PART_C:, WIDE : 2 * WIDE]], axis=0)
+    lift_half = jnp.concatenate([part_c[PART_C:, 1280:1536], part_c[PART_C:, 1536:1792]], axis=0)
+    head = part_c[PART_C:, 1792:2048].astype(f32)[:1]
+    kernel_of = lambda t: half_ref[t]
     slope, z_grad, head_grad, _ = critic_forward(images, lift_half, kernel_of, head, patch_ref)
     pre_grad = lift_pullback(slope, z_grad.astype(bf16), kernel_of)
     lift_out[...] = lift_half.astype(f32) - critic_rate * dot(images[:, :ROWS], pre_grad)
@@ -205,20 +246,17 @@
         kernel_out[:, cols] = kernel_ref[:, cols] - critic_rate * dot(z_turned, patch_ref[t])
 
 
-def generator_step(pulls_ref, latents, first, second):
-    total = pulls_ref[0].astype(f32)
-    for j in range(1, N_GRP):
-        total = total + pulls_ref[j].astype(f32)
+def generator_step(total, latents, first, second):
     inner = exact_dot(latents, first, NT)
     gate = sigmoid(inner)
     second_grad = exact_dot(total, inner * gate)
     inner_grad = exact_dot(jnp.transpose(total), second) * (gate * (1.0 + inner * (1.0 - gate)))
     first_grad = exact_dot(jnp.transpose(inner_grad), latents)
-    return total, first - generator_rate * first_grad, second - generator_rate * second_grad
+    return first - generator_rate * first_grad, second - generator_rate * second_grad
 
 
 def middle_kernel(pick_ref, pulls_ref, noise_ref, first_ref, second_ref, pool_ref, images_ref, first_out, second_out):
-    _, first, second = generator_step(pulls_ref, latents_of(noise_ref, 0), first_ref[...], second_ref[...])
+    first, second = generator_step(sum_of(pulls_ref), latents_of(noise_ref, 0), first_ref[...], second_ref[...])
     first_out[...] = first
     second_out[...] = second
     inner = exact_dot(latents_of(noise_ref, 1), first, NT)
@@ -226,14 +264,17 @@
     put_images(images_ref, fakes, real_image(pool_ref, pick_ref, 1))
 
 
-def last_kernel(place_ref, pulls_ref, noise_ref, first_ref, second_ref, first_out, second_out, own_out):
-    total, first, second = generator_step(pulls_ref, latents_of(noise_ref, 1), first_ref[...], second_ref[...])
+def last_kernel(place_ref, same_ref, cross_ref, noise_ref, first_ref, second_ref, score_ref, first_out, second_out, own_out, scores_out):
+    total = same_ref[:, :FAKE].astype(f32) + cross_ref[:, :FAKE].astype(f32)
+    first, second = generator_step(total, latents_of(noise_ref, 1), first_ref[...], second_ref[...])
     first_out[...] = first
     second_out[...] = second
     own = jnp.zeros((C, C), f32)
     for j in range(N_GRP):
         own = own + jnp.where(place_ref[0] == j, total[:, C * j : C * (j + 1)], 0.0)
     own_out[...] = own
+    scores_out[0, 0] = jnp.max(score_ref[...])
+    scores_out[1, 0] = jnp.sum(same_ref[:, FAKE:].astype(f32)[:1])
 
 
 def vmem(*_):
@@ -252,7 +293,7 @@
         in_specs=[smem()] * scalars + [vmem()] * (len(ins) - scalars),
         out_specs=[vmem()] * len(outs),
         scratch_shapes=list(scratch),
-        compiler_params=pltpu.CompilerParams(vmem_limit_bytes=40 * 1024 * 1024),
+        compiler_params=pltpu.CompilerParams(vmem_limit_bytes=24 * 1024 * 1024),
     )(*ins)
 
 
@@ -261,8 +302,24 @@
     return lax.ppermute(value, "loop", [(s, (s + steps) % count) for s in range(count)])
 
 
+def across(value):
+    return lax.ppermute(value, "grp", [(m, m ^ 8) for m in range(N_GRP)])
+
+
+def shifted_across(value, steps):
+    count = lax.axis_size("loop")
+    pairs = [(l * N_GRP + m, (l + steps) % count * N_GRP + (m ^ 8)) for l in range(count) for m in range(N_GRP)]
+    return lax.ppermute(value, ("loop", "grp"), pairs)
+
+
 def swap(copies):
-    return lax.all_to_all(copies, "grp", 0, 0)
+    count = lax.axis_size("loop")
+    groups = [[8 * i + j for j in range(8)] for i in range(2 * count)]
+    return lax.all_to_all(copies, ("loop", "grp"), 0, 0, axis_index_groups=groups)
+
+
+def together(*values):
+    return lax.optimization_barrier(values)
 
 
 PATCHES = pltpu.VMEM((TAPS, ROWS, CH), bf16)
@@ -277,30 +334,32 @@
     kernel = critic_kernel[0, 0]
     head = critic_head[0, 0][None]
 
+    place = lax.axis_index("grp").astype(jnp.int32)[None]
     own_noise = jnp.swapaxes(noise_latents[0], 1, 2).reshape(ROUNDS * C, 128)
-    noise = swap(jnp.broadcast_to(own_noise[None], (N_GRP,) + own_noise.shape))
-
-    packed = jnp.pad(kernel.astype(bf16), ((0, 16), (0, 0)))
-    packed, images = pl.pallas_call(
-        generate_kernel,
-        name="make_fakes",
-        grid=(1,),
-        out_shape=[jax.ShapeDtypeStruct((CH + 16, KW), bf16), jax.ShapeDtypeStruct((C, WIDE), bf16)],
-        in_specs=[smem()] + [vmem()] * 6 + [pl.BlockSpec(memory_space=pl.ANY)],
-        out_specs=[pl.BlockSpec((16, KW), lambda i: (CH // 16, 0)), vmem()],
-        input_output_aliases={7: 0},
-        compiler_params=pltpu.CompilerParams(vmem_limit_bytes=40 * 1024 * 1024),
-    )(pick, noise, first, second, pool, lift, head, packed)
-
-    moved = shifted(packed, 2)
-
-    copies, lift_1, kernel_1, head_1, score_0 = call(
+    other_noise = across(own_noise)
+    part_a = kernel[:PART_A].astype(bf16)
+    part_b = kernel[PART_A : PART_A + PART_B].astype(bf16)
+    part_a, other_noise = together(part_a, other_noise)
+    moved_a = shifted(part_a, 2)
+    (copies,) = call(
+        noise_copies_kernel, "noise_copies", [((8, 4 * C, 128), bf16)], (place, own_noise, other_noise), scalars=1
+    )
+    noise = swap(copies)
+    (images,) = call(
+        generate_kernel, "make_fakes", [((C, WIDE), bf16)], (pick, noise, first, second, pool), scalars=1
+    )
+    pull, lift_1, kernel_1, head_1, score_0, part_c = call(
         first_step_kernel,
         "first_step",
-        [((N_GRP, C, FAKE), bf16), ((C, CH), f32), ((CH, KW), bf16), ((1, CH), f32), ((8, 128), f32)],
+        [((C, FAKE), bf16), ((C, CH), f32), ((CH, KW), bf16), ((1, CH), f32), ((8, 128), f32), ((PART_C + 16, KW), bf16)],
         (images, lift, kernel, head),
         (PATCHES, HALVES),
     )
+    pull, moved_a = together(pull, moved_a)
+    other_pull = across(pull)
+    part_b, other_pull = together(part_b, other_pull)
+    moved_b = shifted(part_b, 2)
+    (copies,) = call(pair_copies_kernel, "pair_copies", [((8, C, FAKE), bf16)], (pull, other_pull))
     pulls = swap(copies)
     own_images, first_1, second_1 = call(
         middle_kernel,
@@ -309,14 +368,29 @@
         (pick, pulls, noise, first, second, pool),
         scalars=1,
     )
+    own_images, moved_b = together(own_images, moved_b)
     ahead_images = shifted(own_images, -1)
-    (pull,) = call(pull_only_kernel, "second_pull", [((C, WIDE), bf16)], (ahead_images, lift_1, kernel_1, head_1), (PATCHES,))
     behind_images = shifted(own_images, 1)
-    own_pull = shifted(pull, 1)
-    pulls = swap(jnp.broadcast_to(own_pull[None, :, :FAKE], (N_GRP, C, FAKE)))
+    part_c, ahead_images, behind_images = together(part_c, ahead_images, behind_images)
+    moved_c = shifted(part_c, 2)
+    copies, score_1 = call(
+        pull_only_kernel,
+        "second_pull",
+        [((8, C, FAKE), bf16), ((C, 128), bf16)],
+        (ahead_images, lift_1, kernel_1, head_1),
+        (PATCHES,),
+    )
+    (partial,) = call(sum_kernel, "sum_pulls", [((C, WIDE), bf16)], (swap(copies), score_1))
+    partial, moved_c = together(partial, moved_c)
+    same = shifted(partial, 1)
+    cross = shifted_across(partial, 1)
 
     moved_lift, moved_kernel, moved_head = call(
-        moved_first_kernel, "moved_first", [((C, CH), f32), ((CH, KW), f32), ((1, CH), f32)], (moved,), (PATCHES,)
+        moved_first_kernel,
+        "moved_first",
+        [((C, CH), f32), ((CH, KW), f32), ((1, CH), f32)],
+        (moved_a, moved_b, moved_c),
+        (PATCHES, HALVES),
     )
     lift_2, kernel_2, head_2 = call(
         moved_second_kernel,
@@ -325,16 +399,19 @@
         (behind_images, moved_lift, moved_kernel, moved_head),
         (PATCHES, HALVES),
     )
-    place = lax.axis_index("grp").astype(jnp.int32)[None]
-    first_2, second_2, own_grad = call(
+    first_2, second_2, own_grad, scores = pl.pallas_call(
         last_kernel,
-        "generator_last",
-        [((CH, 128), f32), ((C, CH), f32), ((C, C), f32)],
-        (place, pulls, noise, first_1, second_1),
-        scalars=1,
-    )
-    score_1 = jnp.sum(own_pull[0, FAKE : FAKE + 3].astype(f32))
-    scores = jnp.stack([score_0[0, 0], score_1])[:, None]
+        name="generator_last",
+        out_shape=[
+            jax.ShapeDtypeStruct((CH, 128), f32),
+            jax.ShapeDtypeStruct((C, CH), f32),
+            jax.ShapeDtypeStruct((C, C), f32),
+            jax.ShapeDtypeStruct((ROUNDS, 1), f32),
+        ],
+        in_specs=[smem()] + [vmem()] * 6,
+        out_specs=[vmem()] * 3 + [smem()],
+        compiler_params=pltpu.CompilerParams(vmem_limit_bytes=24 * 1024 * 1024),
+    )(place, same, cross, noise, first_1, second_1, score_0)
     return (
         jnp.swapaxes(lift_2, 0, 1)[None, None],
         kernel_2[None, None],

time: 156 us -> 134 us (0.86)
  starting transfers between devices: 94.6 us -> 46.6 us
  blocking collectives: 0 us -> 30.6 us
  local copies, waits for them, and re-layouts: 8.65 us -> 1.99 us
  waiting for transfers between devices: 16.6 us -> 18.7 us
  other arithmetic: 4.3 us -> 2.56 us
    ppermute x4 -> x6, starting transfers between devices: 74.4 us -> 34.2 us  [shifted(): lax.ppermute(value, 'loop', [(s, (s + steps) % count) for s in range(coun...]
    all_to_all x0 -> x3, blocking collectives: none -> 30.6 us  [swap(): lax.all_to_all(copies, ('loop', 'grp'), 0, 0, axis_index_groups=groups)]
    all_to_all x3 -> x0, starting transfers between devices: 20.2 us -> none  [swap(): return lax.all_to_all(copies, 'grp', 0, 0)]
    ppermute x0 -> x3, starting transfers between devices: none -> 12.4 us  [the longest x2 6.19 us: across(): return lax.ppermute(value, 'grp', [(m, m ^ 8) for m in range(N_GRP)])]
    all_to_all x3 -> x0, waiting for transfers between devices: 4.27 us -> none  [swap(): return lax.all_to_all(copies, 'grp', 0, 0)]
    unnamed x22 -> x18, local copies, waits for them, and re-layouts: 4.67 us -> 0.95 us
    ppermute x4 -> x6, waiting for transfers between devices: 12.3 us -> 15.8 us  [shifted(): lax.ppermute(value, 'loop', [(s, (s + steps) % count) for s in range(coun...]
    ppermute x0 -> x3, waiting for transfers between devices: none -> 2.87 us  [the longest x2 2.86 us: across(): return lax.ppermute(value, 'grp', [(m, m ^ 8) for m in range(N_GRP)])]
  transfers between devices with their start and end apart: 7 -> 9, of which waited for: 5 -> 5; matrix products, arithmetic and copies ran while one was open for 4% -> 2% of each run, Pallas kernels for 12% -> 20%
where the time goes in v2:
time: 134 us; the launch traced here: 131 us
  starting transfers between devices  46.6 us (35%)
  blocking collectives  30.6 us (23%)
  Pallas kernels  30.2 us (23%)
  waiting for transfers between devices  18.7 us (14%)
  other arithmetic  2.56 us (2%)
  local copies, waits for them, and re-layouts  1.99 us (1%)
    ppermute x6, starting transfers between devices, shifted(): lax.ppermute(value, 'loop', [(s, (s + steps) % count) for s in range(coun...  34.2 us
    all_to_all x3, blocking collectives, swap(): lax.all_to_all(copies, ('loop', 'grp'), 0, 0, axis_index_groups=groups)  30.6 us
    pallas_call x9, Pallas kernels, call(): pl.pallas_call(kernel, name=name, out_shape=[jax.ShapeDtypeStruct(s, d) f...  26.6 us
    ppermute x6, waiting for transfers between devices, shifted(): lax.ppermute(value, 'loop', [(s, (s + steps) % count) for s in range(coun...  15.8 us
    ppermute x2, starting transfers between devices, across(): return lax.ppermute(value, 'grp', [(m, m ^ 8) for m in range(N_GRP)])  6.19 us
    ppermute x1, starting transfers between devices, shifted_across(): return lax.ppermute(value, ('loop', 'grp'), pairs)  6.17 us
    pallas_call x1, Pallas kernels, per_device(): pl.pallas_call(last_kernel, name='generator_last', out_shape=[jax.ShapeDt...  3.64 us
    ppermute x2, waiting for transfers between devices, across(): return lax.ppermute(value, 'grp', [(m, m ^ 8) for m in range(N_GRP)])  2.86 us
  transfers between devices with their start and end apart: 9, of which 5 were waited for; matrix products, arithmetic and copies ran while one was open for 2% of the time, Pallas kernels for 20%

profile of v2, /device:TPU:6, one launch (start us, length us, event | category | flops | bytes accessed | tf_op | source)
XLA Modules:
  0.0 131.5 jit_solution(4407013348248901593)
XLA Ops:
  0.6 4.3 %collective-permute-start = (bf16[64,128]{1,0:T(8,128)(2,1)}, bf16[64,128]{1,0:T(8,128)(2,1)S(1)}, u32[]{:S(2)}, u32[]{:S(2)}) collective-permute-start(bf16[64,128]{1,0:T(8,128)(2,1)} %bitcast.36), channel_id=1, source_target_pairs={{0,8},{1,9},{2,10},{3,11},{4,12},{5,13},{6,14},{7,15},{8,0},{9,1},... | collective-permute-start | bytes 49160 | tf_op jit(solution)/shard_map/ppermute | solution.py:306
  4.9 1.9 %convert.4 = bf16[1,1,256,2304]{3,2,1,0:T(8,128)(2,1)S(1)} convert(f32[1,1,256,2304]{3,2,1,0:T(8,128)} %param.14) | non-fusion elementwise | flops 589824 | bytes 3538944 | tf_op jit(solution)/shard_map/convert.1
  7.9 10.0 %collective-permute-start.1 = (bf16[96,2304]{1,0:T(8,128)(2,1)S(1)}, bf16[96,2304]{1,0:T(8,128)(2,1)S(1)}, u32[]{:S(2)}, u32[]{:S(2)}) collective-permute-start(bf16[96,2304]{1,0:T(8,128)(2,1)S(1)} %slice_bitcast_fusion), channel_id=1, source_target_pairs={{0,32},{16,48},{32,64},{48,80},{64,96},{80,112},{96,128},{112,144}... | collective-permute-start | bytes 1327112 | tf_op jit(solution)/shard_map/ppermute | solution.py:302
  18.0 10.0 %all_to_all.15.noise_ref = bf16[8,128,128]{2,1,0:T(8,128)(2,1)S(1)} all-to-all(bf16[8,128,128]{2,1,0:T(8,128)(2,1)S(1)} %noise_copies.1), channel_id=1, replica_groups={{0,1,2,3,4,5,6,7},{8,9,10,11,12,13,14,15},{16,17,18,19,20,21,22,23},{24..., dimensions={0} | all-to-all | bytes 524288 | tf_op jit(solution)/shard_map/all_to_all | solution.py:318
  28.0 2.3 %make_fakes.1.images_ref = bf16[32,640]{1,0:T(8,128)(2,1)S(1)} custom-call(s32[2]{0:T(128)S(1)} %bitcast.38, bf16[8,128,128]{2,1,0:T(8,128)(2,1)S(1)} %all_to_all.15.noise_ref, f32[256,128]{1,0:T(8,128)S(1)} %bitcast.29, f32[32,256]{1,0:T(8,128)S(1)} %bitcast.31, bf16[4,32,64]{2,1,0:T(8,128)(2,1)S(1)} %bitcast.33), custom_call_target="tpu_custom_call" | custom-call | tf_op jit(solution)/shard_map/make_fakes/pallas_call | solution.py:289
  30.4 4.7 %first_step.1 = (bf16[32,512]{1,0:T(8,128)(2,1)S(1)}, f32[32,256]{1,0:T(8,128)S(1)}, bf16[256,2304]{1,0:T(8,128)(2,1)S(1)}, f32[1,256]{1,0:T(1,128)S(1)}, f32[8,...) custom-call(bf16[32,640]{1,0:T(8,128)(2,1)S(1)} %make_fakes.1.images_ref, f32[32,256]{1,0:T(8,128)S(1)} %bitcast.35, ...), custom_call_target="tpu_custom_call" | custom-call | tf_op jit(solution)/shard_map/first_step/pallas_call | solution.py:289
  35.1 4.6 %collective-permute-done.1.part_a = bf16[96,2304]{1,0:T(8,128)(2,1)S(1)} collective-permute-done((bf16[96,2304]{1,0:T(8,128)(2,1)S(1)}, bf16[96,2304]{1,0:T(8,128)(2,1)S(1)}, u32[]{:S(2)}, u32[]{:S(2)}) %collective-permute-start.1) | collective-permute-done | bytes 442400 | tf_op jit(solution)/shard_map/ppermute | solution.py:302
  39.8 1.9 %collective-permute-start.2 = (bf16[32,512]{1,0:T(8,128)(2,1)S(1)}, bf16[32,512]{1,0:T(8,128)(2,1)S(1)}, u32[]{:S(2)}, u32[]{:S(2)}) collective-permute-start(bf16[32,512]{1,0:T(8,128)(2,1)S(1)} %get-tuple-element.45.own_ref), channel_id=1, source_target_pairs={{0,8},{1,9},{2,10},{3,11},{4,12},{5,13},{6,14},{7,15},{8,0},{9,1},... | collective-permute-start | bytes 98312 | tf_op jit(solution)/shard_map/ppermute | solution.py:306
  42.7 2.9 %collective-permute-done.2.other_ref = bf16[32,512]{1,0:T(8,128)(2,1)S(1)} collective-permute-done((bf16[32,512]{1,0:T(8,128)(2,1)S(1)}, bf16[32,512]{1,0:T(8,128)(2,1)S(1)}, u32[]{:S(2)}, u32[]{:S(2)}) %collective-permute-start.2) | collective-permute-done | bytes 32800 | tf_op jit(solution)/shard_map/ppermute | solution.py:306
  45.6 4.0 %collective-permute-start.3 = (bf16[80,2304]{1,0:T(8,128)(2,1)S(1)}, bf16[80,2304]{1,0:T(8,128)(2,1)S(1)}, u32[]{:S(2)}, u32[]{:S(2)}) collective-permute-start(bf16[80,2304]{1,0:T(8,128)(2,1)S(1)} %slice_bitcast_fusion.1), channel_id=1, source_target_pairs={{0,32},{16,48},{32,64},{48,80},{64,96},{80,112},{96,128},{112,144}... | collective-permute-start | bytes 1105928 | tf_op jit(solution)/shard_map/ppermute | solution.py:302
  49.6 10.0 %all_to_all.16.pulls_ref = bf16[8,32,512]{2,1,0:T(8,128)(2,1)S(1)} all-to-all(bf16[8,32,512]{2,1,0:T(8,128)(2,1)S(1)} %pair_copies.1), channel_id=1, replica_groups={{0,1,2,3,4,5,6,7},{8,9,10,11,12,13,14,15},{16,17,18,19,20,21,22,23},{24..., dimensions={0} | all-to-all | bytes 524288 | tf_op jit(solution)/shard_map/all_to_all | solution.py:318
  59.7 5.1 %generator_step.1 = (bf16[32,640]{1,0:T(8,128)(2,1)S(1)}, f32[256,128]{1,0:T(8,128)S(1)}, f32[32,256]{1,0:T(8,128)S(1)}) custom-call(s32[2]{0:T(128)S(1)} %bitcast.39, bf16[8,32,512]{2,1,0:T(8,128)(2,1)S(1)} %all_to_all.16.pulls_ref, bf16[8,128,128]{2,1,0:T(8,128)(2,1)S(1)} %all_to_all.15.noise_ref, f32[256,128]{1,0:T(8,128)S(1)} %bitcast.30, ...), custom_call_target="tpu_custom_call" | custom-call | tf_op jit(solution)/shard_map/generator_step/pallas_call | solution.py:289
  64.7 2.8 %collective-permute-done.3.part_b = bf16[80,2304]{1,0:T(8,128)(2,1)S(1)} collective-permute-done((bf16[80,2304]{1,0:T(8,128)(2,1)S(1)}, bf16[80,2304]{1,0:T(8,128)(2,1)S(1)}, u32[]{:S(2)}, u32[]{:S(2)}) %collective-permute-start.3) | collective-permute-done | bytes 368672 | tf_op jit(solution)/shard_map/ppermute | solution.py:302
  67.6 5.0 %collective-permute-start.5 = (bf16[32,640]{1,0:T(8,128)(2,1)S(1)}, bf16[32,640]{1,0:T(8,128)(2,1)S(1)}, u32[]{:S(2)}, u32[]{:S(2)}) collective-permute-start(bf16[32,640]{1,0:T(8,128)(2,1)S(1)} %get-tuple-element.49), channel_id=1, source_target_pairs={{0,16},{16,32},{32,48},{48,64},{64,80},{80,96},{96,112},{112,128},... | collective-permute-start | bytes 122888 | tf_op jit(solution)/shard_map/ppermute | solution.py:302
  72.6 5.0 %collective-permute-start.4 = (bf16[32,640]{1,0:T(8,128)(2,1)S(1)}, bf16[32,640]{1,0:T(8,128)(2,1)S(1)}, u32[]{:S(2)}, u32[]{:S(2)}) collective-permute-start(bf16[32,640]{1,0:T(8,128)(2,1)S(1)} %get-tuple-element.49), channel_id=1, source_target_pairs={{0,496},{16,0},{32,16},{48,32},{64,48},{80,64},{96,80},{112,96},{1... | collective-permute-start | bytes 122888 | tf_op jit(solution)/shard_map/ppermute | solution.py:302
  79.4 3.7 %collective-permute-start.6 = (bf16[96,2304]{1,0:T(8,128)(2,1)S(1)}, bf16[96,2304]{1,0:T(8,128)(2,1)S(1)}, u32[]{:S(2)}, u32[]{:S(2)}) collective-permute-start(bf16[96,2304]{1,0:T(8,128)(2,1)S(1)} %get-tuple-element.59), channel_id=1, source_target_pairs={{0,32},{16,48},{32,64},{48,80},{64,96},{80,112},{96,128},{112,144}... | collective-permute-start | bytes 1327112 | tf_op jit(solution)/shard_map/ppermute | solution.py:302
  83.1 3.6 %second_pull.1 = (bf16[8,32,512]{2,1,0:T(8,128)(2,1)S(1)}, bf16[32,128]{1,0:T(8,128)(2,1)S(1)}) custom-call(bf16[32,640]{1,0:T(8,128)(2,1)S(1)} %collective-permute-done.4.images_ref, f32[32,256]{1,0:T(8,128)S(1)} %get-tuple-element.54.lift_ref, bf16[256,2304]{1,0:T(8,128)(2,1)S(1)} %get-tuple-element.55.kernel_ref, f32[1,256]{1,0:T(1,128)S(1)} %get-tuple-element.56.head_ref), custom_call_target="tpu_custom_call" | custom-call | tf_op jit(solution)/shard_map/second_pull/pallas_call | solution.py:289
  86.7 10.5 %all_to_all.17.pulls_ref = bf16[8,32,512]{2,1,0:T(8,128)(2,1)S(1)} all-to-all(bf16[8,32,512]{2,1,0:T(8,128)(2,1)S(1)} %get-tuple-element.57), channel_id=1, replica_groups={{0,1,2,3,4,5,6,7},{8,9,10,11,12,13,14,15},{16,17,18,19,20,21,22,23},{24..., dimensions={0} | all-to-all | bytes 524288 | tf_op jit(solution)/shard_map/all_to_all | solution.py:318
  97.2 6.6 %collective-permute-done.6.part_c = bf16[96,2304]{1,0:T(8,128)(2,1)S(1)} collective-permute-done((bf16[96,2304]{1,0:T(8,128)(2,1)S(1)}, bf16[96,2304]{1,0:T(8,128)(2,1)S(1)}, u32[]{:S(2)}, u32[]{:S(2)}) %collective-permute-start.6) | collective-permute-done | bytes 442400 | tf_op jit(solution)/shard_map/ppermute | solution.py:302
  103.8 6.2 %collective-permute-start.8 = (bf16[32,640]{1,0:T(8,128)(2,1)S(1)}, bf16[32,640]{1,0:T(8,128)(2,1)S(1)}, u32[]{:S(2)}, u32[]{:S(2)}) collective-permute-start(bf16[32,640]{1,0:T(8,128)(2,1)S(1)} %sum_pulls.1), channel_id=1, source_target_pairs={{0,24},{1,25},{2,26},{3,27},{4,28},{5,29},{6,30},{7,31},{8,16},{9,... | collective-permute-start | bytes 122888 | tf_op jit(solution)/shard_map/ppermute | solution.py:312
  109.9 6.5 %collective-permute-start.7 = (bf16[32,640]{1,0:T(8,128)(2,1)S(1)}, bf16[32,640]{1,0:T(8,128)(2,1)S(1)}, u32[]{:S(2)}, u32[]{:S(2)}) collective-permute-start(bf16[32,640]{1,0:T(8,128)(2,1)S(1)} %sum_pulls.1), channel_id=1, source_target_pairs={{0,16},{16,32},{32,48},{48,64},{64,80},{80,96},{96,112},{112,128},... | collective-permute-start | bytes 122888 | tf_op jit(solution)/shard_map/ppermute | solution.py:302
  116.4 4.7 %moved_first.1 = (f32[32,256]{1,0:T(8,128)S(1)}, f32[256,2304]{1,0:T(8,128)S(1)}, f32[1,256]{1,0:T(1,128)S(1)}) custom-call(bf16[96,2304]{1,0:T(8,128)(2,1)S(1)} %collective-permute-done.1.part_a, bf16[80,2304]{1,0:T(8,128)(2,1)S(1)} %collective-permute-done.3.part_b, bf16[96,2304]{1,0:T(8,128)(2,1)S(1)} %collective-permute-done.6.part_c), custom_call_target="tpu_custom_call" | custom-call | tf_op jit(solution)/shard_map/moved_first/pallas_call | solution.py:289
  121.1 6.1 %moved_second.1 = (f32[32,256]{1,0:T(8,128)}, f32[256,2304]{1,0:T(8,128)}, f32[1,256]{1,0:T(1,128)}) custom-call(bf16[32,640]{1,0:T(8,128)(2,1)S(1)} %collective-permute-done.5.images_ref, f32[32,256]{1,0:T(8,128)S(1)} %get-tuple-element.61.lift_ref, f32[256,2304]{1,0:T(8,128)S(1)} %get-tuple-element.62.kernel_ref, f32[1,256]{1,0:T(1,128)S(1)} %get-tuple-element.63.head_ref), custom_call_target="tpu_custom_call" | custom-call | tf_op jit(solution)/shard_map/moved_second/pallas_call | solution.py:289
  127.2 3.6 %generator_last.1 = (f32[256,128]{1,0:T(8,128)}, f32[32,256]{1,0:T(8,128)}, f32[32,32]{1,0:T(8,128)}, f32[2,1]{1,0:T(2,128)S(1)}) custom-call(s32[1]{0:T(128)} %bitcast.1.place_ref, bf16[32,640]{1,0:T(8,128)(2,1)S(1)} %collective-permute-done.7.same_ref, bf16[32,640]{1,0:T(8,128)(2,1)S(1)} %collective-permute-done.8.cross_ref, ...), custom_call_target="tpu_custom_call" | custom-call | tf_op jit(solution)/shard_map/generator_last/pallas_call | solution.py:402
  (29 shorter events, 4.5 us)
Async XLA Ops:
  0.6 17.3 %copy-start.5 = (bf16[1,2,128,32]{2,3,1,0:T(8,128)(2,1)S(1)}, bf16[1,2,128,32]{2,3,1,0:T(8,128)(2,1)}, u32[]{:S(2)}) copy-start(bf16[1,2,128,32]{2,3,1,0:T(8,128)(2,1)} %param.10) | copy-start | bytes 49156
  0.6 6.4 %collective-permute-start = (bf16[64,128]{1,0:T(8,128)(2,1)}, bf16[64,128]{1,0:T(8,128)(2,1)S(1)}, u32[]{:S(2)}, u32[]{:S(2)}) collective-permute-start(bf16[64,128]{1,0:T(8,128)(2,1)} %bitcast.36), channel_id=1, source_target_pairs={{0,8},{1,9},{2,10},{3,11},{4,12},{5,13},{6,14},{7,15},{8,0},{9,1},... | collective-permute-start | bytes 49160 | tf_op jit(solution)/shard_map/ppermute | solution.py:306
  4.9 25.4 %copy-start = (f32[1,1,256,2304]{3,2,1,0:T(8,128)S(1)}, f32[1,1,256,2304]{3,2,1,0:T(8,128)}, u32[]{:S(2)}) copy-start(f32[1,1,256,2304]{3,2,1,0:T(8,128)} %param.14) | copy-start | bytes 7077892
  6.9 1.0 copy-start.8
  6.9 21.1 %copy-start.1 = (f32[1,256,128]{2,1,0:T(8,128)S(1)}, f32[1,256,128]{2,1,0:T(8,128)}, u32[]{:S(2)}) copy-start(f32[1,256,128]{2,1,0:T(8,128)} %param.11) | copy-start | bytes 393220
  6.9 21.1 %copy-start.2 = (f32[1,32,256]{2,1,0:T(8,128)S(1)}, f32[1,32,256]{2,1,0:T(8,128)}, u32[]{:S(2)}) copy-start(f32[1,32,256]{2,1,0:T(8,128)} %param.12) | copy-start | bytes 98308
  6.9 21.1 %copy-start.3 = (bf16[1,1,4,32,64]{4,3,2,1,0:T(8,128)(2,1)S(1)}, bf16[1,1,4,32,64]{4,3,2,1,0:T(8,128)(2,1)}, u32[]{:S(2)}) copy-start(bf16[1,1,4,32,64]{4,3,2,1,0:T(8,128)(2,1)} %param.8) | copy-start | bytes 49156
  6.9 21.1 %copy-start.6 = (s32[1,1,2,1]{2,3,1,0:T(1,128)S(1)}, s32[1,1,2,1]{2,3,1,0:T(1,128)}, u32[]{:S(2)}) copy-start(s32[1,1,2,1]{2,3,1,0:T(1,128)} %param.9) | copy-start | bytes 28
  6.9 23.4 %copy-start.4 = (f32[1,1,256,32]{2,3,1,0:T(8,128)S(1)}, f32[1,1,256,32]{2,3,1,0:T(8,128)}, u32[]{:S(2)}) copy-start(f32[1,1,256,32]{2,3,1,0:T(8,128)} %param.13) | copy-start | bytes 98308
  7.0 23.4 %copy-start.7 = (f32[1,1,256]{2,1,0:T(1,128)S(1)}, f32[1,1,256]{2,1,0:T(1,128)}, u32[]{:S(2)}) copy-start(f32[1,1,256]{2,1,0:T(1,128)} %param.15) | copy-start | bytes 3076
  7.9 31.9 %collective-permute-start.1 = (bf16[96,2304]{1,0:T(8,128)(2,1)S(1)}, bf16[96,2304]{1,0:T(8,128)(2,1)S(1)}, u32[]{:S(2)}, u32[]{:S(2)}) collective-permute-start(bf16[96,2304]{1,0:T(8,128)(2,1)S(1)} %slice_bitcast_fusion), channel_id=1, source_target_pairs={{0,32},{16,48},{32,64},{48,80},{64,96},{80,112},{96,128},{112,144}... | collective-permute-start | bytes 1327112 | tf_op jit(solution)/shard_map/ppermute | solution.py:302
  39.8 5.8 %collective-permute-start.2 = (bf16[32,512]{1,0:T(8,128)(2,1)S(1)}, bf16[32,512]{1,0:T(8,128)(2,1)S(1)}, u32[]{:S(2)}, u32[]{:S(2)}) collective-permute-start(bf16[32,512]{1,0:T(8,128)(2,1)S(1)} %get-tuple-element.45.own_ref), channel_id=1, source_target_pairs={{0,8},{1,9},{2,10},{3,11},{4,12},{5,13},{6,14},{7,15},{8,0},{9,1},... | collective-permute-start | bytes 98312 | tf_op jit(solution)/shard_map/ppermute | solution.py:306
  45.6 22.0 %collective-permute-start.3 = (bf16[80,2304]{1,0:T(8,128)(2,1)S(1)}, bf16[80,2304]{1,0:T(8,128)(2,1)S(1)}, u32[]{:S(2)}, u32[]{:S(2)}) collective-permute-start(bf16[80,2304]{1,0:T(8,128)(2,1)S(1)} %slice_bitcast_fusion.1), channel_id=1, source_target_pairs={{0,32},{16,48},{32,64},{48,80},{64,96},{80,112},{96,128},{112,144}... | collective-permute-start | bytes 1105928 | tf_op jit(solution)/shard_map/ppermute | solution.py:302
  67.6 10.1 %collective-permute-start.5 = (bf16[32,640]{1,0:T(8,128)(2,1)S(1)}, bf16[32,640]{1,0:T(8,128)(2,1)S(1)}, u32[]{:S(2)}, u32[]{:S(2)}) collective-permute-start(bf16[32,640]{1,0:T(8,128)(2,1)S(1)} %get-tuple-element.49), channel_id=1, source_target_pairs={{0,16},{16,32},{32,48},{48,64},{64,80},{80,96},{96,112},{112,128},... | collective-permute-start | bytes 122888 | tf_op jit(solution)/shard_map/ppermute | solution.py:302
  72.6 6.8 %collective-permute-start.4 = (bf16[32,640]{1,0:T(8,128)(2,1)S(1)}, bf16[32,640]{1,0:T(8,128)(2,1)S(1)}, u32[]{:S(2)}, u32[]{:S(2)}) collective-permute-start(bf16[32,640]{1,0:T(8,128)(2,1)S(1)} %get-tuple-element.49), channel_id=1, source_target_pairs={{0,496},{16,0},{32,16},{48,32},{64,48},{80,64},{96,80},{112,96},{1... | collective-permute-start | bytes 122888 | tf_op jit(solution)/shard_map/ppermute | solution.py:302
  79.4 24.4 %collective-permute-start.6 = (bf16[96,2304]{1,0:T(8,128)(2,1)S(1)}, bf16[96,2304]{1,0:T(8,128)(2,1)S(1)}, u32[]{:S(2)}, u32[]{:S(2)}) collective-permute-start(bf16[96,2304]{1,0:T(8,128)(2,1)S(1)} %get-tuple-element.59), channel_id=1, source_target_pairs={{0,32},{16,48},{32,64},{48,80},{64,96},{80,112},{96,128},{112,144}... | collective-permute-start | bytes 1327112 | tf_op jit(solution)/shard_map/ppermute | solution.py:302
  103.8 23.5 %collective-permute-start.8 = (bf16[32,640]{1,0:T(8,128)(2,1)S(1)}, bf16[32,640]{1,0:T(8,128)(2,1)S(1)}, u32[]{:S(2)}, u32[]{:S(2)}) collective-permute-start(bf16[32,640]{1,0:T(8,128)(2,1)S(1)} %sum_pulls.1), channel_id=1, source_target_pairs={{0,24},{1,25},{2,26},{3,27},{4,28},{5,29},{6,30},{7,31},{8,16},{9,... | collective-permute-start | bytes 122888 | tf_op jit(solution)/shard_map/ppermute | solution.py:312
  109.9 17.3 %collective-permute-start.7 = (bf16[32,640]{1,0:T(8,128)(2,1)S(1)}, bf16[32,640]{1,0:T(8,128)(2,1)S(1)}, u32[]{:S(2)}, u32[]{:S(2)}) collective-permute-start(bf16[32,640]{1,0:T(8,128)(2,1)S(1)} %sum_pulls.1), channel_id=1, source_target_pairs={{0,16},{16,32},{32,48},{48,64},{64,80},{80,96},{96,112},{112,128},... | collective-permute-start | bytes 122888 | tf_op jit(solution)/shard_map/ppermute | solution.py:302

commit v3 on v2

--- a/solution.py
+++ b/solution.py
@@ -17,9 +17,9 @@
 ROWS = 576
 WIDE = 640
 KW = TAPS * CH
-PART_A = 96
-PART_B = 80
-PART_C = CH - PART_A - PART_B
+PART_A = 160
+PART_B = CH - PART_A
+FIRST_WORK = 20_000_000_000
 
 critic_rate = 0.05
 generator_rate = 0.2
@@ -34,8 +34,21 @@
     return lax.dot_general(a, b, dims, preferred_element_type=f32)
 
 
+def split(x):
+    high = x.astype(bf16)
+    return high, (x - high.astype(f32)).astype(bf16)
+
+
 def exact_dot(a, b, dims=NN):
-    return lax.dot_general(a, b, dims, precision=lax.Precision.HIGHEST, preferred_element_type=f32)
+    if b.dtype == bf16:
+        high, low = split(a)
+        return dot(high, b, dims) + dot(low, b, dims)
+    if a.dtype == bf16:
+        high, low = split(b)
+        return dot(a, high, dims) + dot(a, low, dims)
+    a_high, a_low = split(a)
+    b_high, b_low = split(b)
+    return dot(a_high, b_high, dims) + (dot(a_high, b_low, dims) + dot(a_low, b_high, dims))
 
 
 def sigmoid(x):
@@ -123,7 +136,7 @@
     for z in range(2):
         start = 2 * C * z + C * round_index
         halves.append(noise_ref[:, start : start + C, :].reshape(FAKE // 2, 128))
-    return jnp.concatenate(halves, axis=0).astype(f32)
+    return jnp.concatenate(halves, axis=0)
 
 
 def put_images(images_ref, fakes, real):
@@ -142,12 +155,6 @@
         copies_ref[j, 2 * C :] = high
 
 
-def pair_copies_kernel(own_ref, other_ref, copies_ref):
-    pair = (own_ref[...].astype(f32) + other_ref[...].astype(f32)).astype(bf16)
-    for j in range(8):
-        copies_ref[j] = pair
-
-
 def sum_of(pulls_ref):
     total = pulls_ref[0].astype(f32)
     for j in range(1, 8):
@@ -155,9 +162,23 @@
     return total
 
 
-def sum_kernel(pulls_ref, score_ref, out_ref):
+def sum_kernel(pulls_ref, out_ref):
+    out_ref[...] = sum_of(pulls_ref).astype(bf16)
+
+
+def scored_sum_kernel(pulls_ref, score_ref, out_ref):
     out_ref[:, :FAKE] = sum_of(pulls_ref).astype(bf16)
     out_ref[:, FAKE:] = score_ref[...]
+
+
+def put_halves(block_ref, images):
+    block_ref[:, :WIDE] = images[:16]
+    block_ref[:, WIDE : 2 * WIDE] = images[16:]
+
+
+def add_images_kernel(images_ref, part_ref, block_ref):
+    put_halves(block_ref, images_ref[...])
+    block_ref[:, 2 * WIDE :] = jnp.zeros((16, KW - 2 * WIDE), bf16)
 
 
 def generate_kernel(pick_ref, noise_ref, first_ref, second_ref, pool_ref, images_ref):
@@ -167,7 +188,7 @@
     put_images(images_ref, fakes, real_image(pool_ref, pick_ref, 0))
 
 
-def first_step_kernel(images_ref, lift_ref, kernel_ref, head_ref, pull_ref, lift_out, kernel_out, head_out, score_out, rest_out, patch_ref, half_ref):
+def first_step_kernel(images_ref, lift_ref, kernel_ref, head_ref, copies_ref, lift_out, kernel_out, head_out, score_out, rest_out, patch_ref, half_ref):
     for t in range(TAPS):
         half_ref[t] = kernel_ref[:, CH * t : CH * (t + 1)].astype(bf16)
     lift = lift_ref[...]
@@ -177,20 +198,22 @@
     slope, z_grad, head_grad, score = critic_forward(images, lift_half, lambda t: half_ref[t], head, patch_ref)
     z_half = z_grad.astype(bf16)
     pre_grad = lift_pullback(slope, z_half, lambda t: half_ref[t])
-    pull_ref[...] = (-8.0 * dot(lift_half, pre_grad, NT)[:, :FAKE]).astype(bf16)
+    pull = (-8.0 * dot(lift_half, pre_grad, NT)[:, :FAKE]).astype(bf16)
+    for j in range(8):
+        copies_ref[j] = pull
     lift_out[...] = lift - critic_rate * dot(images[:, :ROWS], pre_grad)
     head_out[...] = head - critic_rate * head_grad
     z_turned = jnp.transpose(z_grad).astype(bf16)
     for t in range(TAPS):
         cols = slice(CH * t, CH * (t + 1))
         kernel_out[:, cols] = (kernel_ref[:, cols] - critic_rate * dot(z_turned, patch_ref[t])).astype(bf16)
-        rest_out[:PART_C, cols] = half_ref[t, CH - PART_C :, :]
-    rest_out[PART_C:, :WIDE] = images[:16]
-    rest_out[PART_C:, WIDE : 2 * WIDE] = images[16:]
-    rest_out[PART_C:, 1280:1536] = lift_half[:16]
-    rest_out[PART_C:, 1536:1792] = lift_half[16:]
-    rest_out[PART_C:, 1792:2048] = jnp.broadcast_to(head, (16, CH)).astype(bf16)
-    rest_out[PART_C:, 2048:] = jnp.zeros((16, KW - 2048), bf16)
+        rest_out[:PART_B, cols] = half_ref[t, PART_A:, :]
+    block = rest_out.at[PART_B : PART_B + 16]
+    put_halves(block, images)
+    block[:, 1280:1536] = lift_half[:16]
+    block[:, 1536:1792] = lift_half[16:]
+    block[:, 1792:2048] = jnp.broadcast_to(head, (16, CH)).astype(bf16)
+    block[:, 2048:] = jnp.zeros((16, KW - 2048), bf16)
     score_out[...] = jnp.broadcast_to(score, (8, 128))
 
 
@@ -210,15 +233,15 @@
     score_ref[...] = three.astype(bf16)
 
 
-def moved_first_kernel(part_a, part_b, part_c, lift_out, kernel_out, head_out, patch_ref, half_ref):
+def moved_first_kernel(part_a, part_b, lift_out, kernel_out, head_out, patch_ref, half_ref):
     for t in range(TAPS):
         cols = slice(CH * t, CH * (t + 1))
         half_ref[t, :PART_A] = part_a[:, cols]
-        half_ref[t, PART_A : PART_A + PART_B] = part_b[:, cols]
-        half_ref[t, PART_A + PART_B :] = part_c[:PART_C, cols]
-    images = jnp.concatenate([part_c[PART_C:, :WIDE], part_c[PART_C:, WIDE : 2 * WIDE]], axis=0)
-    lift_half = jnp.concatenate([part_c[PART_C:, 1280:1536], part_c[PART_C:, 1536:1792]], axis=0)
-    head = part_c[PART_C:, 1792:2048].astype(f32)[:1]
+        half_ref[t, PART_A:] = part_b[:PART_B, cols]
+    block = part_b.at[PART_B : PART_B + 16]
+    images = jnp.concatenate([block[:, :WIDE], block[:, WIDE : 2 * WIDE]], axis=0)
+    lift_half = jnp.concatenate([block[:, 1280:1536], block[:, 1536:1792]], axis=0)
+    head = block[:, 1792:2048].astype(f32)[:1]
     kernel_of = lambda t: half_ref[t]
     slope, z_grad, head_grad, _ = critic_forward(images, lift_half, kernel_of, head, patch_ref)
     pre_grad = lift_pullback(slope, z_grad.astype(bf16), kernel_of)
@@ -229,12 +252,13 @@
         kernel_out[:, CH * t : CH * (t + 1)] = kernel_of(t).astype(f32) - critic_rate * dot(z_turned, patch_ref[t])
 
 
-def moved_second_kernel(images_ref, lift_ref, kernel_ref, head_ref, lift_out, kernel_out, head_out, patch_ref, half_ref):
+def moved_second_kernel(part_b, lift_ref, kernel_ref, head_ref, lift_out, kernel_out, head_out, patch_ref, half_ref):
     for t in range(TAPS):
         half_ref[t] = kernel_ref[:, CH * t : CH * (t + 1)].astype(bf16)
     lift = lift_ref[...]
     head = head_ref[...]
-    images = images_ref[...]
+    block = part_b.at[PART_B + 16 :]
+    images = jnp.concatenate([block[:, :WIDE], block[:, WIDE : 2 * WIDE]], axis=0)
     kernel_of = lambda t: half_ref[t]
     slope, z_grad, head_grad, _ = critic_forward(images, lift.astype(bf16), kernel_of, head, patch_ref)
     pre_grad = lift_pullback(slope, z_grad.astype(bf16), kernel_of)
@@ -255,8 +279,8 @@
     return first - generator_rate * first_grad, second - generator_rate * second_grad
 
 
-def middle_kernel(pick_ref, pulls_ref, noise_ref, first_ref, second_ref, pool_ref, images_ref, first_out, second_out):
-    first, second = generator_step(sum_of(pulls_ref), latents_of(noise_ref, 0), first_ref[...], second_ref[...])
+def middle_kernel(pick_ref, own_ref, other_ref, noise_ref, first_ref, second_ref, pool_ref, images_ref, first_out, second_out):
+    first, second = generator_step(own_ref[...].astype(f32) + other_ref[...].astype(f32), latents_of(noise_ref, 0), first_ref[...], second_ref[...])
     first_out[...] = first
     second_out[...] = second
     inner = exact_dot(latents_of(noise_ref, 1), first, NT)
@@ -264,8 +288,8 @@
     put_images(images_ref, fakes, real_image(pool_ref, pick_ref, 1))
 
 
-def last_kernel(place_ref, same_ref, cross_ref, noise_ref, first_ref, second_ref, score_ref, first_out, second_out, own_out, scores_out):
-    total = same_ref[:, :FAKE].astype(f32) + cross_ref[:, :FAKE].astype(f32)
+def last_kernel(place_ref, own_ref, other_ref, noise_ref, first_ref, second_ref, score_ref, first_out, second_out, own_out, scores_out):
+    total = own_ref[:, :FAKE].astype(f32) + other_ref[:, :FAKE].astype(f32)
     first, second = generator_step(total, latents_of(noise_ref, 1), first_ref[...], second_ref[...])
     first_out[...] = first
     second_out[...] = second
@@ -274,7 +298,7 @@
         own = own + jnp.where(place_ref[0] == j, total[:, C * j : C * (j + 1)], 0.0)
     own_out[...] = own
     scores_out[0, 0] = jnp.max(score_ref[...])
-    scores_out[1, 0] = jnp.sum(same_ref[:, FAKE:].astype(f32)[:1])
+    scores_out[1, 0] = jnp.sum(own_ref[:, FAKE:].astype(f32)[:1])
 
 
 def vmem(*_):
@@ -285,7 +309,7 @@
     return pl.BlockSpec(memory_space=pltpu.SMEM)
 
 
-def call(kernel, name, outs, ins, scratch=(), scalars=0):
+def call(kernel, name, outs, ins, scratch=(), scalars=0, work=0):
     return pl.pallas_call(
         kernel,
         name=name,
@@ -293,6 +317,7 @@
         in_specs=[smem()] * scalars + [vmem()] * (len(ins) - scalars),
         out_specs=[vmem()] * len(outs),
         scratch_shapes=list(scratch),
+        cost_estimate=pl.CostEstimate(flops=work, bytes_accessed=0, transcendentals=0) if work else None,
         compiler_params=pltpu.CompilerParams(vmem_limit_bytes=24 * 1024 * 1024),
     )(*ins)
 
@@ -304,12 +329,6 @@
 
 def across(value):
     return lax.ppermute(value, "grp", [(m, m ^ 8) for m in range(N_GRP)])
-
-
-def shifted_across(value, steps):
-    count = lax.axis_size("loop")
-    pairs = [(l * N_GRP + m, (l + steps) % count * N_GRP + (m ^ 8)) for l in range(count) for m in range(N_GRP)]
-    return lax.ppermute(value, ("loop", "grp"), pairs)
 
 
 def swap(copies):
@@ -338,41 +357,46 @@
     own_noise = jnp.swapaxes(noise_latents[0], 1, 2).reshape(ROUNDS * C, 128)
     other_noise = across(own_noise)
     part_a = kernel[:PART_A].astype(bf16)
-    part_b = kernel[PART_A : PART_A + PART_B].astype(bf16)
-    part_a, other_noise = together(part_a, other_noise)
-    moved_a = shifted(part_a, 2)
     (copies,) = call(
         noise_copies_kernel, "noise_copies", [((8, 4 * C, 128), bf16)], (place, own_noise, other_noise), scalars=1
     )
+    part_a, copies = together(part_a, copies)
+    moved_a = shifted(part_a, 2)
     noise = swap(copies)
     (images,) = call(
         generate_kernel, "make_fakes", [((C, WIDE), bf16)], (pick, noise, first, second, pool), scalars=1
     )
-    pull, lift_1, kernel_1, head_1, score_0, part_c = call(
+    copies, lift_1, kernel_1, head_1, score_0, part_b = call(
         first_step_kernel,
         "first_step",
-        [((C, FAKE), bf16), ((C, CH), f32), ((CH, KW), bf16), ((1, CH), f32), ((8, 128), f32), ((PART_C + 16, KW), bf16)],
+        [((8, C, FAKE), bf16), ((C, CH), f32), ((CH, KW), bf16), ((1, CH), f32), ((8, 128), f32), ((PART_B + 32, KW), bf16)],
         (images, lift, kernel, head),
         (PATCHES, HALVES),
-    )
-    pull, moved_a = together(pull, moved_a)
-    other_pull = across(pull)
-    part_b, other_pull = together(part_b, other_pull)
-    moved_b = shifted(part_b, 2)
-    (copies,) = call(pair_copies_kernel, "pair_copies", [((8, C, FAKE), bf16)], (pull, other_pull))
-    pulls = swap(copies)
+        work=FIRST_WORK,
+    )
+    (partial,) = call(sum_kernel, "sum_first", [((C, FAKE), bf16)], (swap(copies),))
+    partial, moved_a = together(partial, moved_a)
+    other = across(partial)
     own_images, first_1, second_1 = call(
         middle_kernel,
         "generator_step",
         [((C, WIDE), bf16), ((CH, 128), f32), ((C, CH), f32)],
-        (pick, pulls, noise, first, second, pool),
+        (pick, partial, other, noise, first, second, pool),
         scalars=1,
     )
-    own_images, moved_b = together(own_images, moved_b)
     ahead_images = shifted(own_images, -1)
-    behind_images = shifted(own_images, 1)
-    part_c, ahead_images, behind_images = together(part_c, ahead_images, behind_images)
-    moved_c = shifted(part_c, 2)
+    part_b = pl.pallas_call(
+        add_images_kernel,
+        name="add_images",
+        grid=(1,),
+        out_shape=jax.ShapeDtypeStruct((PART_B + 32, KW), bf16),
+        in_specs=[vmem(), pl.BlockSpec(memory_space=pl.ANY)],
+        out_specs=pl.BlockSpec((16, KW), lambda i: ((PART_B + 16) // 16, 0)),
+        input_output_aliases={1: 0},
+        compiler_params=pltpu.CompilerParams(vmem_limit_bytes=24 * 1024 * 1024),
+    )(ahead_images, part_b)
+    part_b, ahead_images = together(part_b, ahead_images)
+    moved_b = shifted(part_b, 2)
     copies, score_1 = call(
         pull_only_kernel,
         "second_pull",
@@ -380,23 +404,24 @@
         (ahead_images, lift_1, kernel_1, head_1),
         (PATCHES,),
     )
-    (partial,) = call(sum_kernel, "sum_pulls", [((C, WIDE), bf16)], (swap(copies), score_1))
-    partial, moved_c = together(partial, moved_c)
+    (partial,) = call(scored_sum_kernel, "sum_second", [((C, WIDE), bf16)], (swap(copies), score_1))
+    partial, moved_b = together(partial, moved_b)
     same = shifted(partial, 1)
-    cross = shifted_across(partial, 1)
 
     moved_lift, moved_kernel, moved_head = call(
         moved_first_kernel,
         "moved_first",
         [((C, CH), f32), ((CH, KW), f32), ((1, CH), f32)],
-        (moved_a, moved_b, moved_c),
+        (moved_a, moved_b),
         (PATCHES, HALVES),
     )
+    moved_lift, same = together(moved_lift, same)
+    cross = across(same)
     lift_2, kernel_2, head_2 = call(
         moved_second_kernel,
         "moved_second",
         [((C, CH), f32), ((CH, KW), f32), ((1, CH), f32)],
-        (behind_images, moved_lift, moved_kernel, moved_head),
+        (moved_b, moved_lift, moved_kernel, moved_head),
         (PATCHES, HALVES),
     )
     first_2, second_2, own_grad, scores = pl.pallas_call(
@@ -415,7 +440,7 @@
     return (
         jnp.swapaxes(lift_2, 0, 1)[None, None],
         kernel_2[None, None],
-        head_2[0][None, None],
+        head_2.reshape(1, 1, CH),
         first_2[None],
         second_2[None],
         own_grad[None],

time: 134 us -> 132 us (0.985)
  waiting for transfers between devices: 18.7 us -> 37.9 us
  blocking collectives: 30.6 us -> 20.1 us
  starting transfers between devices: 46.6 us -> 38.5 us
  local copies, waits for them, and re-layouts: 1.99 us -> 6.65 us
  Pallas kernels: 30.2 us -> 26.2 us
  other arithmetic: 2.56 us -> 0.63 us
    ppermute x6 -> x4, waiting for transfers between devices: 15.8 us -> 34 us  [shifted(): lax.ppermute(value, 'loop', [(s, (s + steps) % count) for s in range(coun...]
    ppermute x6 -> x4, starting transfers between devices: 34.2 us -> 21.8 us  [shifted(): lax.ppermute(value, 'loop', [(s, (s + steps) % count) for s in range(coun...]
    all_to_all x3 -> x2, blocking collectives: 30.6 us -> 20.1 us  [swap(): lax.all_to_all(copies, ('loop', 'grp'), 0, 0, axis_index_groups=groups)]
    all_to_all x0 -> x1, starting transfers between devices: none -> 8.44 us  [swap(): lax.all_to_all(copies, ('loop', 'grp'), 0, 0, axis_index_groups=groups)]
    ppermute x1 -> x0, starting transfers between devices: 6.17 us -> none  [shifted_across(): return lax.ppermute(value, ('loop', 'grp'), pairs)]
    unnamed x18 -> x22, local copies, waits for them, and re-layouts: 0.95 us -> 4.34 us
    pallas_call x9, Pallas kernels: 26.6 us -> 24 us  [call(): pl.pallas_call(kernel, name=name, out_shape=[jax.ShapeDtypeStruct(s, d) f...]
    convert_element_type x1, local copies, waits for them, and re-layouts: 0.03 us -> 2.31 us  [per_device(): part_a = kernel[:PART_A].astype(bf16)]
  transfers between devices with their start and end apart: 9 -> 8, of which waited for: 5 -> 5; matrix products, arithmetic and copies ran while one was open for 2% -> 2% of each run, Pallas kernels for 20% -> 16%
where the time goes in v3:
time: 132 us; the launch traced here: 131 us
  starting transfers between devices  38.5 us (29%)
  waiting for transfers between devices  37.9 us (29%)
  Pallas kernels  26.2 us (20%)
  blocking collectives  20.1 us (15%)
  local copies, waits for them, and re-layouts  6.65 us (5%)
    ppermute x4, waiting for transfers between devices, shifted(): lax.ppermute(value, 'loop', [(s, (s + steps) % count) for s in range(coun...  34 us
    pallas_call x9, Pallas kernels, call(): pl.pallas_call(kernel, name=name, out_shape=[jax.ShapeDtypeStruct(s, d) f...  24 us
    ppermute x4, starting transfers between devices, shifted(): lax.ppermute(value, 'loop', [(s, (s + steps) % count) for s in range(coun...  21.8 us
    all_to_all x2, blocking collectives, swap(): lax.all_to_all(copies, ('loop', 'grp'), 0, 0, axis_index_groups=groups)  20.1 us
    all_to_all x1, starting transfers between devices, swap(): lax.all_to_all(copies, ('loop', 'grp'), 0, 0, axis_index_groups=groups)  8.44 us
    ppermute x3, starting transfers between devices, across(): return lax.ppermute(value, 'grp', [(m, m ^ 8) for m in range(N_GRP)])  8.23 us
    unnamed x22, local copies, waits for them, and re-layouts  4.34 us
    ppermute x3, waiting for transfers between devices, across(): return lax.ppermute(value, 'grp', [(m, m ^ 8) for m in range(N_GRP)])  3.89 us
  transfers between devices with their start and end apart: 8, of which 5 were waited for; matrix products, arithmetic and copies ran while one was open for 2% of the time, Pallas kernels for 16%

profile of v3, /device:TPU:6, one launch (start us, length us, event | category | flops | bytes accessed | tf_op | source)
XLA Modules:
  0.0 130.8 jit_solution(9802520679441094911)
XLA Ops:
  0.7 4.4 %collective-permute-start = (bf16[64,128]{1,0:T(8,128)(2,1)}, bf16[64,128]{1,0:T(8,128)(2,1)S(1)}, u32[]{:S(2)}, u32[]{:S(2)}) collective-permute-start(bf16[64,128]{1,0:T(8,128)(2,1)} %bitcast.33), channel_id=1, source_target_pairs={{0,8},{1,9},{2,10},{3,11},{4,12},{5,13},{6,14},{7,15},{8,0},{9,1},... | collective-permute-start | bytes 49160 | tf_op jit(solution)/shard_map/ppermute | solution.py:331
  5.1 2.3 %fusion = bf16[160,2304]{1,0:T(8,128)(2,1)} fusion(f32[1,1,256,2304]{3,2,1,0:T(8,128)} %param.14), kind=kLoop, calls=%fused_computation.1 | loop fusion | bytes 1474560 | tf_op jit(solution)/shard_map/convert_element_type | solution.py:359
  8.8 8.4 %all-to-all-start = ((bf16[8,128,128]{2,1,0:T(8,128)(2,1)}), bf16[8,128,128]{2,1,0:T(8,128)(2,1)S(1)}, u32[]{:S(2)}, u32[]{:S(2)}) async-start(bf16[8,128,128]{2,1,0:T(8,128)(2,1)} %noise_copies.1), calls=%async_computation | async-start | bytes 524288 | tf_op jit(solution)/shard_map/all_to_all | solution.py:337
  17.3 6.5 %collective-permute-start.1 = (bf16[160,2304]{1,0:T(8,128)(2,1)}, bf16[160,2304]{1,0:T(8,128)(2,1)S(1)}, u32[]{:S(2)}, u32[]{:S(2)}) collective-permute-start(bf16[160,2304]{1,0:T(8,128)(2,1)} %fusion), channel_id=1, source_target_pairs={{0,32},{16,48},{32,64},{48,80},{64,96},{80,112},{96,128},{112,144}... | collective-permute-start | bytes 2211848 | tf_op jit(solution)/shard_map/ppermute | solution.py:327
  24.5 0.8 copy-done.4
  26.0 1.3 %make_fakes.1.images_ref = bf16[32,640]{1,0:T(8,128)(2,1)S(1)} custom-call(s32[2]{0:T(128)S(1)} %bitcast.35, bf16[8,128,128]{2,1,0:T(8,128)(2,1)S(1)} %all-to-all-done.noise_ref, f32[256,128]{1,0:T(8,128)S(1)} %bitcast.26, f32[32,256]{1,0:T(8,128)S(1)} %bitcast.29, bf16[4,32,64]{2,1,0:T(8,128)(2,1)S(1)} %bitcast.31), custom_call_target="tpu_custom_call" | custom-call | tf_op jit(solution)/shard_map/make_fakes/pallas_call | solution.py:313
  28.8 4.7 %first_step.1 = (bf16[8,32,512]{2,1,0:T(8,128)(2,1)S(1)}, f32[32,256]{1,0:T(8,128)S(1)}, bf16[256,2304]{1,0:T(8,128)(2,1)S(1)}, f32[1,256]{1,0:T(1,128)S(1)}, f3...) custom-call(bf16[32,640]{1,0:T(8,128)(2,1)S(1)} %make_fakes.1.images_ref, f32[32,256]{1,0:T(8,128)S(1)} %bitcast.37, ...), custom_call_target="tpu_custom_call" | custom-call | flops 20000000000 | tf_op jit(solution)/shard_map/first_step/pallas_call | solution.py:313
  33.5 10.1 %all_to_all.15.pulls_ref = bf16[8,32,512]{2,1,0:T(8,128)(2,1)S(1)} all-to-all(bf16[8,32,512]{2,1,0:T(8,128)(2,1)S(1)} %get-tuple-element.39), channel_id=1, replica_groups={{0,1,2,3,4,5,6,7},{8,9,10,11,12,13,14,15},{16,17,18,19,20,21,22,23},{24..., dimensions={0} | all-to-all | bytes 524288 | tf_op jit(solution)/shard_map/all_to_all | solution.py:337
  43.6 15.2 %collective-permute-done.1.part_a = bf16[160,2304]{1,0:T(8,128)(2,1)S(1)} collective-permute-done((bf16[160,2304]{1,0:T(8,128)(2,1)}, bf16[160,2304]{1,0:T(8,128)(2,1)S(1)}, u32[]{:S(2)}, u32[]{:S(2)}) %collective-permute-start.1) | collective-permute-done | bytes 737312 | tf_op jit(solution)/shard_map/ppermute | solution.py:327
  58.8 1.9 %collective-permute-start.2 = (bf16[32,512]{1,0:T(8,128)(2,1)S(1)}, bf16[32,512]{1,0:T(8,128)(2,1)S(1)}, u32[]{:S(2)}, u32[]{:S(2)}) collective-permute-start(bf16[32,512]{1,0:T(8,128)(2,1)S(1)} %sum_first.1.own_ref), channel_id=1, source_target_pairs={{0,8},{1,9},{2,10},{3,11},{4,12},{5,13},{6,14},{7,15},{8,0},{9,1},... | collective-permute-start | bytes 98312 | tf_op jit(solution)/shard_map/ppermute | solution.py:331
  60.7 3.9 %collective-permute-done.2.other_ref = bf16[32,512]{1,0:T(8,128)(2,1)S(1)} collective-permute-done((bf16[32,512]{1,0:T(8,128)(2,1)S(1)}, bf16[32,512]{1,0:T(8,128)(2,1)S(1)}, u32[]{:S(2)}, u32[]{:S(2)}) %collective-permute-start.2) | collective-permute-done | bytes 32800 | tf_op jit(solution)/shard_map/ppermute | solution.py:331
  64.6 2.8 %generator_step.1 = (bf16[32,640]{1,0:T(8,128)(2,1)S(1)}, f32[256,128]{1,0:T(8,128)S(1)}, f32[32,256]{1,0:T(8,128)S(1)}) custom-call(s32[2]{0:T(128)S(1)} %bitcast.36, bf16[32,512]{1,0:T(8,128)(2,1)S(1)} %sum_first.1.own_ref, bf16[32,512]{1,0:T(8,128)(2,1)S(1)} %collective-permute-done.2.other_ref, bf16[8,128,128]{2,1,0:T(8,128)(2,1)S(1)} %all-to-all-done.noise_ref, ...), custom_call_target="tpu_custom_call" | custom-call | tf_op jit(solution)/shard_map/generator_step/pallas_call | solution.py:313
  67.4 8.2 %collective-permute-start.3 = (bf16[32,640]{1,0:T(8,128)(2,1)S(1)}, bf16[32,640]{1,0:T(8,128)(2,1)S(1)}, u32[]{:S(2)}, u32[]{:S(2)}) collective-permute-start(bf16[32,640]{1,0:T(8,128)(2,1)S(1)} %get-tuple-element.42), channel_id=1, source_target_pairs={{0,496},{16,0},{32,16},{48,32},{64,48},{80,64},{96,80},{112,96},{1... | collective-permute-start | bytes 122888 | tf_op jit(solution)/shard_map/ppermute | solution.py:327
  75.6 1.7 %collective-permute-done.3.images_ref = bf16[32,640]{1,0:T(8,128)(2,1)S(1)} collective-permute-done((bf16[32,640]{1,0:T(8,128)(2,1)S(1)}, bf16[32,640]{1,0:T(8,128)(2,1)S(1)}, u32[]{:S(2)}, u32[]{:S(2)}) %collective-permute-start.3) | collective-permute-done | bytes 40992 | tf_op jit(solution)/shard_map/ppermute | solution.py:327
  77.3 3.6 %collective-permute-start.4 = (bf16[128,2304]{1,0:T(8,128)(2,1)S(1)}, bf16[128,2304]{1,0:T(8,128)(2,1)S(1)}, u32[]{:S(2)}, u32[]{:S(2)}) collective-permute-start(bf16[128,2304]{1,0:T(8,128)(2,1)S(1)} %add_images.1), channel_id=1, source_target_pairs={{0,32},{16,48},{32,64},{48,80},{64,96},{80,112},{96,128},{112,144}... | collective-permute-start | bytes 1769480 | tf_op jit(solution)/shard_map/ppermute | solution.py:327
  80.9 3.6 %second_pull.1 = (bf16[8,32,512]{2,1,0:T(8,128)(2,1)S(1)}, bf16[32,128]{1,0:T(8,128)(2,1)S(1)}) custom-call(bf16[32,640]{1,0:T(8,128)(2,1)S(1)} %collective-permute-done.3.images_ref, f32[32,256]{1,0:T(8,128)S(1)} %get-tuple-element.45.lift_ref, bf16[256,2304]{1,0:T(8,128)(2,1)S(1)} %get-tuple-element.46.kernel_ref, f32[1,256]{1,0:T(1,128)S(1)} %get-tuple-element.47.head_ref), custom_call_target="tpu_custom_call" | custom-call | tf_op jit(solution)/shard_map/second_pull/pallas_call | solution.py:313
  84.5 10.1 %all_to_all.16.pulls_ref = bf16[8,32,512]{2,1,0:T(8,128)(2,1)S(1)} all-to-all(bf16[8,32,512]{2,1,0:T(8,128)(2,1)S(1)} %get-tuple-element.48), channel_id=1, replica_groups={{0,1,2,3,4,5,6,7},{8,9,10,11,12,13,14,15},{16,17,18,19,20,21,22,23},{24..., dimensions={0} | all-to-all | bytes 524288 | tf_op jit(solution)/shard_map/all_to_all | solution.py:337
  94.6 15.2 %collective-permute-done.4.part_b = bf16[128,2304]{1,0:T(8,128)(2,1)S(1)} collective-permute-done((bf16[128,2304]{1,0:T(8,128)(2,1)S(1)}, bf16[128,2304]{1,0:T(8,128)(2,1)S(1)}, u32[]{:S(2)}, u32[]{:S(2)}) %collective-permute-start.4) | collective-permute-done | bytes 589856 | tf_op jit(solution)/shard_map/ppermute | solution.py:327
  109.9 3.5 %collective-permute-start.5 = (bf16[32,640]{1,0:T(8,128)(2,1)S(1)}, bf16[32,640]{1,0:T(8,128)(2,1)S(1)}, u32[]{:S(2)}, u32[]{:S(2)}) collective-permute-start(bf16[32,640]{1,0:T(8,128)(2,1)S(1)} %sum_second.1), channel_id=1, source_target_pairs={{0,16},{16,32},{32,48},{48,64},{64,80},{80,96},{96,112},{112,128},... | collective-permute-start | bytes 122888 | tf_op jit(solution)/shard_map/ppermute | solution.py:327
  113.4 4.7 %moved_first.1 = (f32[32,256]{1,0:T(8,128)S(1)}, f32[256,2304]{1,0:T(8,128)S(1)}, f32[1,256]{1,0:T(1,128)S(1)}) custom-call(bf16[160,2304]{1,0:T(8,128)(2,1)S(1)} %collective-permute-done.1.part_a, bf16[128,2304]{1,0:T(8,128)(2,1)S(1)} %collective-permute-done.4.part_b), custom_call_target="tpu_custom_call" | custom-call | tf_op jit(solution)/shard_map/moved_first/pallas_call | solution.py:313
  118.1 1.9 %collective-permute-done.5.own_ref = bf16[32,640]{1,0:T(8,128)(2,1)S(1)} collective-permute-done((bf16[32,640]{1,0:T(8,128)(2,1)S(1)}, bf16[32,640]{1,0:T(8,128)(2,1)S(1)}, u32[]{:S(2)}, u32[]{:S(2)}) %collective-permute-start.5) | collective-permute-done | bytes 40992 | tf_op jit(solution)/shard_map/ppermute | solution.py:327
  120.0 1.9 %collective-permute-start.6 = (bf16[32,640]{1,0:T(8,128)(2,1)S(1)}, bf16[32,640]{1,0:T(8,128)(2,1)S(1)}, u32[]{:S(2)}, u32[]{:S(2)}) collective-permute-start(bf16[32,640]{1,0:T(8,128)(2,1)S(1)} %collective-permute-done.5.own_ref), channel_id=1, source_target_pairs={{0,8},{1,9},{2,10},{3,11},{4,12},{5,13},{6,14},{7,15},{8,0},{9,1},... | collective-permute-start | bytes 122888 | tf_op jit(solution)/shard_map/ppermute | solution.py:331
  121.9 6.1 %moved_second.1 = (f32[32,256]{1,0:T(8,128)}, f32[256,2304]{1,0:T(8,128)}, f32[1,256]{1,0:T(1,128)}) custom-call(bf16[128,2304]{1,0:T(8,128)(2,1)S(1)} %collective-permute-done.4.part_b, f32[32,256]{1,0:T(8,128)S(1)} %get-tuple-element.55.lift_ref, f32[256,2304]{1,0:T(8,128)S(1)} %get-tuple-element.56.kernel_ref, f32[1,256]{1,0:T(1,128)S(1)} %get-tuple-element.57.head_ref), custom_call_target="tpu_custom_call" | custom-call | tf_op jit(solution)/shard_map/moved_second/pallas_call | solution.py:313
  128.0 2.1 %generator_last.1 = (f32[256,128]{1,0:T(8,128)}, f32[32,256]{1,0:T(8,128)}, f32[32,32]{1,0:T(8,128)}, f32[2,1]{1,0:T(2,128)S(1)}) custom-call(s32[1]{0:T(128)} %bitcast.2.place_ref, bf16[32,640]{1,0:T(8,128)(2,1)S(1)} %collective-permute-done.5.own_ref, bf16[32,640]{1,0:T(8,128)(2,1)S(1)} %collective-permute-done.6.other_ref, ...), custom_call_target="tpu_custom_call" | custom-call | tf_op jit(solution)/shard_map/generator_last/pallas_call | solution.py:427
  (29 shorter events, 5.0 us)
Async XLA Ops:
  0.6 23.1 %copy-start = (f32[1,256,128]{2,1,0:T(8,128)S(1)}, f32[1,256,128]{2,1,0:T(8,128)}, u32[]{:S(2)}) copy-start(f32[1,256,128]{2,1,0:T(8,128)} %param.11) | copy-start | bytes 393220
  0.6 26.7 %copy-start.1 = (f32[1,1,256,2304]{3,2,1,0:T(8,128)S(1)}, f32[1,1,256,2304]{3,2,1,0:T(8,128)}, u32[]{:S(2)}) copy-start(f32[1,1,256,2304]{3,2,1,0:T(8,128)} %param.14) | copy-start | bytes 7077892
  0.7 6.7 %collective-permute-start = (bf16[64,128]{1,0:T(8,128)(2,1)}, bf16[64,128]{1,0:T(8,128)(2,1)S(1)}, u32[]{:S(2)}, u32[]{:S(2)}) collective-permute-start(bf16[64,128]{1,0:T(8,128)(2,1)} %bitcast.33), channel_id=1, source_target_pairs={{0,8},{1,9},{2,10},{3,11},{4,12},{5,13},{6,14},{7,15},{8,0},{9,1},... | collective-permute-start | bytes 49160 | tf_op jit(solution)/shard_map/ppermute | solution.py:331
  7.4 0.7 copy-start.6
  8.8 14.9 %all-to-all-start = ((bf16[8,128,128]{2,1,0:T(8,128)(2,1)}), bf16[8,128,128]{2,1,0:T(8,128)(2,1)S(1)}, u32[]{:S(2)}, u32[]{:S(2)}) async-start(bf16[8,128,128]{2,1,0:T(8,128)(2,1)} %noise_copies.1), calls=%async_computation | async-start | bytes 524288 | tf_op jit(solution)/shard_map/all_to_all | solution.py:337
  17.3 41.6 %collective-permute-start.1 = (bf16[160,2304]{1,0:T(8,128)(2,1)}, bf16[160,2304]{1,0:T(8,128)(2,1)S(1)}, u32[]{:S(2)}, u32[]{:S(2)}) collective-permute-start(bf16[160,2304]{1,0:T(8,128)(2,1)} %fusion), channel_id=1, source_target_pairs={{0,32},{16,48},{32,64},{48,80},{64,96},{80,112},{96,128},{112,144}... | collective-permute-start | bytes 2211848 | tf_op jit(solution)/shard_map/ppermute | solution.py:327
  23.8 0.8 copy-start.2
  24.5 0.8 copy-start.4
  25.3 0.7 copy-start.7
  27.3 0.8 copy-start.9
  28.1 0.7 copy-start.10
  28.8 35.9 %copy-start.3 = (f32[1,32,256]{2,1,0:T(8,128)S(1)}, f32[1,32,256]{2,1,0:T(8,128)}, u32[]{:S(2)}) copy-start(f32[1,32,256]{2,1,0:T(8,128)} %param.12) | copy-start | bytes 98308
  28.8 35.9 %copy-start.5 = (bf16[1,1,4,32,64]{4,3,2,1,0:T(8,128)(2,1)S(1)}, bf16[1,1,4,32,64]{4,3,2,1,0:T(8,128)(2,1)}, u32[]{:S(2)}) copy-start(bf16[1,1,4,32,64]{4,3,2,1,0:T(8,128)(2,1)} %param.8) | copy-start | bytes 49156
  28.8 35.9 %copy-start.8 = (s32[1,1,2,1]{2,3,1,0:T(1,128)S(1)}, s32[1,1,2,1]{2,3,1,0:T(1,128)}, u32[]{:S(2)}) copy-start(s32[1,1,2,1]{2,3,1,0:T(1,128)} %param.9) | copy-start | bytes 28
  58.8 5.8 %collective-permute-start.2 = (bf16[32,512]{1,0:T(8,128)(2,1)S(1)}, bf16[32,512]{1,0:T(8,128)(2,1)S(1)}, u32[]{:S(2)}, u32[]{:S(2)}) collective-permute-start(bf16[32,512]{1,0:T(8,128)(2,1)S(1)} %sum_first.1.own_ref), channel_id=1, source_target_pairs={{0,8},{1,9},{2,10},{3,11},{4,12},{5,13},{6,14},{7,15},{8,0},{9,1},... | collective-permute-start | bytes 98312 | tf_op jit(solution)/shard_map/ppermute | solution.py:331
  67.4 9.9 %collective-permute-start.3 = (bf16[32,640]{1,0:T(8,128)(2,1)S(1)}, bf16[32,640]{1,0:T(8,128)(2,1)S(1)}, u32[]{:S(2)}, u32[]{:S(2)}) collective-permute-start(bf16[32,640]{1,0:T(8,128)(2,1)S(1)} %get-tuple-element.42), channel_id=1, source_target_pairs={{0,496},{16,0},{32,16},{48,32},{64,48},{80,64},{96,80},{112,96},{1... | collective-permute-start | bytes 122888 | tf_op jit(solution)/shard_map/ppermute | solution.py:327
  77.3 32.6 %collective-permute-start.4 = (bf16[128,2304]{1,0:T(8,128)(2,1)S(1)}, bf16[128,2304]{1,0:T(8,128)(2,1)S(1)}, u32[]{:S(2)}, u32[]{:S(2)}) collective-permute-start(bf16[128,2304]{1,0:T(8,128)(2,1)S(1)} %add_images.1), channel_id=1, source_target_pairs={{0,32},{16,48},{32,64},{48,80},{64,96},{80,112},{96,128},{112,144}... | collective-permute-start | bytes 1769480 | tf_op jit(solution)/shard_map/ppermute | solution.py:327
  109.9 10.1 %collective-permute-start.5 = (bf16[32,640]{1,0:T(8,128)(2,1)S(1)}, bf16[32,640]{1,0:T(8,128)(2,1)S(1)}, u32[]{:S(2)}, u32[]{:S(2)}) collective-permute-start(bf16[32,640]{1,0:T(8,128)(2,1)S(1)} %sum_second.1), channel_id=1, source_target_pairs={{0,16},{16,32},{32,48},{48,64},{64,80},{80,96},{96,112},{112,128},... | collective-permute-start | bytes 122888 | tf_op jit(solution)/shard_map/ppermute | solution.py:327
  120.0 8.0 %collective-permute-start.6 = (bf16[32,640]{1,0:T(8,128)(2,1)S(1)}, bf16[32,640]{1,0:T(8,128)(2,1)S(1)}, u32[]{:S(2)}, u32[]{:S(2)}) collective-permute-start(bf16[32,640]{1,0:T(8,128)(2,1)S(1)} %collective-permute-done.5.own_ref), channel_id=1, source_target_pairs={{0,8},{1,9},{2,10},{3,11},{4,12},{5,13},{6,14},{7,15},{8,0},{9,1},... | collective-permute-start | bytes 122888 | tf_op jit(solution)/shard_map/ppermute | solution.py:331

commit v4 on v3

--- a/solution.py
+++ b/solution.py
@@ -19,7 +19,9 @@
 KW = TAPS * CH
 PART_A = 160
 PART_B = CH - PART_A
-FIRST_WORK = 20_000_000_000
+EXTRA = 512
+FIRST_WORK = 2_000_000_000
+COPY_WORK = 4_000_000_000
 
 critic_rate = 0.05
 generator_rate = 0.2
@@ -144,6 +146,19 @@
     images_ref[:, FAKE:] = jnp.concatenate([real, jnp.zeros_like(real)], axis=1)
 
 
+def stage_kernel(kernel_ref, first_ref, second_ref, pool_ref, lift_ref, head_ref, noise_ref, part_ref, first_out, second_out, pool_out, lift_out, head_out, noise_out):
+    part_ref[...] = kernel_ref[...].astype(bf16)
+
+    @pl.when(pl.program_id(0) == 0)
+    def _():
+        first_out[...] = first_ref[...]
+        second_out[...] = second_ref[...]
+        pool_out[...] = pool_ref[...]
+        lift_out[...] = lift_ref[...]
+        head_out[...] = head_ref[...]
+        noise_out[...] = noise_ref[...]
+
+
 def noise_copies_kernel(place_ref, own_ref, other_ref, copies_ref):
     own_first = place_ref[0] < 8
     own = own_ref[...].astype(f32)
@@ -171,14 +186,18 @@
     out_ref[:, FAKE:] = score_ref[...]
 
 
-def put_halves(block_ref, images):
-    block_ref[:, :WIDE] = images[:16]
-    block_ref[:, WIDE : 2 * WIDE] = images[16:]
-
-
-def add_images_kernel(images_ref, part_ref, block_ref):
-    put_halves(block_ref, images_ref[...])
-    block_ref[:, 2 * WIDE :] = jnp.zeros((16, KW - 2 * WIDE), bf16)
+def add_images_kernel(images_ref, part_in, part_ref):
+    part_ref[:, : KW + EXTRA] = part_in[...]
+    images = images_ref[...]
+    part_ref[C : 2 * C, KW:] = images[:, :FAKE]
+    tails = jnp.concatenate([part_in[2 * C :, KW : KW + CELLS], images[:, FAKE : FAKE + CELLS]], axis=1)
+    part_ref[2 * C :, KW : KW + 128] = tails
+
+
+def moved_images(part_ref, which):
+    start = CELLS * which
+    tails = part_ref[2 * C : 3 * C, KW : KW + 128][:, start : start + CELLS]
+    return jnp.concatenate([part_ref[C * which : C * (which + 1), KW:], tails, jnp.zeros_like(tails)], axis=1)
 
 
 def generate_kernel(pick_ref, noise_ref, first_ref, second_ref, pool_ref, images_ref):
@@ -207,13 +226,13 @@
     for t in range(TAPS):
         cols = slice(CH * t, CH * (t + 1))
         kernel_out[:, cols] = (kernel_ref[:, cols] - critic_rate * dot(z_turned, patch_ref[t])).astype(bf16)
-        rest_out[:PART_B, cols] = half_ref[t, PART_A:, :]
-    block = rest_out.at[PART_B : PART_B + 16]
-    put_halves(block, images)
-    block[:, 1280:1536] = lift_half[:16]
-    block[:, 1536:1792] = lift_half[16:]
-    block[:, 1792:2048] = jnp.broadcast_to(head, (16, CH)).astype(bf16)
-    block[:, 2048:] = jnp.zeros((16, KW - 2048), bf16)
+        rest_out[:, cols] = half_ref[t, PART_A:, :]
+    rest_out[:C, KW:] = images[:, :FAKE]
+    rest_out[C : 2 * C, KW:] = jnp.zeros((C, EXTRA), bf16)
+    rest_out[2 * C :, KW : KW + 128] = images[:, FAKE:]
+    rest_out[2 * C :, KW + 128 : KW + 384] = lift_half
+    lane = jnp.concatenate([jnp.broadcast_to(head[:, :128], (16, 128)), jnp.broadcast_to(head[:, 128:], (16, 128))], axis=0)
+    rest_out[2 * C :, KW + 384 :] = lane.astype(bf16)
     score_out[...] = jnp.broadcast_to(score, (8, 128))
 
 
@@ -237,11 +256,11 @@
     for t in range(TAPS):
         cols = slice(CH * t, CH * (t + 1))
         half_ref[t, :PART_A] = part_a[:, cols]
-        half_ref[t, PART_A:] = part_b[:PART_B, cols]
-    block = part_b.at[PART_B : PART_B + 16]
-    images = jnp.concatenate([block[:, :WIDE], block[:, WIDE : 2 * WIDE]], axis=0)
-    lift_half = jnp.concatenate([block[:, 1280:1536], block[:, 1536:1792]], axis=0)
-    head = block[:, 1792:2048].astype(f32)[:1]
+        half_ref[t, PART_A:] = part_b[:, cols]
+    images = moved_images(part_b, 0)
+    lift_half = part_b[2 * C :, KW + 128 : KW + 384]
+    lane = part_b[2 * C :, KW + 384 :].astype(f32)
+    head = jnp.concatenate([lane[:1], lane[16:17]], axis=1)
     kernel_of = lambda t: half_ref[t]
     slope, z_grad, head_grad, _ = critic_forward(images, lift_half, kernel_of, head, patch_ref)
     pre_grad = lift_pullback(slope, z_grad.astype(bf16), kernel_of)
@@ -257,8 +276,7 @@
         half_ref[t] = kernel_ref[:, CH * t : CH * (t + 1)].astype(bf16)
     lift = lift_ref[...]
     head = head_ref[...]
-    block = part_b.at[PART_B + 16 :]
-    images = jnp.concatenate([block[:, :WIDE], block[:, WIDE : 2 * WIDE]], axis=0)
+    images = moved_images(part_b, 1)
     kernel_of = lambda t: half_ref[t]
     slope, z_grad, head_grad, _ = critic_forward(images, lift.astype(bf16), kernel_of, head, patch_ref)
     pre_grad = lift_pullback(slope, z_grad.astype(bf16), kernel_of)
@@ -356,11 +374,20 @@
     place = lax.axis_index("grp").astype(jnp.int32)[None]
     own_noise = jnp.swapaxes(noise_latents[0], 1, 2).reshape(ROUNDS * C, 128)
     other_noise = across(own_noise)
-    part_a = kernel[:PART_A].astype(bf16)
+    small = (first, second, pool, lift, head, own_noise)
+    whole = lambda x: pl.BlockSpec(x.shape, lambda i: (0,) * x.ndim)
+    part_a, first, second, pool, lift, head, own_noise = pl.pallas_call(
+        stage_kernel,
+        name="stage",
+        grid=(PART_A // 32,),
+        out_shape=[jax.ShapeDtypeStruct((PART_A, KW), bf16)] + [jax.ShapeDtypeStruct(x.shape, x.dtype) for x in small],
+        in_specs=[pl.BlockSpec((32, KW), lambda i: (i, 0))] + [whole(x) for x in small],
+        out_specs=[pl.BlockSpec((32, KW), lambda i: (i, 0))] + [whole(x) for x in small],
+        compiler_params=pltpu.CompilerParams(vmem_limit_bytes=24 * 1024 * 1024),
+    )(kernel, *small)
     (copies,) = call(
-        noise_copies_kernel, "noise_copies", [((8, 4 * C, 128), bf16)], (place, own_noise, other_noise), scalars=1
-    )
-    part_a, copies = together(part_a, copies)
+        noise_copies_kernel, "noise_copies", [((8, 4 * C, 128), bf16)], (place, own_noise, other_noise), scalars=1, work=COPY_WORK
+    )
     moved_a = shifted(part_a, 2)
     noise = swap(copies)
     (images,) = call(
@@ -369,7 +396,7 @@
     copies, lift_1, kernel_1, head_1, score_0, part_b = call(
         first_step_kernel,
         "first_step",
-        [((8, C, FAKE), bf16), ((C, CH), f32), ((CH, KW), bf16), ((1, CH), f32), ((8, 128), f32), ((PART_B + 32, KW), bf16)],
+        [((8, C, FAKE), bf16), ((C, CH), f32), ((CH, KW), bf16), ((1, CH), f32), ((8, 128), f32), ((PART_B, KW + EXTRA), bf16)],
         (images, lift, kernel, head),
         (PATCHES, HALVES),
         work=FIRST_WORK,
@@ -385,16 +412,9 @@
         scalars=1,
     )
     ahead_images = shifted(own_images, -1)
-    part_b = pl.pallas_call(
-        add_images_kernel,
-        name="add_images",
-        grid=(1,),
-        out_shape=jax.ShapeDtypeStruct((PART_B + 32, KW), bf16),
-        in_specs=[vmem(), pl.BlockSpec(memory_space=pl.ANY)],
-        out_specs=pl.BlockSpec((16, KW), lambda i: ((PART_B + 16) // 16, 0)),
-        input_output_aliases={1: 0},
-        compiler_params=pltpu.CompilerParams(vmem_limit_bytes=24 * 1024 * 1024),
-    )(ahead_images, part_b)
+    (part_b,) = call(
+        add_images_kernel, "add_images", [((PART_B, KW + EXTRA), bf16)], (ahead_images, part_b)
+    )
     part_b, ahead_images = together(part_b, ahead_images)
     moved_b = shifted(part_b, 2)
     copies, score_1 = call(

time: 132 us -> 126 us (0.955)
  blocking collectives: 20.1 us -> 30.2 us
  waiting for transfers between devices: 37.9 us -> 29.5 us
  starting transfers between devices: 38.5 us -> 32.2 us
    all_to_all x2 -> x3, blocking collectives: 20.1 us -> 30.2 us  [swap(): lax.all_to_all(copies, ('loop', 'grp'), 0, 0, axis_index_groups=groups)]
    all_to_all x1 -> x0, starting transfers between devices: 8.44 us -> none  [swap(): lax.all_to_all(copies, ('loop', 'grp'), 0, 0, axis_index_groups=groups)]
    ppermute x4, waiting for transfers between devices: 34 us -> 25.6 us  [shifted(): lax.ppermute(value, 'loop', [(s, (s + steps) % count) for s in range(coun...]
    convert_element_type x1 -> x0, local copies, waits for them, and re-layouts: 2.31 us -> none  [per_device(): part_a = kernel[:PART_A].astype(bf16)]
    ppermute x4, starting transfers between devices: 21.8 us -> 24.1 us  [shifted(): lax.ppermute(value, 'loop', [(s, (s + steps) % count) for s in range(coun...]
    unnamed x22 -> x18, local copies, waits for them, and re-layouts: 4.34 us -> 6.24 us
    pallas_call x9 -> x10, Pallas kernels: 24 us -> 23.5 us  [call(): pl.pallas_call(kernel, name=name, out_shape=[jax.ShapeDtypeStruct(s, d) f...]
  transfers between devices with their start and end apart: 8 -> 7, of which waited for: 5 -> 5; matrix products, arithmetic and copies ran while one was open for 2% -> 0% of each run, Pallas kernels for 16% -> 17%
where the time goes in v4:
time: 126 us; the launch traced here: 125 us
  starting transfers between devices  32.2 us (26%)
  blocking collectives  30.2 us (24%)
  waiting for transfers between devices  29.5 us (23%)
  Pallas kernels  25.8 us (20%)
  local copies, waits for them, and re-layouts  6.24 us (5%)
    all_to_all x3, blocking collectives, swap(): lax.all_to_all(copies, ('loop', 'grp'), 0, 0, axis_index_groups=groups)  30.2 us
    ppermute x4, waiting for transfers between devices, shifted(): lax.ppermute(value, 'loop', [(s, (s + steps) % count) for s in range(coun...  25.6 us
    ppermute x4, starting transfers between devices, shifted(): lax.ppermute(value, 'loop', [(s, (s + steps) % count) for s in range(coun...  24.1 us
    pallas_call x10, Pallas kernels, call(): pl.pallas_call(kernel, name=name, out_shape=[jax.ShapeDtypeStruct(s, d) f...  23.5 us
    ppermute x3, starting transfers between devices, across(): return lax.ppermute(value, 'grp', [(m, m ^ 8) for m in range(N_GRP)])  8.1 us
    unnamed x18, local copies, waits for them, and re-layouts  6.24 us
    ppermute x3, waiting for transfers between devices, across(): return lax.ppermute(value, 'grp', [(m, m ^ 8) for m in range(N_GRP)])  3.89 us
  transfers between devices with their start and end apart: 7, of which 5 were waited for; matrix products, arithmetic and copies ran while one was open for 0% of the time, Pallas kernels for 17%

profile of v4, /device:TPU:6, one launch (start us, length us, event | category | flops | bytes accessed | tf_op | source)
XLA Modules:
  0.0 125.3 jit_solution(1127602106686217358)
XLA Ops:
  0.6 4.3 %collective-permute-start = (bf16[64,128]{1,0:T(8,128)(2,1)}, bf16[64,128]{1,0:T(8,128)(2,1)S(1)}, u32[]{:S(2)}, u32[]{:S(2)}) collective-permute-start(bf16[64,128]{1,0:T(8,128)(2,1)} %bitcast.30), channel_id=1, source_target_pairs={{0,8},{1,9},{2,10},{3,11},{4,12},{5,13},{6,14},{7,15},{8,0},{9,1},... | collective-permute-start | bytes 49160 | tf_op jit(solution)/shard_map/ppermute | solution.py:349
  4.9 1.7 %copy-done = f32[1,1,256,2304]{3,2,1,0:T(8,128)S(1)} copy-done((f32[1,1,256,2304]{3,2,1,0:T(8,128)S(1)}, f32[1,1,256,2304]{3,2,1,0:T(8,128)}, u32[]{:S(2)}) %copy-start) | copy-done | bytes 2359320
  6.6 0.9 copy-done.2
  11.3 10.0 %collective-permute-start.1 = (bf16[160,2304]{1,0:T(8,128)(2,1)S(1)}, bf16[160,2304]{1,0:T(8,128)(2,1)S(1)}, u32[]{:S(2)}, u32[]{:S(2)}) collective-permute-start(bf16[160,2304]{1,0:T(8,128)(2,1)S(1)} %get-tuple-element.50), channel_id=1, source_target_pairs={{0,32},{16,48},{32,64},{48,80},{64,96},{80,112},{96,128},{112,144}... | collective-permute-start | bytes 2211848 | tf_op jit(solution)/shard_map/ppermute | solution.py:345
  21.4 10.2 %all_to_all.15.noise_ref = bf16[8,128,128]{2,1,0:T(8,128)(2,1)S(1)} all-to-all(bf16[8,128,128]{2,1,0:T(8,128)(2,1)S(1)} %noise_copies.1), channel_id=1, replica_groups={{0,1,2,3,4,5,6,7},{8,9,10,11,12,13,14,15},{16,17,18,19,20,21,22,23},{24..., dimensions={0} | all-to-all | bytes 524288 | tf_op jit(solution)/shard_map/all_to_all | solution.py:355
  31.6 1.3 %make_fakes.1.images_ref = bf16[32,640]{1,0:T(8,128)(2,1)S(1)} custom-call(s32[2]{0:T(128)S(1)} %bitcast.32, bf16[8,128,128]{2,1,0:T(8,128)(2,1)S(1)} %all_to_all.15.noise_ref, f32[256,128]{1,0:T(8,128)S(1)} %get-tuple-element.44.first_ref, f32[32,256]{1,0:T(8,128)S(1)} %get-tuple-element.45.second_ref, bf16[4,32,64]{2,1,0:T(8,128)(2,1)S(1)} %get-tuple-element.46.pool_ref), custom_call_target="tpu_custom_call" | custom-call | tf_op jit(solution)/shard_map/make_fakes/pallas_call | solution.py:331
  33.0 4.8 %first_step.1 = (bf16[8,32,512]{2,1,0:T(8,128)(2,1)S(1)}, f32[32,256]{1,0:T(8,128)S(1)}, bf16[256,2304]{1,0:T(8,128)(2,1)S(1)}, f32[1,256]{1,0:T(1,128)S(1)}, f3...) custom-call(bf16[32,640]{1,0:T(8,128)(2,1)S(1)} %make_fakes.1.images_ref, f32[32,256]{1,0:T(8,128)S(1)} %get-tuple-element.47.lift_ref, ...), custom_call_target="tpu_custom_call" | custom-call | flops 2000000000 | tf_op jit(solution)/shard_map/first_step/pallas_call | solution.py:331
  37.8 9.9 %all_to_all.16.pulls_ref = bf16[8,32,512]{2,1,0:T(8,128)(2,1)S(1)} all-to-all(bf16[8,32,512]{2,1,0:T(8,128)(2,1)S(1)} %get-tuple-element.49), channel_id=1, replica_groups={{0,1,2,3,4,5,6,7},{8,9,10,11,12,13,14,15},{16,17,18,19,20,21,22,23},{24..., dimensions={0} | all-to-all | bytes 524288 | tf_op jit(solution)/shard_map/all_to_all | solution.py:355
  47.8 7.6 %collective-permute-done.1.part_a = bf16[160,2304]{1,0:T(8,128)(2,1)S(1)} collective-permute-done((bf16[160,2304]{1,0:T(8,128)(2,1)S(1)}, bf16[160,2304]{1,0:T(8,128)(2,1)S(1)}, u32[]{:S(2)}, u32[]{:S(2)}) %collective-permute-start.1) | collective-permute-done | bytes 737312 | tf_op jit(solution)/shard_map/ppermute | solution.py:345
  55.4 1.9 %collective-permute-start.2 = (bf16[32,512]{1,0:T(8,128)(2,1)S(1)}, bf16[32,512]{1,0:T(8,128)(2,1)S(1)}, u32[]{:S(2)}, u32[]{:S(2)}) collective-permute-start(bf16[32,512]{1,0:T(8,128)(2,1)S(1)} %sum_first.1.own_ref), channel_id=1, source_target_pairs={{0,8},{1,9},{2,10},{3,11},{4,12},{5,13},{6,14},{7,15},{8,0},{9,1},... | collective-permute-start | bytes 98312 | tf_op jit(solution)/shard_map/ppermute | solution.py:349
  57.3 3.9 %collective-permute-done.2.other_ref = bf16[32,512]{1,0:T(8,128)(2,1)S(1)} collective-permute-done((bf16[32,512]{1,0:T(8,128)(2,1)S(1)}, bf16[32,512]{1,0:T(8,128)(2,1)S(1)}, u32[]{:S(2)}, u32[]{:S(2)}) %collective-permute-start.2) | collective-permute-done | bytes 32800 | tf_op jit(solution)/shard_map/ppermute | solution.py:349
  61.1 2.8 %generator_step.1 = (bf16[32,640]{1,0:T(8,128)(2,1)S(1)}, f32[256,128]{1,0:T(8,128)S(1)}, f32[32,256]{1,0:T(8,128)S(1)}) custom-call(s32[2]{0:T(128)S(1)} %bitcast.33, bf16[32,512]{1,0:T(8,128)(2,1)S(1)} %sum_first.1.own_ref, bf16[32,512]{1,0:T(8,128)(2,1)S(1)} %collective-permute-done.2.other_ref, bf16[8,128,128]{2,1,0:T(8,128)(2,1)S(1)} %all_to_all.15.noise_ref, ...), custom_call_target="tpu_custom_call" | custom-call | tf_op jit(solution)/shard_map/generator_step/pallas_call | solution.py:331
  63.9 8.5 %collective-permute-start.3 = (bf16[32,640]{1,0:T(8,128)(2,1)S(1)}, bf16[32,640]{1,0:T(8,128)(2,1)S(1)}, u32[]{:S(2)}, u32[]{:S(2)}) collective-permute-start(bf16[32,640]{1,0:T(8,128)(2,1)S(1)} %get-tuple-element.52), channel_id=1, source_target_pairs={{0,496},{16,0},{32,16},{48,32},{64,48},{80,64},{96,80},{112,96},{1... | collective-permute-start | bytes 122888 | tf_op jit(solution)/shard_map/ppermute | solution.py:345
  72.4 1.7 %collective-permute-done.3.images_ref = bf16[32,640]{1,0:T(8,128)(2,1)S(1)} collective-permute-done((bf16[32,640]{1,0:T(8,128)(2,1)S(1)}, bf16[32,640]{1,0:T(8,128)(2,1)S(1)}, u32[]{:S(2)}, u32[]{:S(2)}) %collective-permute-start.3) | collective-permute-done | bytes 40992 | tf_op jit(solution)/shard_map/ppermute | solution.py:345
  74.2 2.7 %collective-permute-start.4 = (bf16[96,2816]{1,0:T(8,128)(2,1)S(1)}, bf16[96,2816]{1,0:T(8,128)(2,1)S(1)}, u32[]{:S(2)}, u32[]{:S(2)}) collective-permute-start(bf16[96,2816]{1,0:T(8,128)(2,1)S(1)} %add_images.1), channel_id=1, source_target_pairs={{0,32},{16,48},{32,64},{48,80},{64,96},{80,112},{96,128},{112,144}... | collective-permute-start | bytes 1622024 | tf_op jit(solution)/shard_map/ppermute | solution.py:345
  76.8 3.6 %second_pull.1 = (bf16[8,32,512]{2,1,0:T(8,128)(2,1)S(1)}, bf16[32,128]{1,0:T(8,128)(2,1)S(1)}) custom-call(bf16[32,640]{1,0:T(8,128)(2,1)S(1)} %collective-permute-done.3.images_ref, f32[32,256]{1,0:T(8,128)S(1)} %get-tuple-element.55.lift_ref, bf16[256,2304]{1,0:T(8,128)(2,1)S(1)} %get-tuple-element.56.kernel_ref, f32[1,256]{1,0:T(1,128)S(1)} %get-tuple-element.57.head_ref), custom_call_target="tpu_custom_call" | custom-call | tf_op jit(solution)/shard_map/second_pull/pallas_call | solution.py:331
  80.5 10.0 %all_to_all.17.pulls_ref = bf16[8,32,512]{2,1,0:T(8,128)(2,1)S(1)} all-to-all(bf16[8,32,512]{2,1,0:T(8,128)(2,1)S(1)} %get-tuple-element.58), channel_id=1, replica_groups={{0,1,2,3,4,5,6,7},{8,9,10,11,12,13,14,15},{16,17,18,19,20,21,22,23},{24..., dimensions={0} | all-to-all | bytes 524288 | tf_op jit(solution)/shard_map/all_to_all | solution.py:355
  90.5 13.8 %collective-permute-done.4.part_b = bf16[96,2816]{1,0:T(8,128)(2,1)S(1)} collective-permute-done((bf16[96,2816]{1,0:T(8,128)(2,1)S(1)}, bf16[96,2816]{1,0:T(8,128)(2,1)S(1)}, u32[]{:S(2)}, u32[]{:S(2)}) %collective-permute-start.4) | collective-permute-done | bytes 540704 | tf_op jit(solution)/shard_map/ppermute | solution.py:345
  104.4 2.9 %collective-permute-start.5 = (bf16[32,640]{1,0:T(8,128)(2,1)S(1)}, bf16[32,640]{1,0:T(8,128)(2,1)S(1)}, u32[]{:S(2)}, u32[]{:S(2)}) collective-permute-start(bf16[32,640]{1,0:T(8,128)(2,1)S(1)} %sum_second.1), channel_id=1, source_target_pairs={{0,16},{16,32},{32,48},{48,64},{64,80},{80,96},{96,112},{112,128},... | collective-permute-start | bytes 122888 | tf_op jit(solution)/shard_map/ppermute | solution.py:345
  107.3 4.7 %moved_first.1 = (f32[32,256]{1,0:T(8,128)S(1)}, f32[256,2304]{1,0:T(8,128)S(1)}, f32[1,256]{1,0:T(1,128)S(1)}) custom-call(bf16[160,2304]{1,0:T(8,128)(2,1)S(1)} %collective-permute-done.1.part_a, bf16[96,2816]{1,0:T(8,128)(2,1)S(1)} %collective-permute-done.4.part_b), custom_call_target="tpu_custom_call" | custom-call | tf_op jit(solution)/shard_map/moved_first/pallas_call | solution.py:331
  111.9 2.5 %collective-permute-done.5.own_ref = bf16[32,640]{1,0:T(8,128)(2,1)S(1)} collective-permute-done((bf16[32,640]{1,0:T(8,128)(2,1)S(1)}, bf16[32,640]{1,0:T(8,128)(2,1)S(1)}, u32[]{:S(2)}, u32[]{:S(2)}) %collective-permute-start.5) | collective-permute-done | bytes 40992 | tf_op jit(solution)/shard_map/ppermute | solution.py:345
  114.5 1.9 %collective-permute-start.6 = (bf16[32,640]{1,0:T(8,128)(2,1)S(1)}, bf16[32,640]{1,0:T(8,128)(2,1)S(1)}, u32[]{:S(2)}, u32[]{:S(2)}) collective-permute-start(bf16[32,640]{1,0:T(8,128)(2,1)S(1)} %collective-permute-done.5.own_ref), channel_id=1, source_target_pairs={{0,8},{1,9},{2,10},{3,11},{4,12},{5,13},{6,14},{7,15},{8,0},{9,1},... | collective-permute-start | bytes 122888 | tf_op jit(solution)/shard_map/ppermute | solution.py:349
  116.4 6.1 %moved_second.1 = (f32[32,256]{1,0:T(8,128)}, f32[256,2304]{1,0:T(8,128)}, f32[1,256]{1,0:T(1,128)}) custom-call(bf16[96,2816]{1,0:T(8,128)(2,1)S(1)} %collective-permute-done.4.part_b, f32[32,256]{1,0:T(8,128)S(1)} %get-tuple-element.65.lift_ref, f32[256,2304]{1,0:T(8,128)S(1)} %get-tuple-element.66.kernel_ref, f32[1,256]{1,0:T(1,128)S(1)} %get-tuple-element.67.head_ref), custom_call_target="tpu_custom_call" | custom-call | tf_op jit(solution)/shard_map/moved_second/pallas_call | solution.py:331
  122.5 2.1 %generator_last.1 = (f32[256,128]{1,0:T(8,128)}, f32[32,256]{1,0:T(8,128)}, f32[32,32]{1,0:T(8,128)}, f32[2,1]{1,0:T(2,128)S(1)}) custom-call(s32[1]{0:T(128)} %bitcast.1.place_ref, bf16[32,640]{1,0:T(8,128)(2,1)S(1)} %collective-permute-done.5.own_ref, bf16[32,640]{1,0:T(8,128)(2,1)S(1)} %collective-permute-done.6.other_ref, ...), custom_call_target="tpu_custom_call" | custom-call | tf_op jit(solution)/shard_map/generator_last/pallas_call | solution.py:447
  (24 shorter events, 4.7 us)
Async XLA Ops:
  0.6 20.7 %collective-permute-start = (bf16[64,128]{1,0:T(8,128)(2,1)}, bf16[64,128]{1,0:T(8,128)(2,1)S(1)}, u32[]{:S(2)}, u32[]{:S(2)}) collective-permute-start(bf16[64,128]{1,0:T(8,128)(2,1)} %bitcast.30), channel_id=1, source_target_pairs={{0,8},{1,9},{2,10},{3,11},{4,12},{5,13},{6,14},{7,15},{8,0},{9,1},... | collective-permute-start | bytes 49160 | tf_op jit(solution)/shard_map/ppermute | solution.py:349
  4.9 1.7 %copy-start = (f32[1,1,256,2304]{3,2,1,0:T(8,128)S(1)}, f32[1,1,256,2304]{3,2,1,0:T(8,128)}, u32[]{:S(2)}) copy-start(f32[1,1,256,2304]{3,2,1,0:T(8,128)} %param.14) | copy-start | bytes 7077892
  6.6 0.9 copy-start.2
  7.5 0.8 copy-start.3
  8.3 0.8 copy-start.4
  9.0 0.8 copy-start.5
  9.8 0.7 copy-start.6
  10.5 0.7 copy-start.8
  11.3 44.0 %collective-permute-start.1 = (bf16[160,2304]{1,0:T(8,128)(2,1)S(1)}, bf16[160,2304]{1,0:T(8,128)(2,1)S(1)}, u32[]{:S(2)}, u32[]{:S(2)}) collective-permute-start(bf16[160,2304]{1,0:T(8,128)(2,1)S(1)} %get-tuple-element.50), channel_id=1, source_target_pairs={{0,32},{16,48},{32,64},{48,80},{64,96},{80,112},{96,128},{112,144}... | collective-permute-start | bytes 2211848 | tf_op jit(solution)/shard_map/ppermute | solution.py:345
  21.4 10.2 %copy-start.7 = (s32[1,1,2,1]{2,3,1,0:T(1,128)S(1)}, s32[1,1,2,1]{2,3,1,0:T(1,128)}, u32[]{:S(2)}) copy-start(s32[1,1,2,1]{2,3,1,0:T(1,128)} %param.9) | copy-start | bytes 28
  21.4 11.6 %copy-start.1 = (f32[1,1,256,2304]{3,2,1,0:T(8,128)S(1)}, f32[1,1,256,2304]{3,2,1,0:T(8,128)}, u32[]{:S(2)}) copy-start(f32[1,1,256,2304]{3,2,1,0:T(8,128)} %param.14) | copy-start | bytes 7077892
  55.4 5.8 %collective-permute-start.2 = (bf16[32,512]{1,0:T(8,128)(2,1)S(1)}, bf16[32,512]{1,0:T(8,128)(2,1)S(1)}, u32[]{:S(2)}, u32[]{:S(2)}) collective-permute-start(bf16[32,512]{1,0:T(8,128)(2,1)S(1)} %sum_first.1.own_ref), channel_id=1, source_target_pairs={{0,8},{1,9},{2,10},{3,11},{4,12},{5,13},{6,14},{7,15},{8,0},{9,1},... | collective-permute-start | bytes 98312 | tf_op jit(solution)/shard_map/ppermute | solution.py:349
  63.9 10.1 %collective-permute-start.3 = (bf16[32,640]{1,0:T(8,128)(2,1)S(1)}, bf16[32,640]{1,0:T(8,128)(2,1)S(1)}, u32[]{:S(2)}, u32[]{:S(2)}) collective-permute-start(bf16[32,640]{1,0:T(8,128)(2,1)S(1)} %get-tuple-element.52), channel_id=1, source_target_pairs={{0,496},{16,0},{32,16},{48,32},{64,48},{80,64},{96,80},{112,96},{1... | collective-permute-start | bytes 122888 | tf_op jit(solution)/shard_map/ppermute | solution.py:345
  74.2 30.2 %collective-permute-start.4 = (bf16[96,2816]{1,0:T(8,128)(2,1)S(1)}, bf16[96,2816]{1,0:T(8,128)(2,1)S(1)}, u32[]{:S(2)}, u32[]{:S(2)}) collective-permute-start(bf16[96,2816]{1,0:T(8,128)(2,1)S(1)} %add_images.1), channel_id=1, source_target_pairs={{0,32},{16,48},{32,64},{48,80},{64,96},{80,112},{96,128},{112,144}... | collective-permute-start | bytes 1622024 | tf_op jit(solution)/shard_map/ppermute | solution.py:345
  104.4 10.1 %collective-permute-start.5 = (bf16[32,640]{1,0:T(8,128)(2,1)S(1)}, bf16[32,640]{1,0:T(8,128)(2,1)S(1)}, u32[]{:S(2)}, u32[]{:S(2)}) collective-permute-start(bf16[32,640]{1,0:T(8,128)(2,1)S(1)} %sum_second.1), channel_id=1, source_target_pairs={{0,16},{16,32},{32,48},{48,64},{64,80},{80,96},{96,112},{112,128},... | collective-permute-start | bytes 122888 | tf_op jit(solution)/shard_map/ppermute | solution.py:345
  114.5 8.0 %collective-permute-start.6 = (bf16[32,640]{1,0:T(8,128)(2,1)S(1)}, bf16[32,640]{1,0:T(8,128)(2,1)S(1)}, u32[]{:S(2)}, u32[]{:S(2)}) collective-permute-start(bf16[32,640]{1,0:T(8,128)(2,1)S(1)} %collective-permute-done.5.own_ref), channel_id=1, source_target_pairs={{0,8},{1,9},{2,10},{3,11},{4,12},{5,13},{6,14},{7,15},{8,0},{9,1},... | collective-permute-start | bytes 122888 | tf_op jit(solution)/shard_map/ppermute | solution.py:349

commit v5 on v4

--- a/solution.py
+++ b/solution.py
@@ -146,17 +146,19 @@
     images_ref[:, FAKE:] = jnp.concatenate([real, jnp.zeros_like(real)], axis=1)
 
 
-def stage_kernel(kernel_ref, first_ref, second_ref, pool_ref, lift_ref, head_ref, noise_ref, part_ref, first_out, second_out, pool_out, lift_out, head_out, noise_out):
-    part_ref[...] = kernel_ref[...].astype(bf16)
-
-    @pl.when(pl.program_id(0) == 0)
-    def _():
-        first_out[...] = first_ref[...]
-        second_out[...] = second_ref[...]
-        pool_out[...] = pool_ref[...]
-        lift_out[...] = lift_ref[...]
-        head_out[...] = head_ref[...]
-        noise_out[...] = noise_ref[...]
+def stage_kernel(*refs):
+    count = 6
+    kernel_ref, small = refs[0], refs[1 : 1 + count]
+    part_ref, small_out = refs[1 + count], refs[2 + count : 2 + 2 * count]
+    rows_ref, sems = refs[-2:]
+    copies = [pltpu.make_async_copy(kernel_ref.at[:PART_A], rows_ref, sems.at[count])]
+    copies += [pltpu.make_async_copy(small[k], small_out[k], sems.at[k]) for k in range(count)]
+    for copy in copies:
+        copy.start()
+    copies[0].wait()
+    part_ref[...] = rows_ref[...].astype(bf16)
+    for copy in copies[1:]:
+        copy.wait()
 
 
 def noise_copies_kernel(place_ref, own_ref, other_ref, copies_ref):
@@ -375,15 +377,14 @@
     own_noise = jnp.swapaxes(noise_latents[0], 1, 2).reshape(ROUNDS * C, 128)
     other_noise = across(own_noise)
     small = (first, second, pool, lift, head, own_noise)
-    whole = lambda x: pl.BlockSpec(x.shape, lambda i: (0,) * x.ndim)
     part_a, first, second, pool, lift, head, own_noise = pl.pallas_call(
         stage_kernel,
         name="stage",
-        grid=(PART_A // 32,),
         out_shape=[jax.ShapeDtypeStruct((PART_A, KW), bf16)] + [jax.ShapeDtypeStruct(x.shape, x.dtype) for x in small],
-        in_specs=[pl.BlockSpec((32, KW), lambda i: (i, 0))] + [whole(x) for x in small],
-        out_specs=[pl.BlockSpec((32, KW), lambda i: (i, 0))] + [whole(x) for x in small],
-        compiler_params=pltpu.CompilerParams(vmem_limit_bytes=24 * 1024 * 1024),
+        in_specs=[pl.BlockSpec(memory_space=pltpu.HBM)] * 7,
+        out_specs=[vmem()] * 7,
+        scratch_shapes=[pltpu.VMEM((PART_A, KW), f32), pltpu.SemaphoreType.DMA((7,))],
+        compiler_params=pltpu.CompilerParams(vmem_limit_bytes=56 * 1024 * 1024),
     )(kernel, *small)
     (copies,) = call(
         noise_copies_kernel, "noise_copies", [((8, 4 * C, 128), bf16)], (place, own_noise, other_noise), scalars=1, work=COPY_WORK

time: 126 us -> 122 us (0.968)
  local copies, waits for them, and re-layouts: 6.24 us -> 0.75 us
  Pallas kernels: 25.8 us -> 28.1 us
    unnamed x18 -> x16, local copies, waits for them, and re-layouts: 6.24 us -> 0.75 us
    pallas_call x1, Pallas kernels: 0.16 us -> 2.45 us  [per_device(): pl.pallas_call(stage_kernel, name='stage', out_shape=[jax.ShapeDtypeStruc...]
  transfers between devices with their start and end apart: 7 -> 7, of which waited for: 5 -> 5; matrix products, arithmetic and copies ran while one was open for 0% -> 0% of each run, Pallas kernels for 17% -> 19%
where the time goes in v5:
time: 122 us
  starting transfers between devices  32.2 us (26%)
  blocking collectives  30.2 us (25%)
  waiting for transfers between devices  28.9 us (24%)
  Pallas kernels  28.1 us (23%)
    all_to_all x3, blocking collectives, swap(): lax.all_to_all(copies, ('loop', 'grp'), 0, 0, axis_index_groups=groups)  30.2 us
    ppermute x4, waiting for transfers between devices, shifted(): lax.ppermute(value, 'loop', [(s, (s + steps) % count) for s in range(coun...  25 us
    ppermute x4, starting transfers between devices, shifted(): lax.ppermute(value, 'loop', [(s, (s + steps) % count) for s in range(coun...  24.1 us
    pallas_call x10, Pallas kernels, call(): pl.pallas_call(kernel, name=name, out_shape=[jax.ShapeDtypeStruct(s, d) f...  23.5 us
    ppermute x3, starting transfers between devices, across(): return lax.ppermute(value, 'grp', [(m, m ^ 8) for m in range(N_GRP)])  8.1 us
    ppermute x3, waiting for transfers between devices, across(): return lax.ppermute(value, 'grp', [(m, m ^ 8) for m in range(N_GRP)])  3.89 us
    pallas_call x1, Pallas kernels, per_device(): pl.pallas_call(stage_kernel, name='stage', out_shape=[jax.ShapeDtypeStruc...  2.45 us
  transfers between devices with their start and end apart: 7, of which 5 were waited for; matrix products, arithmetic and copies ran while one was open for 0% of the time, Pallas kernels for 19%

profile of v5, /device:TPU:6, one launch (start us, length us, event | category | flops | bytes accessed | tf_op | source)
XLA Modules:
  0.0 121.5 jit_solution(4408526357748460937)
XLA Ops:
  0.6 4.3 %collective-permute-start = (bf16[64,128]{1,0:T(8,128)(2,1)}, bf16[64,128]{1,0:T(8,128)(2,1)S(1)}, u32[]{:S(2)}, u32[]{:S(2)}) collective-permute-start(bf16[64,128]{1,0:T(8,128)(2,1)} %bitcast.32), channel_id=1, source_target_pairs={{0,8},{1,9},{2,10},{3,11},{4,12},{5,13},{6,14},{7,15},{8,0},{9,1},... | collective-permute-start | bytes 49160 | tf_op jit(solution)/shard_map/ppermute | solution.py:351
  4.9 2.4 %stage.1 = (bf16[160,2304]{1,0:T(8,128)(2,1)}, f32[256,128]{1,0:T(8,128)}, f32[32,256]{1,0:T(8,128)}, bf16[4,32,64]{2,1,0:T(8,128)(2,1)}, f32[32,256]{1,0:T(8,12...) custom-call(f32[256,2304]{1,0:T(8,128)} %bitcast.24, f32[256,128]{1,0:T(8,128)} %bitcast.28, f32[32,256]{1,0:T(8,128)} %bitcast.29, ...), custom_call_target="tpu_custom_call" | custom-call | tf_op jit(solution)/shard_map/stage/pallas_call | solution.py:380
  7.4 10.0 %collective-permute-start.1 = (bf16[160,2304]{1,0:T(8,128)(2,1)}, bf16[160,2304]{1,0:T(8,128)(2,1)S(1)}, u32[]{:S(2)}, u32[]{:S(2)}) collective-permute-start(bf16[160,2304]{1,0:T(8,128)(2,1)} %get-tuple-element.50), channel_id=1, source_target_pairs={{0,32},{16,48},{32,64},{48,80},{64,96},{80,112},{96,128},{112,144}... | collective-permute-start | bytes 2211848 | tf_op jit(solution)/shard_map/ppermute | solution.py:347
  17.4 0.7 copy-done.6
  18.2 10.2 %all_to_all.15.noise_ref = bf16[8,128,128]{2,1,0:T(8,128)(2,1)S(1)} all-to-all(bf16[8,128,128]{2,1,0:T(8,128)(2,1)S(1)} %noise_copies.1), channel_id=1, replica_groups={{0,1,2,3,4,5,6,7},{8,9,10,11,12,13,14,15},{16,17,18,19,20,21,22,23},{24..., dimensions={0} | all-to-all | bytes 524288 | tf_op jit(solution)/shard_map/all_to_all | solution.py:357
  28.4 1.3 %make_fakes.1.images_ref = bf16[32,640]{1,0:T(8,128)(2,1)S(1)} custom-call(s32[2]{0:T(128)S(1)} %bitcast.26, bf16[8,128,128]{2,1,0:T(8,128)(2,1)S(1)} %all_to_all.15.noise_ref, f32[256,128]{1,0:T(8,128)S(1)} %copy-done.1, f32[32,256]{1,0:T(8,128)S(1)} %copy-done.2, bf16[4,32,64]{2,1,0:T(8,128)(2,1)S(1)} %copy-done.3), custom_call_target="tpu_custom_call" | custom-call | tf_op jit(solution)/shard_map/make_fakes/pallas_call | solution.py:333
  29.8 4.8 %first_step.1 = (bf16[8,32,512]{2,1,0:T(8,128)(2,1)S(1)}, f32[32,256]{1,0:T(8,128)S(1)}, bf16[256,2304]{1,0:T(8,128)(2,1)S(1)}, f32[1,256]{1,0:T(1,128)S(1)}, f3...) custom-call(bf16[32,640]{1,0:T(8,128)(2,1)S(1)} %make_fakes.1.images_ref, f32[32,256]{1,0:T(8,128)S(1)} %copy-done.5, ...), custom_call_target="tpu_custom_call" | custom-call | flops 2000000000 | tf_op jit(solution)/shard_map/first_step/pallas_call | solution.py:333
  34.6 9.9 %all_to_all.16.pulls_ref = bf16[8,32,512]{2,1,0:T(8,128)(2,1)S(1)} all-to-all(bf16[8,32,512]{2,1,0:T(8,128)(2,1)S(1)} %get-tuple-element.49), channel_id=1, replica_groups={{0,1,2,3,4,5,6,7},{8,9,10,11,12,13,14,15},{16,17,18,19,20,21,22,23},{24..., dimensions={0} | all-to-all | bytes 524288 | tf_op jit(solution)/shard_map/all_to_all | solution.py:357
  44.6 7.0 %collective-permute-done.1.part_a = bf16[160,2304]{1,0:T(8,128)(2,1)S(1)} collective-permute-done((bf16[160,2304]{1,0:T(8,128)(2,1)}, bf16[160,2304]{1,0:T(8,128)(2,1)S(1)}, u32[]{:S(2)}, u32[]{:S(2)}) %collective-permute-start.1) | collective-permute-done | bytes 737312 | tf_op jit(solution)/shard_map/ppermute | solution.py:347
  51.6 1.9 %collective-permute-start.2 = (bf16[32,512]{1,0:T(8,128)(2,1)S(1)}, bf16[32,512]{1,0:T(8,128)(2,1)S(1)}, u32[]{:S(2)}, u32[]{:S(2)}) collective-permute-start(bf16[32,512]{1,0:T(8,128)(2,1)S(1)} %sum_first.1.own_ref), channel_id=1, source_target_pairs={{0,8},{1,9},{2,10},{3,11},{4,12},{5,13},{6,14},{7,15},{8,0},{9,1},... | collective-permute-start | bytes 98312 | tf_op jit(solution)/shard_map/ppermute | solution.py:351
  53.5 3.9 %collective-permute-done.2.other_ref = bf16[32,512]{1,0:T(8,128)(2,1)S(1)} collective-permute-done((bf16[32,512]{1,0:T(8,128)(2,1)S(1)}, bf16[32,512]{1,0:T(8,128)(2,1)S(1)}, u32[]{:S(2)}, u32[]{:S(2)}) %collective-permute-start.2) | collective-permute-done | bytes 32800 | tf_op jit(solution)/shard_map/ppermute | solution.py:351
  57.4 2.8 %generator_step.1 = (bf16[32,640]{1,0:T(8,128)(2,1)S(1)}, f32[256,128]{1,0:T(8,128)S(1)}, f32[32,256]{1,0:T(8,128)S(1)}) custom-call(s32[2]{0:T(128)S(1)} %bitcast.27, bf16[32,512]{1,0:T(8,128)(2,1)S(1)} %sum_first.1.own_ref, bf16[32,512]{1,0:T(8,128)(2,1)S(1)} %collective-permute-done.2.other_ref, bf16[8,128,128]{2,1,0:T(8,128)(2,1)S(1)} %all_to_all.15.noise_ref, ...), custom_call_target="tpu_custom_call" | custom-call | tf_op jit(solution)/shard_map/generator_step/pallas_call | solution.py:333
  60.2 8.5 %collective-permute-start.3 = (bf16[32,640]{1,0:T(8,128)(2,1)S(1)}, bf16[32,640]{1,0:T(8,128)(2,1)S(1)}, u32[]{:S(2)}, u32[]{:S(2)}) collective-permute-start(bf16[32,640]{1,0:T(8,128)(2,1)S(1)} %get-tuple-element.52), channel_id=1, source_target_pairs={{0,496},{16,0},{32,16},{48,32},{64,48},{80,64},{96,80},{112,96},{1... | collective-permute-start | bytes 122888 | tf_op jit(solution)/shard_map/ppermute | solution.py:347
  68.7 1.7 %collective-permute-done.3.images_ref = bf16[32,640]{1,0:T(8,128)(2,1)S(1)} collective-permute-done((bf16[32,640]{1,0:T(8,128)(2,1)S(1)}, bf16[32,640]{1,0:T(8,128)(2,1)S(1)}, u32[]{:S(2)}, u32[]{:S(2)}) %collective-permute-start.3) | collective-permute-done | bytes 40992 | tf_op jit(solution)/shard_map/ppermute | solution.py:347
  70.4 2.7 %collective-permute-start.4 = (bf16[96,2816]{1,0:T(8,128)(2,1)S(1)}, bf16[96,2816]{1,0:T(8,128)(2,1)S(1)}, u32[]{:S(2)}, u32[]{:S(2)}) collective-permute-start(bf16[96,2816]{1,0:T(8,128)(2,1)S(1)} %add_images.1), channel_id=1, source_target_pairs={{0,32},{16,48},{32,64},{48,80},{64,96},{80,112},{96,128},{112,144}... | collective-permute-start | bytes 1622024 | tf_op jit(solution)/shard_map/ppermute | solution.py:347
  73.1 3.6 %second_pull.1 = (bf16[8,32,512]{2,1,0:T(8,128)(2,1)S(1)}, bf16[32,128]{1,0:T(8,128)(2,1)S(1)}) custom-call(bf16[32,640]{1,0:T(8,128)(2,1)S(1)} %collective-permute-done.3.images_ref, f32[32,256]{1,0:T(8,128)S(1)} %get-tuple-element.55.lift_ref, bf16[256,2304]{1,0:T(8,128)(2,1)S(1)} %get-tuple-element.56.kernel_ref, f32[1,256]{1,0:T(1,128)S(1)} %get-tuple-element.57.head_ref), custom_call_target="tpu_custom_call" | custom-call | tf_op jit(solution)/shard_map/second_pull/pallas_call | solution.py:333
  76.7 10.0 %all_to_all.17.pulls_ref = bf16[8,32,512]{2,1,0:T(8,128)(2,1)S(1)} all-to-all(bf16[8,32,512]{2,1,0:T(8,128)(2,1)S(1)} %get-tuple-element.58), channel_id=1, replica_groups={{0,1,2,3,4,5,6,7},{8,9,10,11,12,13,14,15},{16,17,18,19,20,21,22,23},{24..., dimensions={0} | all-to-all | bytes 524288 | tf_op jit(solution)/shard_map/all_to_all | solution.py:357
  86.8 13.8 %collective-permute-done.4.part_b = bf16[96,2816]{1,0:T(8,128)(2,1)S(1)} collective-permute-done((bf16[96,2816]{1,0:T(8,128)(2,1)S(1)}, bf16[96,2816]{1,0:T(8,128)(2,1)S(1)}, u32[]{:S(2)}, u32[]{:S(2)}) %collective-permute-start.4) | collective-permute-done | bytes 540704 | tf_op jit(solution)/shard_map/ppermute | solution.py:347
  100.6 2.9 %collective-permute-start.5 = (bf16[32,640]{1,0:T(8,128)(2,1)S(1)}, bf16[32,640]{1,0:T(8,128)(2,1)S(1)}, u32[]{:S(2)}, u32[]{:S(2)}) collective-permute-start(bf16[32,640]{1,0:T(8,128)(2,1)S(1)} %sum_second.1), channel_id=1, source_target_pairs={{0,16},{16,32},{32,48},{48,64},{64,80},{80,96},{96,112},{112,128},... | collective-permute-start | bytes 122888 | tf_op jit(solution)/shard_map/ppermute | solution.py:347
  103.5 4.7 %moved_first.1 = (f32[32,256]{1,0:T(8,128)S(1)}, f32[256,2304]{1,0:T(8,128)S(1)}, f32[1,256]{1,0:T(1,128)S(1)}) custom-call(bf16[160,2304]{1,0:T(8,128)(2,1)S(1)} %collective-permute-done.1.part_a, bf16[96,2816]{1,0:T(8,128)(2,1)S(1)} %collective-permute-done.4.part_b), custom_call_target="tpu_custom_call" | custom-call | tf_op jit(solution)/shard_map/moved_first/pallas_call | solution.py:333
  108.2 2.5 %collective-permute-done.5.own_ref = bf16[32,640]{1,0:T(8,128)(2,1)S(1)} collective-permute-done((bf16[32,640]{1,0:T(8,128)(2,1)S(1)}, bf16[32,640]{1,0:T(8,128)(2,1)S(1)}, u32[]{:S(2)}, u32[]{:S(2)}) %collective-permute-start.5) | collective-permute-done | bytes 40992 | tf_op jit(solution)/shard_map/ppermute | solution.py:347
  110.7 1.9 %collective-permute-start.6 = (bf16[32,640]{1,0:T(8,128)(2,1)S(1)}, bf16[32,640]{1,0:T(8,128)(2,1)S(1)}, u32[]{:S(2)}, u32[]{:S(2)}) collective-permute-start(bf16[32,640]{1,0:T(8,128)(2,1)S(1)} %collective-permute-done.5.own_ref), channel_id=1, source_target_pairs={{0,8},{1,9},{2,10},{3,11},{4,12},{5,13},{6,14},{7,15},{8,0},{9,1},... | collective-permute-start | bytes 122888 | tf_op jit(solution)/shard_map/ppermute | solution.py:351
  112.6 6.1 %moved_second.1 = (f32[32,256]{1,0:T(8,128)}, f32[256,2304]{1,0:T(8,128)}, f32[1,256]{1,0:T(1,128)}) custom-call(bf16[96,2816]{1,0:T(8,128)(2,1)S(1)} %collective-permute-done.4.part_b, f32[32,256]{1,0:T(8,128)S(1)} %get-tuple-element.65.lift_ref, f32[256,2304]{1,0:T(8,128)S(1)} %get-tuple-element.66.kernel_ref, f32[1,256]{1,0:T(1,128)S(1)} %get-tuple-element.67.head_ref), custom_call_target="tpu_custom_call" | custom-call | tf_op jit(solution)/shard_map/moved_second/pallas_call | solution.py:333
  118.8 2.1 %generator_last.1 = (f32[256,128]{1,0:T(8,128)}, f32[32,256]{1,0:T(8,128)}, f32[32,32]{1,0:T(8,128)}, f32[2,1]{1,0:T(2,128)S(1)}) custom-call(s32[1]{0:T(128)} %bitcast.1.place_ref, bf16[32,640]{1,0:T(8,128)(2,1)S(1)} %collective-permute-done.5.own_ref, bf16[32,640]{1,0:T(8,128)(2,1)S(1)} %collective-permute-done.6.other_ref, ...), custom_call_target="tpu_custom_call" | custom-call | tf_op jit(solution)/shard_map/generator_last/pallas_call | solution.py:448
  (22 shorter events, 0.8 us)
Async XLA Ops:
  0.6 16.8 %collective-permute-start = (bf16[64,128]{1,0:T(8,128)(2,1)}, bf16[64,128]{1,0:T(8,128)(2,1)S(1)}, u32[]{:S(2)}, u32[]{:S(2)}) collective-permute-start(bf16[64,128]{1,0:T(8,128)(2,1)} %bitcast.32), channel_id=1, source_target_pairs={{0,8},{1,9},{2,10},{3,11},{4,12},{5,13},{6,14},{7,15},{8,0},{9,1},... | collective-permute-start | bytes 49160 | tf_op jit(solution)/shard_map/ppermute | solution.py:351
  7.4 44.2 %collective-permute-start.1 = (bf16[160,2304]{1,0:T(8,128)(2,1)}, bf16[160,2304]{1,0:T(8,128)(2,1)S(1)}, u32[]{:S(2)}, u32[]{:S(2)}) collective-permute-start(bf16[160,2304]{1,0:T(8,128)(2,1)} %get-tuple-element.50), channel_id=1, source_target_pairs={{0,32},{16,48},{32,64},{48,80},{64,96},{80,112},{96,128},{112,144}... | collective-permute-start | bytes 2211848 | tf_op jit(solution)/shard_map/ppermute | solution.py:347
  17.4 0.7 copy-start.6
  18.1 10.3 %copy-start.1 = (f32[256,128]{1,0:T(8,128)S(1)}, f32[256,128]{1,0:T(8,128)}, u32[]{:S(2)}) copy-start(f32[256,128]{1,0:T(8,128)} %get-tuple-element.44.first_ref) | copy-start | bytes 393220
  18.1 10.3 %copy-start.2 = (f32[32,256]{1,0:T(8,128)S(1)}, f32[32,256]{1,0:T(8,128)}, u32[]{:S(2)}) copy-start(f32[32,256]{1,0:T(8,128)} %get-tuple-element.45.second_ref) | copy-start | bytes 98308
  18.1 10.3 %copy-start.3 = (bf16[4,32,64]{2,1,0:T(8,128)(2,1)S(1)}, bf16[4,32,64]{2,1,0:T(8,128)(2,1)}, u32[]{:S(2)}) copy-start(bf16[4,32,64]{2,1,0:T(8,128)(2,1)} %get-tuple-element.46.pool_ref) | copy-start | bytes 49156
  18.1 10.3 %copy-start.4 = (s32[1,1,2,1]{2,3,1,0:T(1,128)S(1)}, s32[1,1,2,1]{2,3,1,0:T(1,128)}, u32[]{:S(2)}) copy-start(s32[1,1,2,1]{2,3,1,0:T(1,128)} %param.9) | copy-start | bytes 28
  18.1 11.6 %copy-start = (f32[1,1,256,2304]{3,2,1,0:T(8,128)S(1)}, f32[1,1,256,2304]{3,2,1,0:T(8,128)}, u32[]{:S(2)}) copy-start(f32[1,1,256,2304]{3,2,1,0:T(8,128)} %param.14) | copy-start | bytes 7077892
  18.2 11.6 %copy-start.5 = (f32[32,256]{1,0:T(8,128)S(1)}, f32[32,256]{1,0:T(8,128)}, u32[]{:S(2)}) copy-start(f32[32,256]{1,0:T(8,128)} %get-tuple-element.47.lift_ref) | copy-start | bytes 98308
  18.2 11.6 %copy-start.7 = (f32[1,256]{1,0:T(1,128)S(1)}, f32[1,256]{1,0:T(1,128)}, u32[]{:S(2)}) copy-start(f32[1,256]{1,0:T(1,128)} %get-tuple-element.48.head_ref) | copy-start | bytes 3076
  51.6 5.8 %collective-permute-start.2 = (bf16[32,512]{1,0:T(8,128)(2,1)S(1)}, bf16[32,512]{1,0:T(8,128)(2,1)S(1)}, u32[]{:S(2)}, u32[]{:S(2)}) collective-permute-start(bf16[32,512]{1,0:T(8,128)(2,1)S(1)} %sum_first.1.own_ref), channel_id=1, source_target_pairs={{0,8},{1,9},{2,10},{3,11},{4,12},{5,13},{6,14},{7,15},{8,0},{9,1},... | collective-permute-start | bytes 98312 | tf_op jit(solution)/shard_map/ppermute | solution.py:351
  60.2 10.1 %collective-permute-start.3 = (bf16[32,640]{1,0:T(8,128)(2,1)S(1)}, bf16[32,640]{1,0:T(8,128)(2,1)S(1)}, u32[]{:S(2)}, u32[]{:S(2)}) collective-permute-start(bf16[32,640]{1,0:T(8,128)(2,1)S(1)} %get-tuple-element.52), channel_id=1, source_target_pairs={{0,496},{16,0},{32,16},{48,32},{64,48},{80,64},{96,80},{112,96},{1... | collective-permute-start | bytes 122888 | tf_op jit(solution)/shard_map/ppermute | solution.py:347
  70.4 30.2 %collective-permute-start.4 = (bf16[96,2816]{1,0:T(8,128)(2,1)S(1)}, bf16[96,2816]{1,0:T(8,128)(2,1)S(1)}, u32[]{:S(2)}, u32[]{:S(2)}) collective-permute-start(bf16[96,2816]{1,0:T(8,128)(2,1)S(1)} %add_images.1), channel_id=1, source_target_pairs={{0,32},{16,48},{32,64},{48,80},{64,96},{80,112},{96,128},{112,144}... | collective-permute-start | bytes 1622024 | tf_op jit(solution)/shard_map/ppermute | solution.py:347
  100.6 10.1 %collective-permute-start.5 = (bf16[32,640]{1,0:T(8,128)(2,1)S(1)}, bf16[32,640]{1,0:T(8,128)(2,1)S(1)}, u32[]{:S(2)}, u32[]{:S(2)}) collective-permute-start(bf16[32,640]{1,0:T(8,128)(2,1)S(1)} %sum_second.1), channel_id=1, source_target_pairs={{0,16},{16,32},{32,48},{48,64},{64,80},{80,96},{96,112},{112,128},... | collective-permute-start | bytes 122888 | tf_op jit(solution)/shard_map/ppermute | solution.py:347
  110.7 8.0 %collective-permute-start.6 = (bf16[32,640]{1,0:T(8,128)(2,1)S(1)}, bf16[32,640]{1,0:T(8,128)(2,1)S(1)}, u32[]{:S(2)}, u32[]{:S(2)}) collective-permute-start(bf16[32,640]{1,0:T(8,128)(2,1)S(1)} %collective-permute-done.5.own_ref), channel_id=1, source_target_pairs={{0,8},{1,9},{2,10},{3,11},{4,12},{5,13},{6,14},{7,15},{8,0},{9,1},... | collective-permute-start | bytes 122888 | tf_op jit(solution)/shard_map/ppermute | solution.py:351

commit v6 on v5

--- a/solution.py
+++ b/solution.py
@@ -273,7 +273,7 @@
         kernel_out[:, CH * t : CH * (t + 1)] = kernel_of(t).astype(f32) - critic_rate * dot(z_turned, patch_ref[t])
 
 
-def moved_second_kernel(part_b, lift_ref, kernel_ref, head_ref, lift_out, kernel_out, head_out, patch_ref, half_ref):
+def moved_second_kernel(part_b, lift_ref, kernel_ref, head_ref, lift_out, kernel_out, head_out, patch_ref, half_ref, new_ref, sems):
     for t in range(TAPS):
         half_ref[t] = kernel_ref[:, CH * t : CH * (t + 1)].astype(bf16)
     lift = lift_ref[...]
@@ -285,9 +285,14 @@
     lift_out[...] = lift - critic_rate * dot(images[:, :ROWS], pre_grad)
     head_out[...] = head - critic_rate * head_grad
     z_turned = jnp.transpose(z_grad).astype(bf16)
+    copies = []
     for t in range(TAPS):
         cols = slice(CH * t, CH * (t + 1))
-        kernel_out[:, cols] = kernel_ref[:, cols] - critic_rate * dot(z_turned, patch_ref[t])
+        new_ref[t] = kernel_ref[:, cols] - critic_rate * dot(z_turned, patch_ref[t])
+        copies.append(pltpu.make_async_copy(new_ref.at[t], kernel_out.at[:, cols], sems.at[t]))
+        copies[t].start()
+    for copy in copies:
+        copy.wait()
 
 
 def generator_step(total, latents, first, second):
@@ -318,7 +323,7 @@
         own = own + jnp.where(place_ref[0] == j, total[:, C * j : C * (j + 1)], 0.0)
     own_out[...] = own
     scores_out[0, 0] = jnp.max(score_ref[...])
-    scores_out[1, 0] = jnp.sum(own_ref[:, FAKE:].astype(f32)[:1])
+    scores_out[0, 1] = jnp.sum(own_ref[:, FAKE:].astype(f32)[:1])
 
 
 def vmem(*_):
@@ -403,8 +408,8 @@
         work=FIRST_WORK,
     )
     (partial,) = call(sum_kernel, "sum_first", [((C, FAKE), bf16)], (swap(copies),))
-    partial, moved_a = together(partial, moved_a)
     other = across(partial)
+    other, moved_a = together(other, moved_a)
     own_images, first_1, second_1 = call(
         middle_kernel,
         "generator_step",
@@ -426,7 +431,6 @@
         (PATCHES,),
     )
     (partial,) = call(scored_sum_kernel, "sum_second", [((C, WIDE), bf16)], (swap(copies), score_1))
-    partial, moved_b = together(partial, moved_b)
     same = shifted(partial, 1)
 
     moved_lift, moved_kernel, moved_head = call(
@@ -438,13 +442,15 @@
     )
     moved_lift, same = together(moved_lift, same)
     cross = across(same)
-    lift_2, kernel_2, head_2 = call(
+    lift_2, kernel_2, head_2 = pl.pallas_call(
         moved_second_kernel,
-        "moved_second",
-        [((C, CH), f32), ((CH, KW), f32), ((1, CH), f32)],
-        (moved_b, moved_lift, moved_kernel, moved_head),
-        (PATCHES, HALVES),
-    )
+        name="moved_second",
+        out_shape=[jax.ShapeDtypeStruct(x, f32) for x in ((C, CH), (CH, KW), (1, CH))],
+        in_specs=[vmem()] * 4,
+        out_specs=[vmem(), pl.BlockSpec(memory_space=pltpu.HBM), vmem()],
+        scratch_shapes=[PATCHES, HALVES, pltpu.VMEM((TAPS, CH, CH), f32), pltpu.SemaphoreType.DMA((TAPS,))],
+        compiler_params=pltpu.CompilerParams(vmem_limit_bytes=24 * 1024 * 1024),
+    )(moved_b, moved_lift, moved_kernel, moved_head)
     first_2, second_2, own_grad, scores = pl.pallas_call(
         last_kernel,
         name="generator_last",
@@ -452,7 +458,7 @@
             jax.ShapeDtypeStruct((CH, 128), f32),
             jax.ShapeDtypeStruct((C, CH), f32),
             jax.ShapeDtypeStruct((C, C), f32),
-            jax.ShapeDtypeStruct((ROUNDS, 1), f32),
+            jax.ShapeDtypeStruct((1, ROUNDS), f32),
         ],
         in_specs=[smem()] + [vmem()] * 6,
         out_specs=[vmem()] * 3 + [smem()],
@@ -465,7 +471,7 @@
         first_2[None],
         second_2[None],
         own_grad[None],
-        scores[None, None],
+        scores.reshape(1, 1, ROUNDS, 1),
     )
 
 

time: 122 us -> 113 us (0.926)
  waiting for transfers between devices: 28.9 us -> 17.4 us
  starting transfers between devices: 32.2 us -> 35.4 us
    ppermute x4, waiting for transfers between devices: 25 us -> 12 us  [shifted(): lax.ppermute(value, 'loop', [(s, (s + steps) % count) for s in range(coun...]
    pallas_call x0 -> x1, Pallas kernels: none -> 6.25 us  [per_device(): pl.pallas_call(moved_second_kernel, name='moved_second', out_shape=[jax.S...]
    pallas_call x10 -> x9, Pallas kernels: 23.5 us -> 17.4 us  [call(): pl.pallas_call(kernel, name=name, out_shape=[jax.ShapeDtypeStruct(s, d) f...]
    ppermute x4, starting transfers between devices: 24.1 us -> 26.7 us  [shifted(): lax.ppermute(value, 'loop', [(s, (s + steps) % count) for s in range(coun...]
    ppermute x3, waiting for transfers between devices: 3.89 us -> 5.39 us  [across(): return lax.ppermute(value, 'grp', [(m, m ^ 8) for m in range(N_GRP)])]
  transfers between devices with their start and end apart: 7 -> 7, of which waited for: 5 -> 3; matrix products, arithmetic and copies ran while one was open for 0% -> 0% of each run, Pallas kernels for 19% -> 21%
where the time goes in v6:
time: 113 us
  starting transfers between devices  35.4 us (31%)
  blocking collectives  30.2 us (27%)
  Pallas kernels  28.2 us (25%)
  waiting for transfers between devices  17.4 us (15%)
    all_to_all x3, blocking collectives, swap(): lax.all_to_all(copies, ('loop', 'grp'), 0, 0, axis_index_groups=groups)  30.2 us
    ppermute x4, starting transfers between devices, shifted(): lax.ppermute(value, 'loop', [(s, (s + steps) % count) for s in range(coun...  26.7 us
    pallas_call x9, Pallas kernels, call(): pl.pallas_call(kernel, name=name, out_shape=[jax.ShapeDtypeStruct(s, d) f...  17.4 us
    ppermute x4, waiting for transfers between devices, shifted(): lax.ppermute(value, 'loop', [(s, (s + steps) % count) for s in range(coun...  12 us
    ppermute x3, starting transfers between devices, across(): return lax.ppermute(value, 'grp', [(m, m ^ 8) for m in range(N_GRP)])  8.67 us
    pallas_call x1, Pallas kernels, per_device(): pl.pallas_call(moved_second_kernel, name='moved_second', out_shape=[jax.S...  6.25 us
    ppermute x3, waiting for transfers between devices, across(): return lax.ppermute(value, 'grp', [(m, m ^ 8) for m in range(N_GRP)])  5.39 us
    pallas_call x1, Pallas kernels, per_device(): pl.pallas_call(stage_kernel, name='stage', out_shape=[jax.ShapeDtypeStruc...  2.45 us
  transfers between devices with their start and end apart: 7, of which 3 were waited for; matrix products, arithmetic and copies ran while one was open for 0% of the time, Pallas kernels for 21%

profile of v6, /device:TPU:6, one launch (start us, length us, event | category | flops | bytes accessed | tf_op | source)
XLA Modules:
  0.0 112.9 jit_solution(8126564300104186027)
XLA Ops:
  0.6 4.3 %collective-permute-start = (bf16[64,128]{1,0:T(8,128)(2,1)}, bf16[64,128]{1,0:T(8,128)(2,1)S(1)}, u32[]{:S(2)}, u32[]{:S(2)}) collective-permute-start(bf16[64,128]{1,0:T(8,128)(2,1)} %bitcast.32), channel_id=1, source_target_pairs={{0,8},{1,9},{2,10},{3,11},{4,12},{5,13},{6,14},{7,15},{8,0},{9,1},... | collective-permute-start | bytes 49160 | tf_op jit(solution)/shard_map/ppermute | solution.py:356
  4.9 2.4 %stage.1 = (bf16[160,2304]{1,0:T(8,128)(2,1)}, f32[256,128]{1,0:T(8,128)}, f32[32,256]{1,0:T(8,128)}, bf16[4,32,64]{2,1,0:T(8,128)(2,1)}, f32[32,256]{1,0:T(8,12...) custom-call(f32[256,2304]{1,0:T(8,128)} %bitcast.24, f32[256,128]{1,0:T(8,128)} %bitcast.28, f32[32,256]{1,0:T(8,128)} %bitcast.29, ...), custom_call_target="tpu_custom_call" | custom-call | tf_op jit(solution)/shard_map/stage/pallas_call | solution.py:385
  7.4 10.0 %collective-permute-start.2 = (bf16[160,2304]{1,0:T(8,128)(2,1)}, bf16[160,2304]{1,0:T(8,128)(2,1)S(1)}, u32[]{:S(2)}, u32[]{:S(2)}) collective-permute-start(bf16[160,2304]{1,0:T(8,128)(2,1)} %get-tuple-element.48), channel_id=1, source_target_pairs={{0,32},{16,48},{32,64},{48,80},{64,96},{80,112},{96,128},{112,144}... | collective-permute-start | bytes 2211848 | tf_op jit(solution)/shard_map/ppermute | solution.py:352
  17.4 0.7 copy-done.6
  18.1 0.0 copy-start
  18.2 10.2 %all_to_all.15.noise_ref = bf16[8,128,128]{2,1,0:T(8,128)(2,1)S(1)} all-to-all(bf16[8,128,128]{2,1,0:T(8,128)(2,1)S(1)} %noise_copies.1), channel_id=1, replica_groups={{0,1,2,3,4,5,6,7},{8,9,10,11,12,13,14,15},{16,17,18,19,20,21,22,23},{24..., dimensions={0} | all-to-all | bytes 524288 | tf_op jit(solution)/shard_map/all_to_all | solution.py:362
  28.4 1.3 %make_fakes.1.images_ref = bf16[32,640]{1,0:T(8,128)(2,1)S(1)} custom-call(s32[2]{0:T(128)S(1)} %bitcast.26, bf16[8,128,128]{2,1,0:T(8,128)(2,1)S(1)} %all_to_all.15.noise_ref, f32[256,128]{1,0:T(8,128)S(1)} %copy-done.1, f32[32,256]{1,0:T(8,128)S(1)} %copy-done.2, bf16[4,32,64]{2,1,0:T(8,128)(2,1)S(1)} %copy-done.3), custom_call_target="tpu_custom_call" | custom-call | tf_op jit(solution)/shard_map/make_fakes/pallas_call | solution.py:338
  29.8 4.8 %first_step.1 = (bf16[8,32,512]{2,1,0:T(8,128)(2,1)S(1)}, f32[32,256]{1,0:T(8,128)S(1)}, bf16[256,2304]{1,0:T(8,128)(2,1)S(1)}, f32[1,256]{1,0:T(1,128)S(1)}, f3...) custom-call(bf16[32,640]{1,0:T(8,128)(2,1)S(1)} %make_fakes.1.images_ref, f32[32,256]{1,0:T(8,128)S(1)} %copy-done.5, ...), custom_call_target="tpu_custom_call" | custom-call | flops 2000000000 | tf_op jit(solution)/shard_map/first_step/pallas_call | solution.py:338
  34.6 9.9 %all_to_all.16.pulls_ref = bf16[8,32,512]{2,1,0:T(8,128)(2,1)S(1)} all-to-all(bf16[8,32,512]{2,1,0:T(8,128)(2,1)S(1)} %get-tuple-element.47), channel_id=1, replica_groups={{0,1,2,3,4,5,6,7},{8,9,10,11,12,13,14,15},{16,17,18,19,20,21,22,23},{24..., dimensions={0} | all-to-all | bytes 524288 | tf_op jit(solution)/shard_map/all_to_all | solution.py:362
  44.6 2.5 %collective-permute-start.1 = (bf16[32,512]{1,0:T(8,128)(2,1)S(1)}, bf16[32,512]{1,0:T(8,128)(2,1)S(1)}, u32[]{:S(2)}, u32[]{:S(2)}) collective-permute-start(bf16[32,512]{1,0:T(8,128)(2,1)S(1)} %sum_first.1.own_ref), channel_id=1, source_target_pairs={{0,8},{1,9},{2,10},{3,11},{4,12},{5,13},{6,14},{7,15},{8,0},{9,1},... | collective-permute-start | bytes 98312 | tf_op jit(solution)/shard_map/ppermute | solution.py:356
  47.0 5.4 %collective-permute-done.1.other_ref = bf16[32,512]{1,0:T(8,128)(2,1)S(1)} collective-permute-done((bf16[32,512]{1,0:T(8,128)(2,1)S(1)}, bf16[32,512]{1,0:T(8,128)(2,1)S(1)}, u32[]{:S(2)}, u32[]{:S(2)}) %collective-permute-start.1) | collective-permute-done | bytes 32800 | tf_op jit(solution)/shard_map/ppermute | solution.py:356
  52.4 2.8 %generator_step.1 = (bf16[32,640]{1,0:T(8,128)(2,1)S(1)}, f32[256,128]{1,0:T(8,128)S(1)}, f32[32,256]{1,0:T(8,128)S(1)}) custom-call(s32[2]{0:T(128)S(1)} %bitcast.27, bf16[32,512]{1,0:T(8,128)(2,1)S(1)} %sum_first.1.own_ref, bf16[32,512]{1,0:T(8,128)(2,1)S(1)} %collective-permute-done.1.other_ref, bf16[8,128,128]{2,1,0:T(8,128)(2,1)S(1)} %all_to_all.15.noise_ref, ...), custom_call_target="tpu_custom_call" | custom-call | tf_op jit(solution)/shard_map/generator_step/pallas_call | solution.py:338
  55.2 8.0 %collective-permute-start.3 = (bf16[32,640]{1,0:T(8,128)(2,1)S(1)}, bf16[32,640]{1,0:T(8,128)(2,1)S(1)}, u32[]{:S(2)}, u32[]{:S(2)}) collective-permute-start(bf16[32,640]{1,0:T(8,128)(2,1)S(1)} %get-tuple-element.50), channel_id=1, source_target_pairs={{0,496},{16,0},{32,16},{48,32},{64,48},{80,64},{96,80},{112,96},{1... | collective-permute-start | bytes 122888 | tf_op jit(solution)/shard_map/ppermute | solution.py:352
  63.2 1.7 %collective-permute-done.3.images_ref = bf16[32,640]{1,0:T(8,128)(2,1)S(1)} collective-permute-done((bf16[32,640]{1,0:T(8,128)(2,1)S(1)}, bf16[32,640]{1,0:T(8,128)(2,1)S(1)}, u32[]{:S(2)}, u32[]{:S(2)}) %collective-permute-start.3) | collective-permute-done | bytes 40992 | tf_op jit(solution)/shard_map/ppermute | solution.py:352
  64.9 0.1 add_images.1
  65.0 1.9 %collective-permute-start.4 = (bf16[96,2816]{1,0:T(8,128)(2,1)S(1)}, bf16[96,2816]{1,0:T(8,128)(2,1)S(1)}, u32[]{:S(2)}, u32[]{:S(2)}) collective-permute-start(bf16[96,2816]{1,0:T(8,128)(2,1)S(1)} %add_images.1), channel_id=1, source_target_pairs={{0,32},{16,48},{32,64},{48,80},{64,96},{80,112},{96,128},{112,144}... | collective-permute-start | bytes 1622024 | tf_op jit(solution)/shard_map/ppermute | solution.py:352
  66.9 3.6 %second_pull.1 = (bf16[8,32,512]{2,1,0:T(8,128)(2,1)S(1)}, bf16[32,128]{1,0:T(8,128)(2,1)S(1)}) custom-call(bf16[32,640]{1,0:T(8,128)(2,1)S(1)} %collective-permute-done.3.images_ref, f32[32,256]{1,0:T(8,128)S(1)} %get-tuple-element.56.lift_ref, bf16[256,2304]{1,0:T(8,128)(2,1)S(1)} %get-tuple-element.57.kernel_ref, f32[1,256]{1,0:T(1,128)S(1)} %get-tuple-element.58.head_ref), custom_call_target="tpu_custom_call" | custom-call | tf_op jit(solution)/shard_map/second_pull/pallas_call | solution.py:338
  70.5 10.0 %all_to_all.17.pulls_ref = bf16[8,32,512]{2,1,0:T(8,128)(2,1)S(1)} all-to-all(bf16[8,32,512]{2,1,0:T(8,128)(2,1)S(1)} %get-tuple-element.59), channel_id=1, replica_groups={{0,1,2,3,4,5,6,7},{8,9,10,11,12,13,14,15},{16,17,18,19,20,21,22,23},{24..., dimensions={0} | all-to-all | bytes 524288 | tf_op jit(solution)/shard_map/all_to_all | solution.py:362
  80.6 6.8 %collective-permute-start.5 = (bf16[32,640]{1,0:T(8,128)(2,1)S(1)}, bf16[32,640]{1,0:T(8,128)(2,1)S(1)}, u32[]{:S(2)}, u32[]{:S(2)}) collective-permute-start(bf16[32,640]{1,0:T(8,128)(2,1)S(1)} %sum_second.1), channel_id=1, source_target_pairs={{0,16},{16,32},{32,48},{48,64},{64,80},{80,96},{96,112},{112,128},... | collective-permute-start | bytes 122888 | tf_op jit(solution)/shard_map/ppermute | solution.py:352
  87.4 10.3 %collective-permute-done.4.part_b = bf16[96,2816]{1,0:T(8,128)(2,1)S(1)} collective-permute-done((bf16[96,2816]{1,0:T(8,128)(2,1)S(1)}, bf16[96,2816]{1,0:T(8,128)(2,1)S(1)}, u32[]{:S(2)}, u32[]{:S(2)}) %collective-permute-start.4) | collective-permute-done | bytes 540704 | tf_op jit(solution)/shard_map/ppermute | solution.py:352
  97.7 4.7 %moved_first.1 = (f32[32,256]{1,0:T(8,128)S(1)}, f32[256,2304]{1,0:T(8,128)S(1)}, f32[1,256]{1,0:T(1,128)S(1)}) custom-call(bf16[160,2304]{1,0:T(8,128)(2,1)S(1)} %collective-permute-done.2.part_a, bf16[96,2816]{1,0:T(8,128)(2,1)S(1)} %collective-permute-done.4.part_b), custom_call_target="tpu_custom_call" | custom-call | tf_op jit(solution)/shard_map/moved_first/pallas_call | solution.py:338
  102.4 1.9 %collective-permute-start.6 = (bf16[32,640]{1,0:T(8,128)(2,1)S(1)}, bf16[32,640]{1,0:T(8,128)(2,1)S(1)}, u32[]{:S(2)}, u32[]{:S(2)}) collective-permute-start(bf16[32,640]{1,0:T(8,128)(2,1)S(1)} %collective-permute-done.5.own_ref), channel_id=1, source_target_pairs={{0,8},{1,9},{2,10},{3,11},{4,12},{5,13},{6,14},{7,15},{8,0},{9,1},... | collective-permute-start | bytes 122888 | tf_op jit(solution)/shard_map/ppermute | solution.py:356
  104.3 6.2 %moved_second.1 = (f32[32,256]{1,0:T(8,128)}, f32[256,2304]{1,0:T(8,128)}, f32[1,256]{1,0:T(1,128)}) custom-call(bf16[96,2816]{1,0:T(8,128)(2,1)S(1)} %collective-permute-done.4.part_b, f32[32,256]{1,0:T(8,128)S(1)} %get-tuple-element.61.lift_ref, f32[256,2304]{1,0:T(8,128)S(1)} %get-tuple-element.62.kernel_ref, f32[1,256]{1,0:T(1,128)S(1)} %get-tuple-element.63.head_ref), custom_call_target="tpu_custom_call" | custom-call | tf_op jit(solution)/shard_map/moved_second/pallas_call | solution.py:445
  110.6 2.2 %generator_last.1 = (f32[256,128]{1,0:T(8,128)}, f32[32,256]{1,0:T(8,128)}, f32[32,32]{1,0:T(8,128)}, f32[1,2]{1,0:T(1,128)}) custom-call(s32[1]{0:T(128)} %bitcast.1.place_ref, bf16[32,640]{1,0:T(8,128)(2,1)S(1)} %collective-permute-done.5.own_ref, bf16[32,640]{1,0:T(8,128)(2,1)S(1)} %collective-permute-done.6.other_ref, ...), custom_call_target="tpu_custom_call" | custom-call | tf_op jit(solution)/shard_map/generator_last/pallas_call | solution.py:454
  (21 shorter events, 0.1 us)
Async XLA Ops:
  0.6 16.8 %collective-permute-start = (bf16[64,128]{1,0:T(8,128)(2,1)}, bf16[64,128]{1,0:T(8,128)(2,1)S(1)}, u32[]{:S(2)}, u32[]{:S(2)}) collective-permute-start(bf16[64,128]{1,0:T(8,128)(2,1)} %bitcast.32), channel_id=1, source_target_pairs={{0,8},{1,9},{2,10},{3,11},{4,12},{5,13},{6,14},{7,15},{8,0},{9,1},... | collective-permute-start | bytes 49160 | tf_op jit(solution)/shard_map/ppermute | solution.py:356
  7.4 45.1 %collective-permute-start.2 = (bf16[160,2304]{1,0:T(8,128)(2,1)}, bf16[160,2304]{1,0:T(8,128)(2,1)S(1)}, u32[]{:S(2)}, u32[]{:S(2)}) collective-permute-start(bf16[160,2304]{1,0:T(8,128)(2,1)} %get-tuple-element.48), channel_id=1, source_target_pairs={{0,32},{16,48},{32,64},{48,80},{64,96},{80,112},{96,128},{112,144}... | collective-permute-start | bytes 2211848 | tf_op jit(solution)/shard_map/ppermute | solution.py:352
  17.4 0.7 copy-start.6
  18.1 10.3 %copy-start.1 = (f32[256,128]{1,0:T(8,128)S(1)}, f32[256,128]{1,0:T(8,128)}, u32[]{:S(2)}) copy-start(f32[256,128]{1,0:T(8,128)} %get-tuple-element.42.first_ref) | copy-start | bytes 393220
  18.1 10.3 %copy-start.2 = (f32[32,256]{1,0:T(8,128)S(1)}, f32[32,256]{1,0:T(8,128)}, u32[]{:S(2)}) copy-start(f32[32,256]{1,0:T(8,128)} %get-tuple-element.43.second_ref) | copy-start | bytes 98308
  18.1 10.3 %copy-start.3 = (bf16[4,32,64]{2,1,0:T(8,128)(2,1)S(1)}, bf16[4,32,64]{2,1,0:T(8,128)(2,1)}, u32[]{:S(2)}) copy-start(bf16[4,32,64]{2,1,0:T(8,128)(2,1)} %get-tuple-element.44.pool_ref) | copy-start | bytes 49156
  18.1 10.3 %copy-start.4 = (s32[1,1,2,1]{2,3,1,0:T(1,128)S(1)}, s32[1,1,2,1]{2,3,1,0:T(1,128)}, u32[]{:S(2)}) copy-start(s32[1,1,2,1]{2,3,1,0:T(1,128)} %param.9) | copy-start | bytes 28
  18.1 11.6 %copy-start = (f32[1,1,256,2304]{3,2,1,0:T(8,128)S(1)}, f32[1,1,256,2304]{3,2,1,0:T(8,128)}, u32[]{:S(2)}) copy-start(f32[1,1,256,2304]{3,2,1,0:T(8,128)} %param.14) | copy-start | bytes 7077892
  18.2 11.6 %copy-start.5 = (f32[32,256]{1,0:T(8,128)S(1)}, f32[32,256]{1,0:T(8,128)}, u32[]{:S(2)}) copy-start(f32[32,256]{1,0:T(8,128)} %get-tuple-element.45.lift_ref) | copy-start | bytes 98308
  18.2 11.6 %copy-start.7 = (f32[1,256]{1,0:T(1,128)S(1)}, f32[1,256]{1,0:T(1,128)}, u32[]{:S(2)}) copy-start(f32[1,256]{1,0:T(1,128)} %get-tuple-element.46.head_ref) | copy-start | bytes 3076
  44.6 7.9 %collective-permute-start.1 = (bf16[32,512]{1,0:T(8,128)(2,1)S(1)}, bf16[32,512]{1,0:T(8,128)(2,1)S(1)}, u32[]{:S(2)}, u32[]{:S(2)}) collective-permute-start(bf16[32,512]{1,0:T(8,128)(2,1)S(1)} %sum_first.1.own_ref), channel_id=1, source_target_pairs={{0,8},{1,9},{2,10},{3,11},{4,12},{5,13},{6,14},{7,15},{8,0},{9,1},... | collective-permute-start | bytes 98312 | tf_op jit(solution)/shard_map/ppermute | solution.py:356
  55.2 9.7 %collective-permute-start.3 = (bf16[32,640]{1,0:T(8,128)(2,1)S(1)}, bf16[32,640]{1,0:T(8,128)(2,1)S(1)}, u32[]{:S(2)}, u32[]{:S(2)}) collective-permute-start(bf16[32,640]{1,0:T(8,128)(2,1)S(1)} %get-tuple-element.50), channel_id=1, source_target_pairs={{0,496},{16,0},{32,16},{48,32},{64,48},{80,64},{96,80},{112,96},{1... | collective-permute-start | bytes 122888 | tf_op jit(solution)/shard_map/ppermute | solution.py:352
  65.0 32.7 %collective-permute-start.4 = (bf16[96,2816]{1,0:T(8,128)(2,1)S(1)}, bf16[96,2816]{1,0:T(8,128)(2,1)S(1)}, u32[]{:S(2)}, u32[]{:S(2)}) collective-permute-start(bf16[96,2816]{1,0:T(8,128)(2,1)S(1)} %add_images.1), channel_id=1, source_target_pairs={{0,32},{16,48},{32,64},{48,80},{64,96},{80,112},{96,128},{112,144}... | collective-permute-start | bytes 1622024 | tf_op jit(solution)/shard_map/ppermute | solution.py:352
  80.6 21.7 %collective-permute-start.5 = (bf16[32,640]{1,0:T(8,128)(2,1)S(1)}, bf16[32,640]{1,0:T(8,128)(2,1)S(1)}, u32[]{:S(2)}, u32[]{:S(2)}) collective-permute-start(bf16[32,640]{1,0:T(8,128)(2,1)S(1)} %sum_second.1), channel_id=1, source_target_pairs={{0,16},{16,32},{32,48},{48,64},{64,80},{80,96},{96,112},{112,128},... | collective-permute-start | bytes 122888 | tf_op jit(solution)/shard_map/ppermute | solution.py:352
  102.4 8.2 %collective-permute-start.6 = (bf16[32,640]{1,0:T(8,128)(2,1)S(1)}, bf16[32,640]{1,0:T(8,128)(2,1)S(1)}, u32[]{:S(2)}, u32[]{:S(2)}) collective-permute-start(bf16[32,640]{1,0:T(8,128)(2,1)S(1)} %collective-permute-done.5.own_ref), channel_id=1, source_target_pairs={{0,8},{1,9},{2,10},{3,11},{4,12},{5,13},{6,14},{7,15},{8,0},{9,1},... | collective-permute-start | bytes 122888 | tf_op jit(solution)/shard_map/ppermute | solution.py:356

commit v7 on v6

--- a/solution.py
+++ b/solution.py
@@ -86,21 +86,21 @@
     gate = sigmoid(pre)
     lifted = (pre * gate).astype(bf16).astype(f32)
     slope = gate * (1.0 + pre * (1.0 - gate))
-    z = None
     for b in range(3):
         dx = b - 1
-        across = lifted
+        side = lifted
         if dx:
-            across = jnp.where(reads_x[dx], pltpu.roll(lifted, (-dx) % ROWS, 0), 0.0)
-        for a in range(3):
-            dy = a - 1
-            tap = move_rows(across, 8 * dy)
-            if dy:
-                tap = jnp.where(reads_y[dy], tap, 0.0)
-            tap = tap.astype(bf16)
-            patch_ref[3 * a + b] = tap
-            part = dot(tap, kernel_of(3 * a + b), NT)
-            z = part if z is None else z + part
+            side = jnp.where(reads_x[dx], pltpu.roll(lifted, (-dx) % ROWS, 0), 0.0)
+        patch_ref[b] = side.astype(bf16)
+    z = None
+    for a in (1, 0, 2):
+        dy = a - 1
+        part = dot(patch_ref[0], kernel_of(3 * a), NT)
+        part = part + dot(patch_ref[1], kernel_of(3 * a + 1), NT)
+        part = part + dot(patch_ref[2], kernel_of(3 * a + 2), NT)
+        if dy:
+            part = jnp.where(reads_y[dy], move_rows(part, 8 * dy), 0.0)
+        z = part if z is None else z + part
     gate = sigmoid(z)
     hidden = z * gate
     weight = jnp.where(row_ids(CH) < FAKE, 1.0 / 64.0, -1.0 / 8.0)
@@ -110,23 +110,35 @@
     return slope, z_grad, head_grad, real_score
 
 
-def lift_pullback(slope, z_grad, kernel_of):
-    reads_x, reads_y = masks()
+def row_parts(z_grad):
+    _, reads_y = masks()
+    parts = []
+    for a in range(3):
+        dy = a - 1
+        part = z_grad
+        if dy:
+            part = move_rows(jnp.where(reads_y[dy], part, 0.0), -8 * dy)
+        parts.append(part)
+    return parts
+
+
+def lift_pullback(slope, parts, kernel_of):
+    reads_x, _ = masks()
+    halves = [part.astype(bf16) for part in parts]
     total = None
     for b in range(3):
         dx = b - 1
-        across = None
-        for a in range(3):
-            dy = a - 1
-            tap = dot(z_grad, kernel_of(3 * a + b))
-            if dy:
-                tap = jnp.where(reads_y[dy], tap, 0.0)
-            tap = move_rows(tap, -8 * dy)
-            across = tap if across is None else across + tap
+        side = dot(halves[0], kernel_of(b))
+        side = side + dot(halves[1], kernel_of(3 + b))
+        side = side + dot(halves[2], kernel_of(6 + b))
         if dx:
-            across = pltpu.roll(jnp.where(reads_x[dx], across, 0.0), dx % ROWS, 0)
-        total = across if total is None else total + across
+            side = pltpu.roll(jnp.where(reads_x[dx], side, 0.0), dx % ROWS, 0)
+        total = side if total is None else total + side
     return (total * slope).astype(bf16)
+
+
+def turned(parts):
+    return [jnp.transpose(part).astype(bf16) for part in parts]
 
 
 def real_image(pool_ref, pick_ref, round_index):
@@ -217,17 +229,17 @@
     lift_half = lift.astype(bf16)
     images = images_ref[...]
     slope, z_grad, head_grad, score = critic_forward(images, lift_half, lambda t: half_ref[t], head, patch_ref)
-    z_half = z_grad.astype(bf16)
-    pre_grad = lift_pullback(slope, z_half, lambda t: half_ref[t])
+    parts = row_parts(z_grad)
+    pre_grad = lift_pullback(slope, parts, lambda t: half_ref[t])
     pull = (-8.0 * dot(lift_half, pre_grad, NT)[:, :FAKE]).astype(bf16)
     for j in range(8):
         copies_ref[j] = pull
     lift_out[...] = lift - critic_rate * dot(images[:, :ROWS], pre_grad)
     head_out[...] = head - critic_rate * head_grad
-    z_turned = jnp.transpose(z_grad).astype(bf16)
+    z_turned = turned(parts)
     for t in range(TAPS):
         cols = slice(CH * t, CH * (t + 1))
-        kernel_out[:, cols] = (kernel_ref[:, cols] - critic_rate * dot(z_turned, patch_ref[t])).astype(bf16)
+        kernel_out[:, cols] = (kernel_ref[:, cols] - critic_rate * dot(z_turned[t // 3], patch_ref[t % 3])).astype(bf16)
         rest_out[:, cols] = half_ref[t, PART_A:, :]
     rest_out[:C, KW:] = images[:, :FAKE]
     rest_out[C : 2 * C, KW:] = jnp.zeros((C, EXTRA), bf16)
@@ -242,7 +254,8 @@
     lift_half = lift_ref[...].astype(bf16)
     kernel_of = lambda t: kernel_ref[:, CH * t : CH * (t + 1)]
     slope, z_grad, _, score = critic_forward(images_ref[...], lift_half, kernel_of, head_ref[...], patch_ref)
-    pre_grad = lift_pullback(slope, z_grad.astype(bf16), kernel_of)
+    parts = row_parts(z_grad)
+    pre_grad = lift_pullback(slope, parts, kernel_of)
     pull = (-8.0 * dot(lift_half, pre_grad, NT)[:, :FAKE]).astype(bf16)
     for j in range(8):
         copies_ref[j] = pull
@@ -265,12 +278,13 @@
     head = jnp.concatenate([lane[:1], lane[16:17]], axis=1)
     kernel_of = lambda t: half_ref[t]
     slope, z_grad, head_grad, _ = critic_forward(images, lift_half, kernel_of, head, patch_ref)
-    pre_grad = lift_pullback(slope, z_grad.astype(bf16), kernel_of)
+    parts = row_parts(z_grad)
+    pre_grad = lift_pullback(slope, parts, kernel_of)
     lift_out[...] = lift_half.astype(f32) - critic_rate * dot(images[:, :ROWS], pre_grad)
     head_out[...] = head - critic_rate * head_grad
-    z_turned = jnp.transpose(z_grad).astype(bf16)
+    z_turned = turned(parts)
     for t in range(TAPS):
-        kernel_out[:, CH * t : CH * (t + 1)] = kernel_of(t).astype(f32) - critic_rate * dot(z_turned, patch_ref[t])
+        kernel_out[:, CH * t : CH * (t + 1)] = kernel_of(t).astype(f32) - critic_rate * dot(z_turned[t // 3], patch_ref[t % 3])
 
 
 def moved_second_kernel(part_b, lift_ref, kernel_ref, head_ref, lift_out, kernel_out, head_out, patch_ref, half_ref, new_ref, sems):
@@ -281,14 +295,15 @@
     images = moved_images(part_b, 1)
     kernel_of = lambda t: half_ref[t]
     slope, z_grad, head_grad, _ = critic_forward(images, lift.astype(bf16), kernel_of, head, patch_ref)
-    pre_grad = lift_pullback(slope, z_grad.astype(bf16), kernel_of)
+    parts = row_parts(z_grad)
+    pre_grad = lift_pullback(slope, parts, kernel_of)
     lift_out[...] = lift - critic_rate * dot(images[:, :ROWS], pre_grad)
     head_out[...] = head - critic_rate * head_grad
-    z_turned = jnp.transpose(z_grad).astype(bf16)
+    z_turned = turned(parts)
     copies = []
     for t in range(TAPS):
         cols = slice(CH * t, CH * (t + 1))
-        new_ref[t] = kernel_ref[:, cols] - critic_rate * dot(z_turned, patch_ref[t])
+        new_ref[t] = kernel_ref[:, cols] - critic_rate * dot(z_turned[t // 3], patch_ref[t % 3])
         copies.append(pltpu.make_async_copy(new_ref.at[t], kernel_out.at[:, cols], sems.at[t]))
         copies[t].start()
     for copy in copies:
@@ -366,7 +381,7 @@
     return lax.optimization_barrier(values)
 
 
-PATCHES = pltpu.VMEM((TAPS, ROWS, CH), bf16)
+PATCHES = pltpu.VMEM((3, ROWS, CH), bf16)
 HALVES = pltpu.VMEM((TAPS, CH, CH), bf16)
 
 

time: 113 us -> 112 us (level)
  Pallas kernels: 28.2 us -> 24.5 us
  waiting for transfers between devices: 17.4 us -> 19 us
    pallas_call x9, Pallas kernels: 17.4 us -> 14.7 us  [call(): pl.pallas_call(kernel, name=name, out_shape=[jax.ShapeDtypeStruct(s, d) f...]
  transfers between devices with their start and end apart: 7 -> 7, of which waited for: 3 -> 3; matrix products, arithmetic and copies ran while one was open for 0% -> 0% of each run, Pallas kernels for 21% -> 18%
where the time goes in v7:
time: 112 us; the launch traced here: 111 us
  starting transfers between devices  35.3 us (32%)
  blocking collectives  30.2 us (27%)
  Pallas kernels  24.5 us (22%)
  waiting for transfers between devices  19 us (17%)
    all_to_all x3, blocking collectives, swap(): lax.all_to_all(copies, ('loop', 'grp'), 0, 0, axis_index_groups=groups)  30.2 us
    ppermute x4, starting transfers between devices, shifted(): lax.ppermute(value, 'loop', [(s, (s + steps) % count) for s in range(coun...  26.5 us
    pallas_call x9, Pallas kernels, call(): pl.pallas_call(kernel, name=name, out_shape=[jax.ShapeDtypeStruct(s, d) f...  14.7 us
    ppermute x4, waiting for transfers between devices, shifted(): lax.ppermute(value, 'loop', [(s, (s + steps) % count) for s in range(coun...  12.8 us
    ppermute x3, starting transfers between devices, across(): return lax.ppermute(value, 'grp', [(m, m ^ 8) for m in range(N_GRP)])  8.84 us
    ppermute x3, waiting for transfers between devices, across(): return lax.ppermute(value, 'grp', [(m, m ^ 8) for m in range(N_GRP)])  6.25 us
    pallas_call x1, Pallas kernels, per_device(): pl.pallas_call(moved_second_kernel, name='moved_second', out_shape=[jax.S...  5.27 us
    pallas_call x1, Pallas kernels, per_device(): pl.pallas_call(stage_kernel, name='stage', out_shape=[jax.ShapeDtypeStruc...  2.45 us
  transfers between devices with their start and end apart: 7, of which 3 were waited for; matrix products, arithmetic and copies ran while one was open for 0% of the time, Pallas kernels for 18%

profile of v7, /device:TPU:6, one launch (start us, length us, event | category | flops | bytes accessed | tf_op | source)
XLA Modules:
  0.0 110.8 jit_solution(13494344323754818638)
XLA Ops:
  0.6 4.3 %collective-permute-start = (bf16[64,128]{1,0:T(8,128)(2,1)}, bf16[64,128]{1,0:T(8,128)(2,1)S(1)}, u32[]{:S(2)}, u32[]{:S(2)}) collective-permute-start(bf16[64,128]{1,0:T(8,128)(2,1)} %bitcast.32), channel_id=1, source_target_pairs={{0,8},{1,9},{2,10},{3,11},{4,12},{5,13},{6,14},{7,15},{8,0},{9,1},... | collective-permute-start | bytes 49160 | tf_op jit(solution)/shard_map/ppermute | solution.py:371
  4.9 2.4 %stage.1 = (bf16[160,2304]{1,0:T(8,128)(2,1)}, f32[256,128]{1,0:T(8,128)}, f32[32,256]{1,0:T(8,128)}, bf16[4,32,64]{2,1,0:T(8,128)(2,1)}, f32[32,256]{1,0:T(8,12...) custom-call(f32[256,2304]{1,0:T(8,128)} %bitcast.24, f32[256,128]{1,0:T(8,128)} %bitcast.28, f32[32,256]{1,0:T(8,128)} %bitcast.29, ...), custom_call_target="tpu_custom_call" | custom-call | tf_op jit(solution)/shard_map/stage/pallas_call | solution.py:400
  7.4 10.0 %collective-permute-start.2 = (bf16[160,2304]{1,0:T(8,128)(2,1)}, bf16[160,2304]{1,0:T(8,128)(2,1)S(1)}, u32[]{:S(2)}, u32[]{:S(2)}) collective-permute-start(bf16[160,2304]{1,0:T(8,128)(2,1)} %get-tuple-element.48), channel_id=1, source_target_pairs={{0,32},{16,48},{32,64},{48,80},{64,96},{80,112},{96,128},{112,144}... | collective-permute-start | bytes 2211848 | tf_op jit(solution)/shard_map/ppermute | solution.py:367
  17.4 0.0 copy-start.6
  17.4 0.7 copy-done.6
  18.2 10.2 %all_to_all.15.noise_ref = bf16[8,128,128]{2,1,0:T(8,128)(2,1)S(1)} all-to-all(bf16[8,128,128]{2,1,0:T(8,128)(2,1)S(1)} %noise_copies.1), channel_id=1, replica_groups={{0,1,2,3,4,5,6,7},{8,9,10,11,12,13,14,15},{16,17,18,19,20,21,22,23},{24..., dimensions={0} | all-to-all | bytes 524288 | tf_op jit(solution)/shard_map/all_to_all | solution.py:377
  28.4 1.3 %make_fakes.1.images_ref = bf16[32,640]{1,0:T(8,128)(2,1)S(1)} custom-call(s32[2]{0:T(128)S(1)} %bitcast.26, bf16[8,128,128]{2,1,0:T(8,128)(2,1)S(1)} %all_to_all.15.noise_ref, f32[256,128]{1,0:T(8,128)S(1)} %copy-done.1, f32[32,256]{1,0:T(8,128)S(1)} %copy-done.2, bf16[4,32,64]{2,1,0:T(8,128)(2,1)S(1)} %copy-done.3), custom_call_target="tpu_custom_call" | custom-call | tf_op jit(solution)/shard_map/make_fakes/pallas_call | solution.py:353
  29.8 4.0 %first_step.1 = (bf16[8,32,512]{2,1,0:T(8,128)(2,1)S(1)}, f32[32,256]{1,0:T(8,128)S(1)}, bf16[256,2304]{1,0:T(8,128)(2,1)S(1)}, f32[1,256]{1,0:T(1,128)S(1)}, f3...) custom-call(bf16[32,640]{1,0:T(8,128)(2,1)S(1)} %make_fakes.1.images_ref, f32[32,256]{1,0:T(8,128)S(1)} %copy-done.5, ...), custom_call_target="tpu_custom_call" | custom-call | flops 2000000000 | tf_op jit(solution)/shard_map/first_step/pallas_call | solution.py:353
  33.8 9.9 %all_to_all.16.pulls_ref = bf16[8,32,512]{2,1,0:T(8,128)(2,1)S(1)} all-to-all(bf16[8,32,512]{2,1,0:T(8,128)(2,1)S(1)} %get-tuple-element.47), channel_id=1, replica_groups={{0,1,2,3,4,5,6,7},{8,9,10,11,12,13,14,15},{16,17,18,19,20,21,22,23},{24..., dimensions={0} | all-to-all | bytes 524288 | tf_op jit(solution)/shard_map/all_to_all | solution.py:377
  43.8 2.5 %collective-permute-start.1 = (bf16[32,512]{1,0:T(8,128)(2,1)S(1)}, bf16[32,512]{1,0:T(8,128)(2,1)S(1)}, u32[]{:S(2)}, u32[]{:S(2)}) collective-permute-start(bf16[32,512]{1,0:T(8,128)(2,1)S(1)} %sum_first.1.own_ref), channel_id=1, source_target_pairs={{0,8},{1,9},{2,10},{3,11},{4,12},{5,13},{6,14},{7,15},{8,0},{9,1},... | collective-permute-start | bytes 98312 | tf_op jit(solution)/shard_map/ppermute | solution.py:371
  46.2 6.2 %collective-permute-done.1.other_ref = bf16[32,512]{1,0:T(8,128)(2,1)S(1)} collective-permute-done((bf16[32,512]{1,0:T(8,128)(2,1)S(1)}, bf16[32,512]{1,0:T(8,128)(2,1)S(1)}, u32[]{:S(2)}, u32[]{:S(2)}) %collective-permute-start.1) | collective-permute-done | bytes 32800 | tf_op jit(solution)/shard_map/ppermute | solution.py:371
  52.5 2.8 %generator_step.1 = (bf16[32,640]{1,0:T(8,128)(2,1)S(1)}, f32[256,128]{1,0:T(8,128)S(1)}, f32[32,256]{1,0:T(8,128)S(1)}) custom-call(s32[2]{0:T(128)S(1)} %bitcast.27, bf16[32,512]{1,0:T(8,128)(2,1)S(1)} %sum_first.1.own_ref, bf16[32,512]{1,0:T(8,128)(2,1)S(1)} %collective-permute-done.1.other_ref, bf16[8,128,128]{2,1,0:T(8,128)(2,1)S(1)} %all_to_all.15.noise_ref, ...), custom_call_target="tpu_custom_call" | custom-call | tf_op jit(solution)/shard_map/generator_step/pallas_call | solution.py:353
  55.3 8.0 %collective-permute-start.3 = (bf16[32,640]{1,0:T(8,128)(2,1)S(1)}, bf16[32,640]{1,0:T(8,128)(2,1)S(1)}, u32[]{:S(2)}, u32[]{:S(2)}) collective-permute-start(bf16[32,640]{1,0:T(8,128)(2,1)S(1)} %get-tuple-element.50), channel_id=1, source_target_pairs={{0,496},{16,0},{32,16},{48,32},{64,48},{80,64},{96,80},{112,96},{1... | collective-permute-start | bytes 122888 | tf_op jit(solution)/shard_map/ppermute | solution.py:367
  63.2 1.7 %collective-permute-done.3.images_ref = bf16[32,640]{1,0:T(8,128)(2,1)S(1)} collective-permute-done((bf16[32,640]{1,0:T(8,128)(2,1)S(1)}, bf16[32,640]{1,0:T(8,128)(2,1)S(1)}, u32[]{:S(2)}, u32[]{:S(2)}) %collective-permute-start.3) | collective-permute-done | bytes 40992 | tf_op jit(solution)/shard_map/ppermute | solution.py:367
  64.9 0.1 add_images.1
  65.0 1.9 %collective-permute-start.4 = (bf16[96,2816]{1,0:T(8,128)(2,1)S(1)}, bf16[96,2816]{1,0:T(8,128)(2,1)S(1)}, u32[]{:S(2)}, u32[]{:S(2)}) collective-permute-start(bf16[96,2816]{1,0:T(8,128)(2,1)S(1)} %add_images.1), channel_id=1, source_target_pairs={{0,32},{16,48},{32,64},{48,80},{64,96},{80,112},{96,128},{112,144}... | collective-permute-start | bytes 1622024 | tf_op jit(solution)/shard_map/ppermute | solution.py:367
  66.9 2.6 %second_pull.1 = (bf16[8,32,512]{2,1,0:T(8,128)(2,1)S(1)}, bf16[32,128]{1,0:T(8,128)(2,1)S(1)}) custom-call(bf16[32,640]{1,0:T(8,128)(2,1)S(1)} %collective-permute-done.3.images_ref, f32[32,256]{1,0:T(8,128)S(1)} %get-tuple-element.56.lift_ref, bf16[256,2304]{1,0:T(8,128)(2,1)S(1)} %get-tuple-element.57.kernel_ref, f32[1,256]{1,0:T(1,128)S(1)} %get-tuple-element.58.head_ref), custom_call_target="tpu_custom_call" | custom-call | tf_op jit(solution)/shard_map/second_pull/pallas_call | solution.py:353
  69.5 10.0 %all_to_all.17.pulls_ref = bf16[8,32,512]{2,1,0:T(8,128)(2,1)S(1)} all-to-all(bf16[8,32,512]{2,1,0:T(8,128)(2,1)S(1)} %get-tuple-element.59), channel_id=1, replica_groups={{0,1,2,3,4,5,6,7},{8,9,10,11,12,13,14,15},{16,17,18,19,20,21,22,23},{24..., dimensions={0} | all-to-all | bytes 524288 | tf_op jit(solution)/shard_map/all_to_all | solution.py:377
  79.6 6.6 %collective-permute-start.5 = (bf16[32,640]{1,0:T(8,128)(2,1)S(1)}, bf16[32,640]{1,0:T(8,128)(2,1)S(1)}, u32[]{:S(2)}, u32[]{:S(2)}) collective-permute-start(bf16[32,640]{1,0:T(8,128)(2,1)S(1)} %sum_second.1), channel_id=1, source_target_pairs={{0,16},{16,32},{32,48},{48,64},{64,80},{80,96},{96,112},{112,128},... | collective-permute-start | bytes 122888 | tf_op jit(solution)/shard_map/ppermute | solution.py:367
  86.2 11.1 %collective-permute-done.4.part_b = bf16[96,2816]{1,0:T(8,128)(2,1)S(1)} collective-permute-done((bf16[96,2816]{1,0:T(8,128)(2,1)S(1)}, bf16[96,2816]{1,0:T(8,128)(2,1)S(1)}, u32[]{:S(2)}, u32[]{:S(2)}) %collective-permute-start.4) | collective-permute-done | bytes 540704 | tf_op jit(solution)/shard_map/ppermute | solution.py:367
  97.3 3.8 %moved_first.1 = (f32[32,256]{1,0:T(8,128)S(1)}, f32[256,2304]{1,0:T(8,128)S(1)}, f32[1,256]{1,0:T(1,128)S(1)}) custom-call(bf16[160,2304]{1,0:T(8,128)(2,1)S(1)} %collective-permute-done.2.part_a, bf16[96,2816]{1,0:T(8,128)(2,1)S(1)} %collective-permute-done.4.part_b), custom_call_target="tpu_custom_call" | custom-call | tf_op jit(solution)/shard_map/moved_first/pallas_call | solution.py:353
  101.1 2.1 %collective-permute-start.6 = (bf16[32,640]{1,0:T(8,128)(2,1)S(1)}, bf16[32,640]{1,0:T(8,128)(2,1)S(1)}, u32[]{:S(2)}, u32[]{:S(2)}) collective-permute-start(bf16[32,640]{1,0:T(8,128)(2,1)S(1)} %collective-permute-done.5.own_ref), channel_id=1, source_target_pairs={{0,8},{1,9},{2,10},{3,11},{4,12},{5,13},{6,14},{7,15},{8,0},{9,1},... | collective-permute-start | bytes 122888 | tf_op jit(solution)/shard_map/ppermute | solution.py:371
  103.2 5.3 %moved_second.1 = (f32[32,256]{1,0:T(8,128)}, f32[256,2304]{1,0:T(8,128)}, f32[1,256]{1,0:T(1,128)}) custom-call(bf16[96,2816]{1,0:T(8,128)(2,1)S(1)} %collective-permute-done.4.part_b, f32[32,256]{1,0:T(8,128)S(1)} %get-tuple-element.61.lift_ref, f32[256,2304]{1,0:T(8,128)S(1)} %get-tuple-element.62.kernel_ref, f32[1,256]{1,0:T(1,128)S(1)} %get-tuple-element.63.head_ref), custom_call_target="tpu_custom_call" | custom-call | tf_op jit(solution)/shard_map/moved_second/pallas_call | solution.py:460
  108.5 2.2 %generator_last.1 = (f32[256,128]{1,0:T(8,128)}, f32[32,256]{1,0:T(8,128)}, f32[32,32]{1,0:T(8,128)}, f32[1,2]{1,0:T(1,128)}) custom-call(s32[1]{0:T(128)} %bitcast.1.place_ref, bf16[32,640]{1,0:T(8,128)(2,1)S(1)} %collective-permute-done.5.own_ref, bf16[32,640]{1,0:T(8,128)(2,1)S(1)} %collective-permute-done.6.other_ref, ...), custom_call_target="tpu_custom_call" | custom-call | tf_op jit(solution)/shard_map/generator_last/pallas_call | solution.py:469
  (21 shorter events, 0.1 us)
Async XLA Ops:
  0.6 16.8 %collective-permute-start = (bf16[64,128]{1,0:T(8,128)(2,1)}, bf16[64,128]{1,0:T(8,128)(2,1)S(1)}, u32[]{:S(2)}, u32[]{:S(2)}) collective-permute-start(bf16[64,128]{1,0:T(8,128)(2,1)} %bitcast.32), channel_id=1, source_target_pairs={{0,8},{1,9},{2,10},{3,11},{4,12},{5,13},{6,14},{7,15},{8,0},{9,1},... | collective-permute-start | bytes 49160 | tf_op jit(solution)/shard_map/ppermute | solution.py:371
  7.4 45.1 %collective-permute-start.2 = (bf16[160,2304]{1,0:T(8,128)(2,1)}, bf16[160,2304]{1,0:T(8,128)(2,1)S(1)}, u32[]{:S(2)}, u32[]{:S(2)}) collective-permute-start(bf16[160,2304]{1,0:T(8,128)(2,1)} %get-tuple-element.48), channel_id=1, source_target_pairs={{0,32},{16,48},{32,64},{48,80},{64,96},{80,112},{96,128},{112,144}... | collective-permute-start | bytes 2211848 | tf_op jit(solution)/shard_map/ppermute | solution.py:367
  17.4 0.7 copy-start.6
  18.1 10.3 %copy-start.1 = (f32[256,128]{1,0:T(8,128)S(1)}, f32[256,128]{1,0:T(8,128)}, u32[]{:S(2)}) copy-start(f32[256,128]{1,0:T(8,128)} %get-tuple-element.42.first_ref) | copy-start | bytes 393220
  18.1 10.3 %copy-start.2 = (f32[32,256]{1,0:T(8,128)S(1)}, f32[32,256]{1,0:T(8,128)}, u32[]{:S(2)}) copy-start(f32[32,256]{1,0:T(8,128)} %get-tuple-element.43.second_ref) | copy-start | bytes 98308
  18.1 10.3 %copy-start.3 = (bf16[4,32,64]{2,1,0:T(8,128)(2,1)S(1)}, bf16[4,32,64]{2,1,0:T(8,128)(2,1)}, u32[]{:S(2)}) copy-start(bf16[4,32,64]{2,1,0:T(8,128)(2,1)} %get-tuple-element.44.pool_ref) | copy-start | bytes 49156
  18.1 10.3 %copy-start.4 = (s32[1,1,2,1]{2,3,1,0:T(1,128)S(1)}, s32[1,1,2,1]{2,3,1,0:T(1,128)}, u32[]{:S(2)}) copy-start(s32[1,1,2,1]{2,3,1,0:T(1,128)} %param.9) | copy-start | bytes 28
  18.1 11.6 %copy-start = (f32[1,1,256,2304]{3,2,1,0:T(8,128)S(1)}, f32[1,1,256,2304]{3,2,1,0:T(8,128)}, u32[]{:S(2)}) copy-start(f32[1,1,256,2304]{3,2,1,0:T(8,128)} %param.14) | copy-start | bytes 7077892
  18.2 11.6 %copy-start.5 = (f32[32,256]{1,0:T(8,128)S(1)}, f32[32,256]{1,0:T(8,128)}, u32[]{:S(2)}) copy-start(f32[32,256]{1,0:T(8,128)} %get-tuple-element.45.lift_ref) | copy-start | bytes 98308
  18.2 11.6 %copy-start.7 = (f32[1,256]{1,0:T(1,128)S(1)}, f32[1,256]{1,0:T(1,128)}, u32[]{:S(2)}) copy-start(f32[1,256]{1,0:T(1,128)} %get-tuple-element.46.head_ref) | copy-start | bytes 3076
  43.8 8.7 %collective-permute-start.1 = (bf16[32,512]{1,0:T(8,128)(2,1)S(1)}, bf16[32,512]{1,0:T(8,128)(2,1)S(1)}, u32[]{:S(2)}, u32[]{:S(2)}) collective-permute-start(bf16[32,512]{1,0:T(8,128)(2,1)S(1)} %sum_first.1.own_ref), channel_id=1, source_target_pairs={{0,8},{1,9},{2,10},{3,11},{4,12},{5,13},{6,14},{7,15},{8,0},{9,1},... | collective-permute-start | bytes 98312 | tf_op jit(solution)/shard_map/ppermute | solution.py:371
  55.3 9.6 %collective-permute-start.3 = (bf16[32,640]{1,0:T(8,128)(2,1)S(1)}, bf16[32,640]{1,0:T(8,128)(2,1)S(1)}, u32[]{:S(2)}, u32[]{:S(2)}) collective-permute-start(bf16[32,640]{1,0:T(8,128)(2,1)S(1)} %get-tuple-element.50), channel_id=1, source_target_pairs={{0,496},{16,0},{32,16},{48,32},{64,48},{80,64},{96,80},{112,96},{1... | collective-permute-start | bytes 122888 | tf_op jit(solution)/shard_map/ppermute | solution.py:367
  65.0 32.4 %collective-permute-start.4 = (bf16[96,2816]{1,0:T(8,128)(2,1)S(1)}, bf16[96,2816]{1,0:T(8,128)(2,1)S(1)}, u32[]{:S(2)}, u32[]{:S(2)}) collective-permute-start(bf16[96,2816]{1,0:T(8,128)(2,1)S(1)} %add_images.1), channel_id=1, source_target_pairs={{0,32},{16,48},{32,64},{48,80},{64,96},{80,112},{96,128},{112,144}... | collective-permute-start | bytes 1622024 | tf_op jit(solution)/shard_map/ppermute | solution.py:367
  79.6 21.5 %collective-permute-start.5 = (bf16[32,640]{1,0:T(8,128)(2,1)S(1)}, bf16[32,640]{1,0:T(8,128)(2,1)S(1)}, u32[]{:S(2)}, u32[]{:S(2)}) collective-permute-start(bf16[32,640]{1,0:T(8,128)(2,1)S(1)} %sum_second.1), channel_id=1, source_target_pairs={{0,16},{16,32},{32,48},{48,64},{64,80},{80,96},{96,112},{112,128},... | collective-permute-start | bytes 122888 | tf_op jit(solution)/shard_map/ppermute | solution.py:367
  101.1 7.4 %collective-permute-start.6 = (bf16[32,640]{1,0:T(8,128)(2,1)S(1)}, bf16[32,640]{1,0:T(8,128)(2,1)S(1)}, u32[]{:S(2)}, u32[]{:S(2)}) collective-permute-start(bf16[32,640]{1,0:T(8,128)(2,1)S(1)} %collective-permute-done.5.own_ref), channel_id=1, source_target_pairs={{0,8},{1,9},{2,10},{3,11},{4,12},{5,13},{6,14},{7,15},{8,0},{9,1},... | collective-permute-start | bytes 122888 | tf_op jit(solution)/shard_map/ppermute | solution.py:371

commit v8 on v7

--- a/solution.py
+++ b/solution.py
@@ -20,8 +20,8 @@
 PART_A = 160
 PART_B = CH - PART_A
 EXTRA = 512
-FIRST_WORK = 2_000_000_000
-COPY_WORK = 4_000_000_000
+FIRST_WORK = 20_000_000_000
+COPY_WORK = 1_000_000
 
 critic_rate = 0.05
 generator_rate = 0.2
@@ -409,6 +409,7 @@
     (copies,) = call(
         noise_copies_kernel, "noise_copies", [((8, 4 * C, 128), bf16)], (place, own_noise, other_noise), scalars=1, work=COPY_WORK
     )
+    part_a, copies = together(part_a, copies)
     moved_a = shifted(part_a, 2)
     noise = swap(copies)
     (images,) = call(
@@ -424,7 +425,6 @@
     )
     (partial,) = call(sum_kernel, "sum_first", [((C, FAKE), bf16)], (swap(copies),))
     other = across(partial)
-    other, moved_a = together(other, moved_a)
     own_images, first_1, second_1 = call(
         middle_kernel,
         "generator_step",
@@ -436,7 +436,7 @@
     (part_b,) = call(
         add_images_kernel, "add_images", [((PART_B, KW + EXTRA), bf16)], (ahead_images, part_b)
     )
-    part_b, ahead_images = together(part_b, ahead_images)
+    part_b, ahead_images, moved_a = together(part_b, ahead_images, moved_a)
     moved_b = shifted(part_b, 2)
     copies, score_1 = call(
         pull_only_kernel,

time: 112 us -> 117 us (1.045)
  blocking collectives: 30.2 us -> 20.2 us
  waiting for transfers between devices: 19 us -> 26.3 us
  starting transfers between devices: 35.3 us -> 39.3 us
  local copies, waits for them, and re-layouts: 0.75 us -> 4.58 us
    all_to_all x3 -> x2, blocking collectives: 30.2 us -> 20.2 us  [swap(): lax.all_to_all(copies, ('loop', 'grp'), 0, 0, axis_index_groups=groups)]
    all_to_all x0 -> x1, starting transfers between devices: none -> 8.28 us  [swap(): lax.all_to_all(copies, ('loop', 'grp'), 0, 0, axis_index_groups=groups)]
    ppermute x3, waiting for transfers between devices: 6.25 us -> 13.8 us  [across(): return lax.ppermute(value, 'grp', [(m, m ^ 8) for m in range(N_GRP)])]
    ppermute x4, starting transfers between devices: 26.5 us -> 21.1 us  [shifted(): lax.ppermute(value, 'loop', [(s, (s + steps) % count) for s in range(coun...]
    unnamed x16 -> x22, local copies, waits for them, and re-layouts: 0.75 us -> 4.58 us
  transfers between devices with their start and end apart: 7 -> 8, of which waited for: 3 -> 3; matrix products, arithmetic and copies ran while one was open for 0% -> 0% of each run, Pallas kernels for 18% -> 19%
where the time goes in v8:
time: 117 us
  starting transfers between devices  39.3 us (34%)
  waiting for transfers between devices  26.3 us (22%)
  Pallas kernels  25.2 us (22%)
  blocking collectives  20.2 us (17%)
  local copies, waits for them, and re-layouts  4.58 us (4%)
    ppermute x4, starting transfers between devices, shifted(): lax.ppermute(value, 'loop', [(s, (s + steps) % count) for s in range(coun...  21.1 us
    all_to_all x2, blocking collectives, swap(): lax.all_to_all(copies, ('loop', 'grp'), 0, 0, axis_index_groups=groups)  20.2 us
    pallas_call x9, Pallas kernels, call(): pl.pallas_call(kernel, name=name, out_shape=[jax.ShapeDtypeStruct(s, d) f...  15.3 us
    ppermute x3, waiting for transfers between devices, across(): return lax.ppermute(value, 'grp', [(m, m ^ 8) for m in range(N_GRP)])  13.8 us
    ppermute x4, waiting for transfers between devices, shifted(): lax.ppermute(value, 'loop', [(s, (s + steps) % count) for s in range(coun...  12.4 us
    ppermute x3, starting transfers between devices, across(): return lax.ppermute(value, 'grp', [(m, m ^ 8) for m in range(N_GRP)])  9.87 us
    all_to_all x1, starting transfers between devices, swap(): lax.all_to_all(copies, ('loop', 'grp'), 0, 0, axis_index_groups=groups)  8.28 us
    pallas_call x1, Pallas kernels, per_device(): pl.pallas_call(moved_second_kernel, name='moved_second', out_shape=[jax.S...  5.3 us
  transfers between devices with their start and end apart: 8, of which 3 were waited for; matrix products, arithmetic and copies ran while one was open for 0% of the time, Pallas kernels for 19%

profile of v8, /device:TPU:6, one launch (start us, length us, event | category | flops | bytes accessed | tf_op | source)
XLA Modules:
  0.0 116.6 jit_solution(6727781755124419037)
XLA Ops:
  0.7 4.4 %collective-permute-start = (bf16[64,128]{1,0:T(8,128)(2,1)}, bf16[64,128]{1,0:T(8,128)(2,1)S(1)}, u32[]{:S(2)}, u32[]{:S(2)}) collective-permute-start(bf16[64,128]{1,0:T(8,128)(2,1)} %bitcast.32), channel_id=1, source_target_pairs={{0,8},{1,9},{2,10},{3,11},{4,12},{5,13},{6,14},{7,15},{8,0},{9,1},... | collective-permute-start | bytes 49160 | tf_op jit(solution)/shard_map/ppermute | solution.py:371
  5.1 2.4 %stage.1 = (bf16[160,2304]{1,0:T(8,128)(2,1)}, f32[256,128]{1,0:T(8,128)}, f32[32,256]{1,0:T(8,128)}, bf16[4,32,64]{2,1,0:T(8,128)(2,1)}, f32[32,256]{1,0:T(8,12...) custom-call(f32[256,2304]{1,0:T(8,128)} %bitcast.24, f32[256,128]{1,0:T(8,128)} %bitcast.28, f32[32,256]{1,0:T(8,128)} %bitcast.29, ...), custom_call_target="tpu_custom_call" | custom-call | tf_op jit(solution)/shard_map/stage/pallas_call | solution.py:400
  9.0 8.3 %all-to-all-start = ((bf16[8,128,128]{2,1,0:T(8,128)(2,1)}), bf16[8,128,128]{2,1,0:T(8,128)(2,1)S(1)}, u32[]{:S(2)}, u32[]{:S(2)}) async-start(bf16[8,128,128]{2,1,0:T(8,128)(2,1)} %noise_copies.1), calls=%async_computation | async-start | bytes 524288 | tf_op jit(solution)/shard_map/all_to_all | solution.py:377
  17.3 6.5 %collective-permute-start.3 = (bf16[160,2304]{1,0:T(8,128)(2,1)}, bf16[160,2304]{1,0:T(8,128)(2,1)S(1)}, u32[]{:S(2)}, u32[]{:S(2)}) collective-permute-start(bf16[160,2304]{1,0:T(8,128)(2,1)} %get-tuple-element.53), channel_id=1, source_target_pairs={{0,32},{16,48},{32,64},{48,80},{64,96},{80,112},{96,128},{112,144}... | collective-permute-start | bytes 2211848 | tf_op jit(solution)/shard_map/ppermute | solution.py:367
  23.8 0.9 copy-done.1
  24.7 0.8 copy-done.3
  25.5 0.8 copy-done.5
  26.2 1.3 %make_fakes.1.images_ref = bf16[32,640]{1,0:T(8,128)(2,1)S(1)} custom-call(s32[2]{0:T(128)S(1)} %bitcast.26, bf16[8,128,128]{2,1,0:T(8,128)(2,1)S(1)} %all-to-all-done.noise_ref, f32[256,128]{1,0:T(8,128)S(1)} %copy-done.1, f32[32,256]{1,0:T(8,128)S(1)} %copy-done.3, bf16[4,32,64]{2,1,0:T(8,128)(2,1)S(1)} %copy-done.5), custom_call_target="tpu_custom_call" | custom-call | tf_op jit(solution)/shard_map/make_fakes/pallas_call | solution.py:353
  29.1 3.9 %first_step.1 = (bf16[8,32,512]{2,1,0:T(8,128)(2,1)S(1)}, f32[32,256]{1,0:T(8,128)S(1)}, bf16[256,2304]{1,0:T(8,128)(2,1)S(1)}, f32[1,256]{1,0:T(1,128)S(1)}, f3...) custom-call(bf16[32,640]{1,0:T(8,128)(2,1)S(1)} %make_fakes.1.images_ref, f32[32,256]{1,0:T(8,128)S(1)} %copy-done.9, ...), custom_call_target="tpu_custom_call" | custom-call | flops 20000000000 | tf_op jit(solution)/shard_map/first_step/pallas_call | solution.py:353
  33.0 10.1 %all_to_all.15.pulls_ref = bf16[8,32,512]{2,1,0:T(8,128)(2,1)S(1)} all-to-all(bf16[8,32,512]{2,1,0:T(8,128)(2,1)S(1)} %get-tuple-element.50), channel_id=1, replica_groups={{0,1,2,3,4,5,6,7},{8,9,10,11,12,13,14,15},{16,17,18,19,20,21,22,23},{24..., dimensions={0} | all-to-all | bytes 524288 | tf_op jit(solution)/shard_map/all_to_all | solution.py:377
  43.1 3.4 %collective-permute-start.1 = (bf16[32,512]{1,0:T(8,128)(2,1)S(1)}, bf16[32,512]{1,0:T(8,128)(2,1)S(1)}, u32[]{:S(2)}, u32[]{:S(2)}) collective-permute-start(bf16[32,512]{1,0:T(8,128)(2,1)S(1)} %sum_first.1.own_ref), channel_id=1, source_target_pairs={{0,8},{1,9},{2,10},{3,11},{4,12},{5,13},{6,14},{7,15},{8,0},{9,1},... | collective-permute-start | bytes 98312 | tf_op jit(solution)/shard_map/ppermute | solution.py:371
  46.4 13.8 %collective-permute-done.1.other_ref = bf16[32,512]{1,0:T(8,128)(2,1)S(1)} collective-permute-done((bf16[32,512]{1,0:T(8,128)(2,1)S(1)}, bf16[32,512]{1,0:T(8,128)(2,1)S(1)}, u32[]{:S(2)}, u32[]{:S(2)}) %collective-permute-start.1) | collective-permute-done | bytes 32800 | tf_op jit(solution)/shard_map/ppermute | solution.py:371
  60.3 2.8 %generator_step.1 = (bf16[32,640]{1,0:T(8,128)(2,1)S(1)}, f32[256,128]{1,0:T(8,128)S(1)}, f32[32,256]{1,0:T(8,128)S(1)}) custom-call(s32[2]{0:T(128)S(1)} %bitcast.27, bf16[32,512]{1,0:T(8,128)(2,1)S(1)} %sum_first.1.own_ref, bf16[32,512]{1,0:T(8,128)(2,1)S(1)} %collective-permute-done.1.other_ref, bf16[8,128,128]{2,1,0:T(8,128)(2,1)S(1)} %all-to-all-done.noise_ref, ...), custom_call_target="tpu_custom_call" | custom-call | tf_op jit(solution)/shard_map/generator_step/pallas_call | solution.py:353
  63.1 4.6 %collective-permute-start.2 = (bf16[32,640]{1,0:T(8,128)(2,1)S(1)}, bf16[32,640]{1,0:T(8,128)(2,1)S(1)}, u32[]{:S(2)}, u32[]{:S(2)}) collective-permute-start(bf16[32,640]{1,0:T(8,128)(2,1)S(1)} %get-tuple-element.51), channel_id=1, source_target_pairs={{0,496},{16,0},{32,16},{48,32},{64,48},{80,64},{96,80},{112,96},{1... | collective-permute-start | bytes 122888 | tf_op jit(solution)/shard_map/ppermute | solution.py:367
  67.7 2.5 %collective-permute-done.2.images_ref = bf16[32,640]{1,0:T(8,128)(2,1)S(1)} collective-permute-done((bf16[32,640]{1,0:T(8,128)(2,1)S(1)}, bf16[32,640]{1,0:T(8,128)(2,1)S(1)}, u32[]{:S(2)}, u32[]{:S(2)}) %collective-permute-start.2) | collective-permute-done | bytes 40992 | tf_op jit(solution)/shard_map/ppermute | solution.py:367
  70.3 2.9 %collective-permute-start.4 = (bf16[96,2816]{1,0:T(8,128)(2,1)S(1)}, bf16[96,2816]{1,0:T(8,128)(2,1)S(1)}, u32[]{:S(2)}, u32[]{:S(2)}) collective-permute-start(bf16[96,2816]{1,0:T(8,128)(2,1)S(1)} %add_images.1), channel_id=1, source_target_pairs={{0,32},{16,48},{32,64},{48,80},{64,96},{80,112},{96,128},{112,144}... | collective-permute-start | bytes 1622024 | tf_op jit(solution)/shard_map/ppermute | solution.py:367
  73.3 2.6 %second_pull.1 = (bf16[8,32,512]{2,1,0:T(8,128)(2,1)S(1)}, bf16[32,128]{1,0:T(8,128)(2,1)S(1)}) custom-call(bf16[32,640]{1,0:T(8,128)(2,1)S(1)} %collective-permute-done.2.images_ref, f32[32,256]{1,0:T(8,128)S(1)} %get-tuple-element.58.lift_ref, bf16[256,2304]{1,0:T(8,128)(2,1)S(1)} %get-tuple-element.59.kernel_ref, f32[1,256]{1,0:T(1,128)S(1)} %get-tuple-element.60.head_ref), custom_call_target="tpu_custom_call" | custom-call | tf_op jit(solution)/shard_map/second_pull/pallas_call | solution.py:353
  75.9 10.2 %all_to_all.16.pulls_ref = bf16[8,32,512]{2,1,0:T(8,128)(2,1)S(1)} all-to-all(bf16[8,32,512]{2,1,0:T(8,128)(2,1)S(1)} %get-tuple-element.61), channel_id=1, replica_groups={{0,1,2,3,4,5,6,7},{8,9,10,11,12,13,14,15},{16,17,18,19,20,21,22,23},{24..., dimensions={0} | all-to-all | bytes 524288 | tf_op jit(solution)/shard_map/all_to_all | solution.py:377
  86.1 7.0 %collective-permute-start.5 = (bf16[32,640]{1,0:T(8,128)(2,1)S(1)}, bf16[32,640]{1,0:T(8,128)(2,1)S(1)}, u32[]{:S(2)}, u32[]{:S(2)}) collective-permute-start(bf16[32,640]{1,0:T(8,128)(2,1)S(1)} %sum_second.1), channel_id=1, source_target_pairs={{0,16},{16,32},{32,48},{48,64},{64,80},{80,96},{96,112},{112,128},... | collective-permute-start | bytes 122888 | tf_op jit(solution)/shard_map/ppermute | solution.py:367
  93.2 9.9 %collective-permute-done.4.part_b = bf16[96,2816]{1,0:T(8,128)(2,1)S(1)} collective-permute-done((bf16[96,2816]{1,0:T(8,128)(2,1)S(1)}, bf16[96,2816]{1,0:T(8,128)(2,1)S(1)}, u32[]{:S(2)}, u32[]{:S(2)}) %collective-permute-start.4) | collective-permute-done | bytes 540704 | tf_op jit(solution)/shard_map/ppermute | solution.py:367
  103.0 3.8 %moved_first.1 = (f32[32,256]{1,0:T(8,128)S(1)}, f32[256,2304]{1,0:T(8,128)S(1)}, f32[1,256]{1,0:T(1,128)S(1)}) custom-call(bf16[160,2304]{1,0:T(8,128)(2,1)S(1)} %collective-permute-done.3.part_a, bf16[96,2816]{1,0:T(8,128)(2,1)S(1)} %collective-permute-done.4.part_b), custom_call_target="tpu_custom_call" | custom-call | tf_op jit(solution)/shard_map/moved_first/pallas_call | solution.py:353
  106.8 2.1 %collective-permute-start.6 = (bf16[32,640]{1,0:T(8,128)(2,1)S(1)}, bf16[32,640]{1,0:T(8,128)(2,1)S(1)}, u32[]{:S(2)}, u32[]{:S(2)}) collective-permute-start(bf16[32,640]{1,0:T(8,128)(2,1)S(1)} %collective-permute-done.5.own_ref), channel_id=1, source_target_pairs={{0,8},{1,9},{2,10},{3,11},{4,12},{5,13},{6,14},{7,15},{8,0},{9,1},... | collective-permute-start | bytes 122888 | tf_op jit(solution)/shard_map/ppermute | solution.py:371
  108.9 5.3 %moved_second.1 = (f32[32,256]{1,0:T(8,128)}, f32[256,2304]{1,0:T(8,128)}, f32[1,256]{1,0:T(1,128)}) custom-call(bf16[96,2816]{1,0:T(8,128)(2,1)S(1)} %collective-permute-done.4.part_b, f32[32,256]{1,0:T(8,128)S(1)} %get-tuple-element.63.lift_ref, f32[256,2304]{1,0:T(8,128)S(1)} %get-tuple-element.64.kernel_ref, f32[1,256]{1,0:T(1,128)S(1)} %get-tuple-element.65.head_ref), custom_call_target="tpu_custom_call" | custom-call | tf_op jit(solution)/shard_map/moved_second/pallas_call | solution.py:460
  114.3 2.1 %generator_last.1 = (f32[256,128]{1,0:T(8,128)}, f32[32,256]{1,0:T(8,128)}, f32[32,32]{1,0:T(8,128)}, f32[1,2]{1,0:T(1,128)}) custom-call(s32[1]{0:T(128)} %bitcast.11.place_ref, bf16[32,640]{1,0:T(8,128)(2,1)S(1)} %collective-permute-done.5.own_ref, bf16[32,640]{1,0:T(8,128)(2,1)S(1)} %collective-permute-done.6.other_ref, ...), custom_call_target="tpu_custom_call" | custom-call | tf_op jit(solution)/shard_map/generator_last/pallas_call | solution.py:469
  (28 shorter events, 3.1 us)
Async XLA Ops:
  0.6 26.9 %copy-start = (f32[1,1,256,2304]{3,2,1,0:T(8,128)S(1)}, f32[1,1,256,2304]{3,2,1,0:T(8,128)}, u32[]{:S(2)}) copy-start(f32[1,1,256,2304]{3,2,1,0:T(8,128)} %param.14) | copy-start | bytes 7077892
  0.6 23.1 %copy-start.8 = (s32[1,1,2,1]{2,3,1,0:T(1,128)S(1)}, s32[1,1,2,1]{2,3,1,0:T(1,128)}, u32[]{:S(2)}) copy-start(s32[1,1,2,1]{2,3,1,0:T(1,128)} %param.9) | copy-start | bytes 28
  0.7 6.9 %collective-permute-start = (bf16[64,128]{1,0:T(8,128)(2,1)}, bf16[64,128]{1,0:T(8,128)(2,1)S(1)}, u32[]{:S(2)}, u32[]{:S(2)}) collective-permute-start(bf16[64,128]{1,0:T(8,128)(2,1)} %bitcast.32), channel_id=1, source_target_pairs={{0,8},{1,9},{2,10},{3,11},{4,12},{5,13},{6,14},{7,15},{8,0},{9,1},... | collective-permute-start | bytes 49160 | tf_op jit(solution)/shard_map/ppermute | solution.py:371
  7.5 0.7 copy-start.7
  9.0 14.8 %all-to-all-start = ((bf16[8,128,128]{2,1,0:T(8,128)(2,1)}), bf16[8,128,128]{2,1,0:T(8,128)(2,1)S(1)}, u32[]{:S(2)}, u32[]{:S(2)}) async-start(bf16[8,128,128]{2,1,0:T(8,128)(2,1)} %noise_copies.1), calls=%async_computation | async-start | bytes 524288 | tf_op jit(solution)/shard_map/all_to_all | solution.py:377
  17.3 53.1 %collective-permute-start.3 = (bf16[160,2304]{1,0:T(8,128)(2,1)}, bf16[160,2304]{1,0:T(8,128)(2,1)S(1)}, u32[]{:S(2)}, u32[]{:S(2)}) collective-permute-start(bf16[160,2304]{1,0:T(8,128)(2,1)} %get-tuple-element.53), channel_id=1, source_target_pairs={{0,32},{16,48},{32,64},{48,80},{64,96},{80,112},{96,128},{112,144}... | collective-permute-start | bytes 2211848 | tf_op jit(solution)/shard_map/ppermute | solution.py:367
  23.8 0.9 copy-start.1
  24.7 0.8 copy-start.3
  25.5 0.8 copy-start.5
  27.6 0.8 copy-start.9
  28.4 0.7 copy-start.10
  29.1 31.2 %copy-start.2 = (f32[256,128]{1,0:T(8,128)S(1)}, f32[256,128]{1,0:T(8,128)}, u32[]{:S(2)}) copy-start(f32[256,128]{1,0:T(8,128)} %get-tuple-element.45.first_ref) | copy-start | bytes 393220
  29.1 31.2 %copy-start.4 = (f32[32,256]{1,0:T(8,128)S(1)}, f32[32,256]{1,0:T(8,128)}, u32[]{:S(2)}) copy-start(f32[32,256]{1,0:T(8,128)} %get-tuple-element.46.second_ref) | copy-start | bytes 98308
  29.1 31.2 %copy-start.6 = (bf16[4,32,64]{2,1,0:T(8,128)(2,1)S(1)}, bf16[4,32,64]{2,1,0:T(8,128)(2,1)}, u32[]{:S(2)}) copy-start(bf16[4,32,64]{2,1,0:T(8,128)(2,1)} %get-tuple-element.47.pool_ref) | copy-start | bytes 49156
  43.1 17.2 %collective-permute-start.1 = (bf16[32,512]{1,0:T(8,128)(2,1)S(1)}, bf16[32,512]{1,0:T(8,128)(2,1)S(1)}, u32[]{:S(2)}, u32[]{:S(2)}) collective-permute-start(bf16[32,512]{1,0:T(8,128)(2,1)S(1)} %sum_first.1.own_ref), channel_id=1, source_target_pairs={{0,8},{1,9},{2,10},{3,11},{4,12},{5,13},{6,14},{7,15},{8,0},{9,1},... | collective-permute-start | bytes 98312 | tf_op jit(solution)/shard_map/ppermute | solution.py:371
  63.1 7.2 %collective-permute-start.2 = (bf16[32,640]{1,0:T(8,128)(2,1)S(1)}, bf16[32,640]{1,0:T(8,128)(2,1)S(1)}, u32[]{:S(2)}, u32[]{:S(2)}) collective-permute-start(bf16[32,640]{1,0:T(8,128)(2,1)S(1)} %get-tuple-element.51), channel_id=1, source_target_pairs={{0,496},{16,0},{32,16},{48,32},{64,48},{80,64},{96,80},{112,96},{1... | collective-permute-start | bytes 122888 | tf_op jit(solution)/shard_map/ppermute | solution.py:367
  70.3 32.7 %collective-permute-start.4 = (bf16[96,2816]{1,0:T(8,128)(2,1)S(1)}, bf16[96,2816]{1,0:T(8,128)(2,1)S(1)}, u32[]{:S(2)}, u32[]{:S(2)}) collective-permute-start(bf16[96,2816]{1,0:T(8,128)(2,1)S(1)} %add_images.1), channel_id=1, source_target_pairs={{0,32},{16,48},{32,64},{48,80},{64,96},{80,112},{96,128},{112,144}... | collective-permute-start | bytes 1622024 | tf_op jit(solution)/shard_map/ppermute | solution.py:367
  86.1 20.7 %collective-permute-start.5 = (bf16[32,640]{1,0:T(8,128)(2,1)S(1)}, bf16[32,640]{1,0:T(8,128)(2,1)S(1)}, u32[]{:S(2)}, u32[]{:S(2)}) collective-permute-start(bf16[32,640]{1,0:T(8,128)(2,1)S(1)} %sum_second.1), channel_id=1, source_target_pairs={{0,16},{16,32},{32,48},{48,64},{64,80},{80,96},{96,112},{112,128},... | collective-permute-start | bytes 122888 | tf_op jit(solution)/shard_map/ppermute | solution.py:367
  106.8 7.4 %collective-permute-start.6 = (bf16[32,640]{1,0:T(8,128)(2,1)S(1)}, bf16[32,640]{1,0:T(8,128)(2,1)S(1)}, u32[]{:S(2)}, u32[]{:S(2)}) collective-permute-start(bf16[32,640]{1,0:T(8,128)(2,1)S(1)} %collective-permute-done.5.own_ref), channel_id=1, source_target_pairs={{0,8},{1,9},{2,10},{3,11},{4,12},{5,13},{6,14},{7,15},{8,0},{9,1},... | collective-permute-start | bytes 122888 | tf_op jit(solution)/shard_map/ppermute | solution.py:371
